TPU v7x, 32 devices: a whole 2x2x4 slice. The times are simulated.
32 devices in a mesh: groups: 2 (over x), tm: 16 (over z, y, core).
Axes of the slice: x: 2, y: 2, z: 4, core: 2. Of those that a mesh axis runs over, the one named last changes fastest.
Arguments:
- signal: bfloat16 [128, 32768], P('groups', 'tm'), parts along dimension 0, may hold values from -24 to 24
- warp_blocks: int32 [4, 256], P('groups'), parts along dimension 0, may hold values from 0 to 255, as said below
- taps: int32 [4, 128, 8], P('groups'), parts along dimension 0, may hold values from 0 to 255
- tap_weights: float32 [4, 128, 8], P('groups'), parts along dimension 0, may hold values from -2 to 2
- replica: float32 [16384], replicated, may hold values from -0.046875 to 0.046875
Outputs:
- ambiguity: bfloat16 [4, 64, 32768], P('groups', None, 'tm'), parts along dimension 0
There are 2 independent parts, one for each index of `groups`. A program takes and returns all parts, laid end to end along the dimension named above; an argument that names none is the same for every part. Nothing has to cross between parts.
Inputs may be any that keep to these rules, and one draw needn't show every extreme that they name: warp_blocks[h, j] = ((e_h + 128 * j + floor(r_h * 128 * j / 32768)) // 128) mod 256, with floor division, for an integer epoch e_h in 0 to 32767 and an integer rate r_h with -983 <= r_h <= 983, both drawn for each hypothesis; hypothesis 0 has e_0 = 32640. Consecutive entries of one hypothesis therefore differ by 0, 1 or 2 modulo 256.
All inputs are finite; a program needn't handle non-finite values.
Results may differ from a plain program's by a relative error of at most 0.0062.
Values may be sent and summed in bfloat16 or wider, within the bound.
No kernel may reach another device: no remote copies, remote signals or barrier semaphores. Data moves between devices by JAX's collectives and lax.ppermute only.
A program may use at most 64 MiB of HBM per device.

v0:
```python
import functools
import math

import jax
import jax.numpy as jnp
import numpy as np
from jax import lax
from jax.experimental import pallas as pl
from jax.experimental.pallas import tpu as pltpu
from jax.sharding import PartitionSpec as P

BEAMS = 64
BLOCK = 128
PAIR = 2 * BLOCK
TAPS = 8
REPLICA = 16384
HYPS = 2
F32 = jnp.float32
BF16 = jnp.bfloat16
VMEM = pl.BlockSpec(memory_space=pltpu.VMEM)
ANY = pl.BlockSpec(memory_space=pl.ANY)


def transform_tables(points):
    k, p = np.arange(points)[:, None], np.arange(points)[None, :]
    angle = 2.0 * math.pi * (k * p % points) / points
    cos, sin = np.cos(angle), np.sin(angle)
    left = np.block([[cos, sin], [-sin, cos]]).astype(np.float32)
    k, p = np.arange(PAIR)[:, None], np.arange(PAIR)[None, :]
    angle = 2.0 * math.pi * (k * p % PAIR) / PAIR
    cos, sin = np.cos(angle), np.sin(angle)
    right = np.block([[cos, -sin], [sin, cos]]).astype(np.float32)
    k, q = np.arange(points)[:, None], np.arange(PAIR)[None, :]
    angle = 2.0 * math.pi * (k * q) / (points * PAIR)
    turn = np.concatenate([np.cos(angle), -np.sin(angle)], axis=1).astype(np.float32)
    parts = []
    for table in (left, right):
        high = table.astype(jnp.bfloat16)
        low = (table - high.astype(np.float32)).astype(jnp.bfloat16)
        parts.append(np.concatenate([high, low], axis=0))
    return jnp.asarray(parts[0]), jnp.asarray(parts[1]), jnp.asarray(turn)


def split(value):
    high = value.astype(BF16)
    return high, (value - high.astype(F32)).astype(BF16)


def dot(left, right):
    return jnp.dot(left, right, preferred_element_type=F32)


def spread_kernel(signal_ref, out_ref):
    upper = lax.broadcasted_iota(jnp.int32, (8, BLOCK), 0) < 4
    groups, blocks = signal_ref.shape[0] // 16, signal_ref.shape[1] // BLOCK
    for group in range(groups):
        for quad in range(0, blocks, 4):
            tiles = []
            for block in range(quad, quad + 4):
                value = signal_ref[group * 16 : group * 16 + 16, block * BLOCK : (block + 1) * BLOCK].astype(F32)
                tiles.append((value[:8], value[8:]))
            for half in range(2):
                parts = [tile[half] for tile in tiles]
                turned = [pltpu.roll(part, 4, 0) for part in parts]
                first = [jnp.where(upper, parts[d], turned[d + 1]) for d in (0, 2)]
                second = [jnp.where(upper, turned[d], parts[d + 1]) for d in (0, 2)]
                device = group * 4 + half * 2
                rows = slice(quad * 4, quad * 4 + 16)
                out_ref[device, rows, :] = jnp.concatenate(first, axis=0).astype(BF16)
                out_ref[device + 1, rows, :] = jnp.concatenate(second, axis=0).astype(BF16)


def spread(signal, segments):
    beams, blocks = signal.shape[0] // segments, signal.shape[1] // BLOCK
    if beams != 4 or signal.shape[0] % 16 or blocks % 4:
        send = signal.reshape(segments, beams, blocks, BLOCK).transpose(0, 2, 1, 3)
        return send.reshape(segments, blocks * beams, BLOCK)
    return pl.pallas_call(
        spread_kernel,
        out_shape=jax.ShapeDtypeStruct((segments, blocks * beams, BLOCK), BF16),
        in_specs=[VMEM],
        out_specs=VMEM,
        name="spread_beams",
    )(signal)


def prepare_kernel(replica_ref, taps_ref, weights_ref, sources_ref, left_ref, right_ref, turn_ref, interp_ref, chosen_ref, spectrum_ref):
    window = lax.broadcasted_iota(jnp.int32, (PAIR, BLOCK), 0)
    for hyp in range(HYPS):
        total = jnp.zeros((PAIR, BLOCK), F32)
        for tap in range(TAPS):
            hit = taps_ref[hyp, tap : tap + 1, :] == window
            total = total + jnp.where(hit, weights_ref[hyp, tap : tap + 1, :], 0.0)
        interp_ref[:, hyp * BLOCK : (hyp + 1) * BLOCK] = total.astype(BF16)

    blocks = chosen_ref.shape[1]
    column = lax.broadcasted_iota(jnp.int32, (blocks, blocks), 1)
    for hyp in range(HYPS):
        rows = slice(hyp * blocks, (hyp + 1) * blocks)
        chosen_ref[rows, :] = (sources_ref[rows, :] == column).astype(F32).astype(BF16)

    points = turn_ref.shape[0]
    lines = replica_ref.shape[0]
    high, low = split(replica_ref[...])
    both = dot(left_ref[:, :lines], high)
    value = both[: 2 * points] + both[2 * points :] + dot(left_ref[: 2 * points, :lines], low)
    value_re, value_im = value[:points], value[points:]
    turn_re, turn_im = turn_ref[:, :PAIR], turn_ref[:, PAIR:]
    turned = jnp.concatenate(
        [value_re * turn_re - value_im * turn_im, value_re * turn_im + value_im * turn_re], axis=1
    )
    high, low = split(turned)
    upper, lower = right_ref[: 2 * PAIR, :], right_ref[2 * PAIR :, :]
    value = (dot(high, upper) + dot(high, lower) + dot(low, upper)) * (1.0 / (points * PAIR))
    spectrum_ref[:, :PAIR] = value[:, :PAIR]
    spectrum_ref[:, PAIR:] = -value[:, PAIR:]


def prepare(replica, taps, tap_weights, warp_blocks, tables):
    blocks = warp_blocks.shape[1]
    points = blocks // 2
    ordered = warp_blocks.reshape(HYPS, points, 2).transpose(0, 2, 1).reshape(HYPS * blocks, 1)
    operands = (replica.reshape(-1, PAIR), taps.transpose(0, 2, 1), tap_weights.transpose(0, 2, 1), ordered, *tables)
    shapes = ((PAIR, HYPS * BLOCK), BF16), ((HYPS * blocks, blocks), BF16), ((points, 2 * PAIR), F32)

    def whole(shape):
        return pl.BlockSpec(shape, lambda g: (0,) * len(shape))

    return pl.pallas_call(
        prepare_kernel,
        grid=(1,),
        out_shape=[jax.ShapeDtypeStruct(*shape) for shape in shapes],
        in_specs=[whole(operand.shape) for operand in operands],
        out_specs=[whole(shape[0]) for shape in shapes],
        compiler_params=pltpu.CompilerParams(vmem_limit_bytes=56 * 1024 * 1024),
        cost_estimate=pl.CostEstimate(flops=500_000_000, bytes_accessed=16_000_000, transcendentals=0),
        name="prepare_tables",
    )(*operands)


def split_sum(total):
    high = total.astype(BF16).astype(F32)
    middle = (total - high).astype(BF16).astype(F32)
    return high, middle, total - high - middle


def complex_rows(beams):
    if beams % 2:
        return [(hyp, beam, None) for hyp in range(HYPS) for beam in range(beams)]
    return [(hyp, beam, beam + 1) for hyp in range(HYPS) for beam in range(0, beams, 2)]


def correlate_kernel(
    beams,
    segments,
    source_ref,
    interp_hbm,
    chosen_hbm,
    left_hbm,
    turn_hbm,
    right_hbm,
    spectrum_hbm,
    out_ref,
    interp_ref,
    chosen_ref,
    left_ref,
    turn_ref,
    right_ref,
    spectrum_ref,
    sems,
    next_ref,
    block_ref,
    column_ref,
    row_ref,
    wide_ref,
):
    fetches = [
        pltpu.make_async_copy(source, target, sems.at[index])
        for index, (source, target) in enumerate(
            (
                (interp_hbm, interp_ref),
                (chosen_hbm, chosen_ref),
                (left_hbm, left_ref),
                (turn_hbm, turn_ref),
                (right_hbm, right_ref),
                (spectrum_hbm, spectrum_ref),
            )
        )
    ]
    for fetch in fetches:
        fetch.start()
    get_interp, get_chosen, get_left, get_turn, get_right, get_spectrum = fetches
    points = turn_ref.shape[0]
    blocks = 2 * points
    lines = source_ref.shape[0]
    rows = complex_rows(beams)
    chunk = min(512, lines)

    get_interp.wait()
    for start in range(0, lines, chunk):
        next_ref[start : start + chunk, :] = dot(source_ref[start : start + chunk, :], interp_ref[BLOCK:, :])
    next_ref[lines : lines + 8, :] = next_ref[0:8, :]
    for start in range(0, lines, chunk):
        value = (
            dot(source_ref[start : start + chunk, :], interp_ref[:BLOCK, :])
            + next_ref[start + beams : start + beams + chunk, :]
        )
        for hyp in range(HYPS):
            block_ref[hyp, start : start + chunk, :] = value[:, hyp * BLOCK : (hyp + 1) * BLOCK]

    get_chosen.wait()
    for hyp in range(HYPS):
        warped = jnp.concatenate(
            [block_ref[hyp, pl.ds(beam, blocks, stride=beams), :].astype(BF16) for beam in range(beams)], axis=1
        )
        gathered = dot(chosen_ref[hyp * blocks : (hyp + 1) * blocks, :], warped).astype(BF16)
        for index, (row_hyp, *pair) in enumerate(rows):
            if row_hyp != hyp:
                continue
            for part, beam in enumerate(pair):
                for half in range(2):
                    lane = index * PAIR + half * BLOCK
                    target = (slice(part * points, (part + 1) * points), slice(lane, lane + BLOCK))
                    if beam is None:
                        column_ref[target] = jnp.zeros((points, BLOCK), BF16)
                    else:
                        column_ref[target] = gathered[
                            half * points : (half + 1) * points, beam * BLOCK : (beam + 1) * BLOCK
                        ]

    def left_product(index):
        both = dot(left_ref[...], column_ref[:, index * PAIR : (index + 1) * PAIR])
        value = both[: 2 * points] + both[2 * points :]
        return value[:points], value[points:]

    def right_product():
        value = row_ref[...]
        wide_ref[...] = dot(value, right_ref[: 2 * PAIR, :]) + dot(value, right_ref[2 * PAIR :, :])

    get_left.wait()
    get_turn.wait()
    turn_re, turn_im = turn_ref[:, :PAIR], turn_ref[:, PAIR:]
    for index in range(len(rows)):
        real, imag = left_product(index)
        place = slice(index * points, (index + 1) * points)
        row_ref[place, :PAIR] = (real * turn_re - imag * turn_im).astype(BF16)
        row_ref[place, PAIR:] = (real * turn_im + imag * turn_re).astype(BF16)
    get_right.wait()
    right_product()
    get_spectrum.wait()
    spectrum_re, spectrum_im = spectrum_ref[:, :PAIR], spectrum_ref[:, PAIR:]
    for index in range(len(rows)):
        place = slice(index * points, (index + 1) * points)
        real, imag = wide_ref[place, :PAIR], wide_ref[place, PAIR:]
        row_ref[place, PAIR:] = (real * spectrum_re - imag * spectrum_im).astype(BF16)
        row_ref[place, :PAIR] = (real * spectrum_im + imag * spectrum_re).astype(BF16)
    right_product()
    for index in range(len(rows)):
        place = slice(index * points, (index + 1) * points)
        lanes = slice(index * PAIR, (index + 1) * PAIR)
        imag, real = wide_ref[place, :PAIR], wide_ref[place, PAIR:]
        column_ref[points:, lanes] = (real * turn_re + imag * turn_im).astype(BF16)
        column_ref[:points, lanes] = (imag * turn_re - real * turn_im).astype(BF16)

    share = points // segments
    sums = [jnp.zeros((8, PAIR), F32) for _ in range(HYPS)]
    for index, (hyp, real_beam, imag_beam) in enumerate(rows):
        imag, real = left_product(index)
        for beam, value in ((real_beam, real), (imag_beam, imag)):
            if beam is None:
                continue
            power = value * value
            sums[hyp] = sums[hyp] + jnp.sum(power.reshape(points // 8, 8, PAIR), axis=0)
            first = (hyp * beams + beam) * 2 * share
            for segment in range(segments):
                piece = power[segment * share : (segment + 1) * share, :]
                out_ref[segment, first : first + 2 * share, :] = jnp.concatenate(
                    [piece[:, :BLOCK], piece[:, BLOCK:]], axis=0
                ).astype(BF16)
    place = lax.broadcasted_iota(jnp.int32, (16, BLOCK), 0)
    tail = jnp.zeros((16, BLOCK), F32)
    for hyp in range(HYPS):
        total = jnp.sum(jnp.sum(sums[hyp], axis=1, keepdims=True), axis=0, keepdims=True)
        for index, piece in enumerate(split_sum(total)):
            tail = jnp.where(place == hyp * 3 + index, piece, tail)
    tail = tail.astype(BF16)
    for segment in range(segments):
        out_ref[segment, HYPS * beams * 2 * share :, :] = tail


def correlate(source, interp, chosen, spectrum, tables, beams, segments):
    left, right, turn = tables
    points = turn.shape[0]
    lines = source.shape[0]
    count = len(complex_rows(beams))
    fetched = (interp, chosen, left, turn, right, spectrum)
    out_rows = HYPS * beams * 2 * (points // segments) + 16
    return pl.pallas_call(
        functools.partial(correlate_kernel, beams, segments),
        out_shape=jax.ShapeDtypeStruct((segments, out_rows, BLOCK), BF16),
        in_specs=[VMEM] + [ANY] * len(fetched),
        out_specs=VMEM,
        scratch_shapes=[pltpu.VMEM(array.shape, array.dtype) for array in fetched]
        + [
            pltpu.SemaphoreType.DMA((len(fetched),)),
            pltpu.VMEM((lines + 8, PAIR), F32),
            pltpu.VMEM((HYPS, lines, BLOCK), F32),
            pltpu.VMEM((2 * points, count * PAIR), BF16),
            pltpu.VMEM((count * points, 2 * PAIR), BF16),
            pltpu.VMEM((count * points, 2 * PAIR), F32),
        ],
        compiler_params=pltpu.CompilerParams(vmem_limit_bytes=56 * 1024 * 1024),
        cost_estimate=pl.CostEstimate(flops=4_000_000_000, bytes_accessed=6_000_000, transcendentals=0),
        name="warp_correlate",
    )(source, *fetched)


def finish_kernel(count, power_ref, sums_ref, out_ref, scratch_ref):
    hyp = pl.program_id(0)
    sums = sums_ref[...].astype(F32)
    place = lax.broadcasted_iota(jnp.int32, sums.shape, 1)
    picked = jnp.where((place >= 3 * hyp) & (place < 3 * hyp + 3), sums, 0.0)
    total = jnp.sum(jnp.sum(picked, axis=0), axis=0, keepdims=True)
    inverse = 1.0 / (total / count + 1e-06)
    devices, lines, _ = power_ref.shape
    for device in range(devices):
        scratch_ref[device * lines : (device + 1) * lines, :] = power_ref[device].astype(F32) * inverse
    beams = out_ref.shape[1]
    step = devices * lines // beams
    for line in range(step):
        half, block = divmod(line, step // 2)
        lane = block * PAIR + half * BLOCK
        out_ref[0, :, lane : lane + BLOCK] = scratch_ref[pl.ds(line, beams, stride=step), :].astype(BF16)


def finish(received, count, beams):
    segments, out_rows, _ = received.shape
    lines = (out_rows - 16) // HYPS
    samples = lines // beams * BLOCK
    return pl.pallas_call(
        functools.partial(finish_kernel, count),
        grid=(HYPS,),
        out_shape=jax.ShapeDtypeStruct((HYPS, segments * beams, samples), BF16),
        in_specs=[
            pl.BlockSpec((segments, lines, BLOCK), lambda g: (0, g, 0)),
            pl.BlockSpec((segments, 16, BLOCK), lambda g: (0, HYPS * lines // 16, 0)),
        ],
        out_specs=pl.BlockSpec((1, segments * beams, samples), lambda g: (g, 0, 0)),
        scratch_shapes=[pltpu.VMEM((segments * lines, BLOCK), F32)],
        cost_estimate=pl.CostEstimate(flops=1_000_000, bytes_accessed=1_200_000, transcendentals=0),
        name="scale_power",
    )(received, received)


def body(signal, warp_blocks, taps, tap_weights, replica):
    segments = lax.axis_size("tm")
    beams = signal.shape[0] // segments
    samples = signal.shape[1] * segments
    received = lax.all_to_all(spread(signal, segments), "tm", split_axis=0, concat_axis=0, tiled=True)
    tables = transform_tables(samples // PAIR)
    interp, chosen, spectrum = prepare(replica, taps, tap_weights, warp_blocks, tables)
    sent = correlate(received.reshape(-1, BLOCK), interp, chosen, spectrum, tables, beams, segments)
    back = lax.all_to_all(sent, "tm", split_axis=0, concat_axis=0, tiled=True)
    return finish(back, float(BEAMS * samples), beams)


def solution(mesh):
    in_specs = (
        P("groups", "tm"),
        P("groups", None),
        P("groups", None, None),
        P("groups", None, None),
        P(),
    )
    out_specs = P("groups", None, "tm")
    return jax.shard_map(body, mesh=mesh, in_specs=in_specs, out_specs=out_specs, check_vma=False)
```

profile of v0, /device:TPU:0, one launch (start us, length us, event | category | flops | bytes accessed | tf_op | source)
XLA Modules:
  0.0 49.5 jit_solution(12327193452354741820)
XLA Ops:
  0.0 1.7 %spread_beams.1 = bf16[16,64,128]{2,1,0:T(8,128)(2,1)} custom-call(bf16[64,2048]{1,0:T(8,128)(2,1)} %signal_ref.1), custom_call_target="tpu_custom_call" | custom-call | tf_op jit(solution)/shard_map/spread_beams/pallas_call | solution.py:78
  1.7 0.0 copy-start.1
  1.7 7.5 %all-to-all-start = ((bf16[16,64,128]{2,1,0:T(8,128)(2,1)}), bf16[16,64,128]{2,1,0:T(8,128)(2,1)S(1)}, u32[]{:S(2)}, u32[]{:S(2)}) async-start(bf16[16,64,128]{2,1,0:T(8,128)(2,1)} %spread_beams.1), calls=%async_computation | async-start | bytes 524288 | tf_op jit(solution)/shard_map/all_to_all | solution.py:359
  9.2 0.0 copy-done.1
  9.2 0.0 copy-start.2
  9.3 0.6 %reshape.13.replica_ref = f32[64,256]{1,0:T(8,128)} reshape(f32[16384]{0:T(1024)S(1)} %copy-done.1) | data formatting | bytes 131072 | tf_op jit(solution)/shard_map/reshape | solution.py:123
  9.9 0.0 copy-done.2
  9.9 0.1 reshape.14
  10.1 0.1 copy.10
  10.2 0.9 %copy.11.sources_ref = s32[512,1]{1,0:T(8,128)} copy(s32[512,1]{0,1:T(1,128)S(1)} %bitcast.9) | data formatting | bytes 4096 | tf_op jit(solution)/shard_map/reshape | solution.py:122
  11.0 3.2 %prepare_tables.1 = (bf16[256,256]{1,0:T(8,128)(2,1)}, bf16[512,256]{1,0:T(8,128)(2,1)}, f32[128,512]{1,0:T(8,128)}) custom-call(f32[64,256]{1,0:T(8,128)} %reshape.13.replica_ref, s32[2,8,128]{2,1,0:T(8,128)} %bitcast.7, f32[2,8,128]{2,1,0:T(8,128)} %bitcast.8, s32[512,1]{1,0:T(8,128)} %copy.11.sources_ref, ...), custom_call_target="tpu_custom_call" | custom-call | flops 500000000 | bytes 16000000 | tf_op jit(solution)/shard_map/prepare_tables/pallas_call | solution.py:129
  14.2 5.0 %all-to-all-done = bf16[16,64,128]{2,1,0:T(8,128)(2,1)S(1)} async-done(((bf16[16,64,128]{2,1,0:T(8,128)(2,1)}), bf16[16,64,128]{2,1,0:T(8,128)(2,1)S(1)}, u32[]{:S(2)}, u32[]{:S(2)}) %all-to-all-start) | async-done | bytes 262176 | tf_op jit(solution)/shard_map/all_to_all | solution.py:359
  19.3 0.0 copy-start
  19.3 0.7 %copy-done = bf16[16,64,128]{2,1,0:T(8,128)(2,1)} copy-done((bf16[16,64,128]{2,1,0:T(8,128)(2,1)}, bf16[16,64,128]{2,1,0:T(8,128)(2,1)S(1)}, u32[]{:S(2)}) %copy-start) | copy-done | bytes 262168
  20.0 5.8 %warp_correlate.1 = bf16[16,144,128]{2,1,0:T(8,128)(2,1)} custom-call(bf16[1024,128]{1,0:T(8,128)(2,1)} %bitcast.6, bf16[256,256]{1,0:T(8,128)(2,1)} %get-tuple-element.8.interp_hbm, bf16[512,256]{1,0:T(8,128)(2,1)} %get-tuple-element.9.chosen_hbm, bf16[512,256]{1,0:T(8,128)(2,1)} %constant.6.clone.left_ref.left_hbm, ...), custom_call_target="tpu_custom_call" | custom-call | flops 4000000000 | bytes 6000000 | tf_op jit(solution)/shard_map/warp_correlate/pallas_call | solution.py:298
  25.8 21.5 %all_to_all.10.power_ref.sums_ref = bf16[16,144,128]{2,1,0:T(8,128)(2,1)} all-to-all(bf16[16,144,128]{2,1,0:T(8,128)(2,1)} %warp_correlate.1), channel_id=1, replica_groups=mesh['groups'=2,'tm'=16] {'tm'}, dimensions={0} | all-to-all | bytes 1179648 | tf_op jit(solution)/shard_map/all_to_all | solution.py:363
  47.4 2.2 %scale_power.1 = bf16[2,64,2048]{2,1,0:T(8,128)(2,1)} custom-call(bf16[16,144,128]{2,1,0:T(8,128)(2,1)} %all_to_all.10.power_ref.sums_ref, bf16[16,144,128]{2,1,0:T(8,128)(2,1)} %all_to_all.10.power_ref.sums_ref), custom_call_target="tpu_custom_call" | custom-call | flops 1000000 | bytes 1200000 | tf_op jit(solution)/shard_map/scale_power/pallas_call | solution.py:340
Async XLA Ops:
  1.7 7.5 %copy-start.1 = (f32[16384]{0:T(1024)S(1)}, f32[16384]{0:T(1024)}, u32[]{:S(2)}) copy-start(f32[16384]{0:T(1024)} %param.12) | copy-start | bytes 196612
  1.7 17.6 %all-to-all-start = ((bf16[16,64,128]{2,1,0:T(8,128)(2,1)}), bf16[16,64,128]{2,1,0:T(8,128)(2,1)S(1)}, u32[]{:S(2)}, u32[]{:S(2)}) async-start(bf16[16,64,128]{2,1,0:T(8,128)(2,1)} %spread_beams.1), calls=%async_computation | async-start | bytes 524288 | tf_op jit(solution)/shard_map/all_to_all | solution.py:359
  9.2 0.7 %copy-start.2 = (s32[2,256]{1,0:T(2,128)S(1)}, s32[2,256]{1,0:T(2,128)}, u32[]{:S(2)}) copy-start(s32[2,256]{1,0:T(2,128)} %param.9) | copy-start | bytes 6148
  19.3 0.7 %copy-start = (bf16[16,64,128]{2,1,0:T(8,128)(2,1)}, bf16[16,64,128]{2,1,0:T(8,128)(2,1)S(1)}, u32[]{:S(2)}) copy-start(bf16[16,64,128]{2,1,0:T(8,128)(2,1)S(1)} %all-to-all-done) | copy-start | bytes 786436
where the time goes:
time: 50 us; the launch traced here: 49.5 us
  blocking collectives  21.5 us (43%)
  Pallas kernels  12.9 us (26%)
  starting transfers between devices  7.52 us (15%)
  waiting for transfers between devices  5.05 us (10%)
  local copies, waits for them, and re-layouts  2.46 us (5%)
    all_to_all x1, blocking collectives, body(): back = lax.all_to_all(sent, 'tm', split_axis=0, concat_axis=0, tiled=True)  21.5 us
    all_to_all x1, starting transfers between devices, body(): lax.all_to_all(spread(signal, segments), 'tm', split_axis=0, concat_axis=...  7.52 us
    pallas_call x1, Pallas kernels, correlate(): pl.pallas_call(functools.partial(correlate_kernel, beams, segments), out_...  5.83 us
    all_to_all x1, waiting for transfers between devices, body(): lax.all_to_all(spread(signal, segments), 'tm', split_axis=0, concat_axis=...  5.05 us
    pallas_call x1, Pallas kernels, prepare(): pl.pallas_call(prepare_kernel, grid=(1,), out_shape=[jax.ShapeDtypeStruct...  3.21 us
    pallas_call x1, Pallas kernels, finish(): pl.pallas_call(functools.partial(finish_kernel, count), grid=(HYPS,), out...  2.16 us
    pallas_call x1, Pallas kernels, spread(): pl.pallas_call(spread_kernel, out_shape=jax.ShapeDtypeStruct((segments, b...  1.71 us
    reshape x2, local copies, waits for them, and re-layouts, prepare(): warp_blocks.reshape(HYPS, points, 2).transpose(0, 2, 1)  1.01 us
  transfers between devices with their start and end apart: 1, of which 1 were waited for; matrix products, arithmetic and copies ran while one was open for 3% of the time, Pallas kernels for 6%

commit v1 on v0

--- a/solution.py
+++ b/solution.py
@@ -18,6 +18,7 @@
 F32 = jnp.float32
 BF16 = jnp.bfloat16
 VMEM = pl.BlockSpec(memory_space=pltpu.VMEM)
+SMEM = pl.BlockSpec(memory_space=pltpu.SMEM)
 ANY = pl.BlockSpec(memory_space=pl.ANY)
 
 
@@ -144,6 +145,24 @@
     return high, middle, total - high - middle
 
 
+def tail_of(totals):
+    place = lax.broadcasted_iota(jnp.int32, (16, BLOCK), 0)
+    tail = jnp.zeros((16, BLOCK), F32)
+    for hyp, total in enumerate(totals):
+        for index, piece in enumerate(split_sum(total)):
+            tail = jnp.where(place == hyp * 3 + index, piece, tail)
+    return tail.astype(BF16)
+
+
+def totals_of(tails):
+    place = lax.broadcasted_iota(jnp.int32, (16, BLOCK), 0)
+    total = functools.reduce(jnp.add, [tail.astype(F32) for tail in tails])
+    return [
+        jnp.sum(jnp.where((place >= 3 * hyp) & (place < 3 * hyp + 3), total, 0.0), axis=0, keepdims=True)
+        for hyp in range(HYPS)
+    ]
+
+
 def complex_rows(beams):
     if beams % 2:
         return [(hyp, beam, None) for hyp in range(HYPS) for beam in range(beams)]
@@ -153,6 +172,8 @@
 def correlate_kernel(
     beams,
     segments,
+    paired,
+    place_ref,
     source_ref,
     interp_hbm,
     chosen_hbm,
@@ -160,7 +181,10 @@
     turn_hbm,
     right_hbm,
     spectrum_hbm,
-    out_ref,
+    *refs,
+):
+    out_refs, refs = refs[: 1 + paired], refs[1 + paired :]
+    (
     interp_ref,
     chosen_ref,
     left_ref,
@@ -173,7 +197,7 @@
     column_ref,
     row_ref,
     wide_ref,
-):
+    ) = refs
     fetches = [
         pltpu.make_async_copy(source, target, sems.at[index])
         for index, (source, target) in enumerate(
@@ -272,34 +296,44 @@
             power = value * value
             sums[hyp] = sums[hyp] + jnp.sum(power.reshape(points // 8, 8, PAIR), axis=0)
             first = (hyp * beams + beam) * 2 * share
-            for segment in range(segments):
-                piece = power[segment * share : (segment + 1) * share, :]
-                out_ref[segment, first : first + 2 * share, :] = jnp.concatenate(
-                    [piece[:, :BLOCK], piece[:, BLOCK:]], axis=0
-                ).astype(BF16)
-    place = lax.broadcasted_iota(jnp.int32, (16, BLOCK), 0)
-    tail = jnp.zeros((16, BLOCK), F32)
-    for hyp in range(HYPS):
-        total = jnp.sum(jnp.sum(sums[hyp], axis=1, keepdims=True), axis=0, keepdims=True)
-        for index, piece in enumerate(split_sum(total)):
-            tail = jnp.where(place == hyp * 3 + index, piece, tail)
-    tail = tail.astype(BF16)
-    for segment in range(segments):
-        out_ref[segment, HYPS * beams * 2 * share :, :] = tail
-
-
-def correlate(source, interp, chosen, spectrum, tables, beams, segments):
+            pieces = [power[segment * share : (segment + 1) * share, :] for segment in range(segments)]
+            pieces = [jnp.concatenate([piece[:, :BLOCK], piece[:, BLOCK:]], axis=0) for piece in pieces]
+            if paired:
+                is_even = place_ref[0] % 2 == 0
+                for chip in range(segments // 2):
+                    start = chip * HYPS * beams * 2 * share + first
+                    even, odd = pieces[2 * chip], pieces[2 * chip + 1]
+                    out_refs[0][start : start + 2 * share, :] = jnp.where(is_even, even, odd).astype(BF16)
+                    out_refs[1][start : start + 2 * share, :] = jnp.where(is_even, odd, even).astype(BF16)
+            else:
+                for segment, piece in enumerate(pieces):
+                    out_refs[0][segment, first : first + 2 * share, :] = piece.astype(BF16)
+    tail = tail_of([jnp.sum(jnp.sum(value, axis=1, keepdims=True), axis=0, keepdims=True) for value in sums])
+    if paired:
+        for out_ref in out_refs:
+            out_ref[out_ref.shape[0] - 16 :, :] = tail
+    else:
+        for segment in range(segments):
+            out_refs[0][segment, HYPS * beams * 2 * share :, :] = tail
+
+
+def correlate(place, source, interp, chosen, spectrum, tables, beams, segments, paired):
     left, right, turn = tables
     points = turn.shape[0]
     lines = source.shape[0]
     count = len(complex_rows(beams))
     fetched = (interp, chosen, left, turn, right, spectrum)
     out_rows = HYPS * beams * 2 * (points // segments) + 16
-    return pl.pallas_call(
-        functools.partial(correlate_kernel, beams, segments),
-        out_shape=jax.ShapeDtypeStruct((segments, out_rows, BLOCK), BF16),
-        in_specs=[VMEM] + [ANY] * len(fetched),
-        out_specs=VMEM,
+    if paired:
+        shape = jax.ShapeDtypeStruct((segments // 2 * (out_rows - 16) + 16, BLOCK), BF16)
+        out_shape, out_specs = (shape, shape), (VMEM, VMEM)
+    else:
+        out_shape, out_specs = jax.ShapeDtypeStruct((segments, out_rows, BLOCK), BF16), VMEM
+    return pl.pallas_call(
+        functools.partial(correlate_kernel, beams, segments, paired),
+        out_shape=out_shape,
+        in_specs=[SMEM, VMEM] + [ANY] * len(fetched),
+        out_specs=out_specs,
         scratch_shapes=[pltpu.VMEM(array.shape, array.dtype) for array in fetched]
         + [
             pltpu.SemaphoreType.DMA((len(fetched),)),
@@ -312,7 +346,7 @@
         compiler_params=pltpu.CompilerParams(vmem_limit_bytes=56 * 1024 * 1024),
         cost_estimate=pl.CostEstimate(flops=4_000_000_000, bytes_accessed=6_000_000, transcendentals=0),
         name="warp_correlate",
-    )(source, *fetched)
+    )(place, source, *fetched)
 
 
 def finish_kernel(count, power_ref, sums_ref, out_ref, scratch_ref):
@@ -352,16 +386,97 @@
     )(received, received)
 
 
+def arrange_kernel(place_ref, mine_ref, got_ref, *out_refs):
+    chip = place_ref[0] // 2
+    count = len(out_refs)
+    lines = (mine_ref.shape[0] - 16) // count
+    tails = [ref[count * lines :, :] for ref in (mine_ref, got_ref)]
+    tail = tail_of([total[:, :1] for total in totals_of(tails)])
+    for offset, out_ref in enumerate(out_refs):
+        rows = pl.ds(pl.multiple_of((chip ^ offset) * lines, lines), lines)
+        out_ref[:lines, :] = mine_ref[rows, :]
+        out_ref[lines : 2 * lines, :] = got_ref[rows, :]
+        out_ref[2 * lines :, :] = tail
+
+
+def arrange(place, mine, got, chips):
+    lines = (mine.shape[0] - 16) // chips
+    shape = jax.ShapeDtypeStruct((2 * lines + 16, BLOCK), BF16)
+    return pl.pallas_call(
+        arrange_kernel,
+        out_shape=[shape] * chips,
+        in_specs=[SMEM, VMEM, VMEM],
+        out_specs=[VMEM] * chips,
+        compiler_params=pltpu.CompilerParams(vmem_limit_bytes=16 * 1024 * 1024),
+        cost_estimate=pl.CostEstimate(flops=1_000_000, bytes_accessed=1_200_000, transcendentals=0),
+        name="arrange_chips",
+    )(place, mine, got)
+
+
+def join_kernel(count, place_ref, *refs):
+    chunk_refs, out_ref, scratch_ref = refs[:-2], refs[-2], refs[-1]
+    chip, core = place_ref[0] // 2, place_ref[0] % 2
+    lines = chunk_refs[0].shape[0] - 16
+    totals = totals_of([ref[lines:, :] for ref in chunk_refs])
+    inverse = [1.0 / (total / count + 1e-06) for total in totals]
+    run = lines // 2 // HYPS
+    for offset, ref in enumerate(chunk_refs):
+        for part in range(2):
+            start = pl.multiple_of(((chip ^ offset) * 2 + (core ^ part)) * run, run)
+            for hyp in range(HYPS):
+                first = (part * HYPS + hyp) * run
+                scratch_ref[hyp, pl.ds(start, run), :] = ref[first : first + run, :].astype(F32) * inverse[hyp]
+    beams = out_ref.shape[1]
+    step = scratch_ref.shape[1] // beams
+    for hyp in range(HYPS):
+        for line in range(step):
+            half, block = divmod(line, step // 2)
+            lane = block * PAIR + half * BLOCK
+            out_ref[hyp, :, lane : lane + BLOCK] = scratch_ref[hyp, pl.ds(line, beams, stride=step), :].astype(BF16)
+
+
+def join(place, chunks, count, beams):
+    lines = chunks[0].shape[0] - 16
+    rows = lines // HYPS * len(chunks)
+    return pl.pallas_call(
+        functools.partial(join_kernel, count),
+        out_shape=jax.ShapeDtypeStruct((HYPS, beams, rows // beams * BLOCK), BF16),
+        in_specs=[SMEM] + [VMEM] * len(chunks),
+        out_specs=VMEM,
+        scratch_shapes=[pltpu.VMEM((HYPS, rows, BLOCK), F32)],
+        compiler_params=pltpu.CompilerParams(vmem_limit_bytes=16 * 1024 * 1024),
+        cost_estimate=pl.CostEstimate(flops=1_000_000, bytes_accessed=1_200_000, transcendentals=0),
+        name="scale_power",
+    )(place, *chunks)
+
+
+def exchange(value, offset, segments):
+    return lax.ppermute(value, "tm", [(index, index ^ offset) for index in range(segments)])
+
+
 def body(signal, warp_blocks, taps, tap_weights, replica):
     segments = lax.axis_size("tm")
     beams = signal.shape[0] // segments
     samples = signal.shape[1] * segments
+    count = float(BEAMS * samples)
+    paired = segments == 16
+    place = lax.axis_index("tm").astype(jnp.int32).reshape(1)
     received = lax.all_to_all(spread(signal, segments), "tm", split_axis=0, concat_axis=0, tiled=True)
     tables = transform_tables(samples // PAIR)
     interp, chosen, spectrum = prepare(replica, taps, tap_weights, warp_blocks, tables)
-    sent = correlate(received.reshape(-1, BLOCK), interp, chosen, spectrum, tables, beams, segments)
-    back = lax.all_to_all(sent, "tm", split_axis=0, concat_axis=0, tiled=True)
-    return finish(back, float(BEAMS * samples), beams)
+    sent = correlate(
+        place, received.reshape(-1, BLOCK), interp, chosen, spectrum, tables, beams, segments, paired
+    )
+    if not paired:
+        back = lax.all_to_all(sent, "tm", split_axis=0, concat_axis=0, tiled=True)
+        return finish(back, count, beams)
+    mine, theirs = sent
+    chips = segments // 2
+    chunks = arrange(place, mine, exchange(theirs, 1, segments), chips)
+    order = [offset for offset in (5, 4, 7, 6, 3, 2, 1) if offset < chips]
+    arrived = {offset: exchange(chunks[offset], 2 * offset, segments) for offset in order}
+    arrived[0] = chunks[0]
+    return join(place, [arrived[offset] for offset in range(chips)], count, signal.shape[0])
 
 
 def solution(mesh):

time: 50 us -> 46.2 us (0.924)
  blocking collectives: 21.5 us -> 0 us
  starting transfers between devices: 7.52 us -> 18.8 us
  waiting for transfers between devices: 5.05 us -> 11.5 us
  local copies, waits for them, and re-layouts: 2.46 us -> 3.43 us
  Pallas kernels: 12.9 us -> 12 us
    all_to_all x1 -> x0, blocking collectives: 21.5 us -> none  [body(): back = lax.all_to_all(sent, 'tm', split_axis=0, concat_axis=0, tiled=True)]
    ppermute x0 -> x8, starting transfers between devices: none -> 11.3 us  [exchange(): lax.ppermute(value, 'tm', [(index, index ^ offset) for index in range(seg...]
    ppermute x0 -> x8, waiting for transfers between devices: none -> 6.4 us  [exchange(): lax.ppermute(value, 'tm', [(index, index ^ offset) for index in range(seg...]
    unnamed x6 -> x8, local copies, waits for them, and re-layouts: 0.74 us -> 1.7 us
    pallas_call x2 -> x3, Pallas kernels: 8 us -> 7.13 us  [the longest x1 5.79 us: correlate(): pl.pallas_call(functools.partial(correlate_kernel, beams, segments, paire...]
  transfers between devices with their start and end apart: 1 -> 9, of which waited for: 1 -> 4; matrix products, arithmetic and copies ran while one was open for 3% -> 4% of each run, Pallas kernels for 6% -> 7%
where the time goes in v1:
time: 46.2 us; the launch traced here: 45.8 us
  starting transfers between devices  18.8 us (41%)
  Pallas kernels  12 us (26%)
  waiting for transfers between devices  11.5 us (25%)
  local copies, waits for them, and re-layouts  3.43 us (7%)
    ppermute x8, starting transfers between devices, exchange(): lax.ppermute(value, 'tm', [(index, index ^ offset) for index in range(seg...  11.3 us
    all_to_all x1, starting transfers between devices, body(): lax.all_to_all(spread(signal, segments), 'tm', split_axis=0, concat_axis=...  7.52 us
    ppermute x8, waiting for transfers between devices, exchange(): lax.ppermute(value, 'tm', [(index, index ^ offset) for index in range(seg...  6.4 us
    pallas_call x1, Pallas kernels, correlate(): pl.pallas_call(functools.partial(correlate_kernel, beams, segments, paire...  5.79 us
    all_to_all x1, waiting for transfers between devices, body(): lax.all_to_all(spread(signal, segments), 'tm', split_axis=0, concat_axis=...  5.05 us
    pallas_call x1, Pallas kernels, prepare(): pl.pallas_call(prepare_kernel, grid=(1,), out_shape=[jax.ShapeDtypeStruct...  3.21 us
    pallas_call x1, Pallas kernels, spread(): pl.pallas_call(spread_kernel, out_shape=jax.ShapeDtypeStruct((segments, b...  1.71 us
    unnamed x8, local copies, waits for them, and re-layouts  1.7 us
  transfers between devices with their start and end apart: 9, of which 4 were waited for; matrix products, arithmetic and copies ran while one was open for 4% of the time, Pallas kernels for 7%

profile of v1, /device:TPU:0, one launch (start us, length us, event | category | flops | bytes accessed | tf_op | source)
XLA Modules:
  0.0 45.8 jit_solution(9500617173773399218)
XLA Ops:
  0.0 1.7 %spread_beams.1 = bf16[16,64,128]{2,1,0:T(8,128)(2,1)} custom-call(bf16[64,2048]{1,0:T(8,128)(2,1)} %signal_ref.1), custom_call_target="tpu_custom_call" | custom-call | tf_op jit(solution)/shard_map/spread_beams/pallas_call | solution.py:79
  1.7 0.0 copy-start.2
  1.7 7.5 %all-to-all-start = ((bf16[16,64,128]{2,1,0:T(8,128)(2,1)}), bf16[16,64,128]{2,1,0:T(8,128)(2,1)S(1)}, u32[]{:S(2)}, u32[]{:S(2)}) async-start(bf16[16,64,128]{2,1,0:T(8,128)(2,1)} %spread_beams.1), calls=%async_computation | async-start | bytes 524288 | tf_op jit(solution)/shard_map/all_to_all | solution.py:464
  9.2 0.0 copy-done.2
  9.3 0.0 copy-start.3
  9.3 0.6 %reshape.17.replica_ref = f32[64,256]{1,0:T(8,128)} reshape(f32[16384]{0:T(1024)S(1)} %copy-done.2) | data formatting | bytes 131072 | tf_op jit(solution)/shard_map/reshape | solution.py:124
  9.9 0.0 copy-done.3
  9.9 0.1 reshape.18
  10.1 0.1 copy.10
  10.2 0.9 %copy.11.sources_ref = s32[512,1]{1,0:T(8,128)} copy(s32[512,1]{0,1:T(1,128)S(1)} %bitcast.10) | data formatting | bytes 4096 | tf_op jit(solution)/shard_map/reshape | solution.py:123
  11.0 3.2 %prepare_tables.1 = (bf16[256,256]{1,0:T(8,128)(2,1)}, bf16[512,256]{1,0:T(8,128)(2,1)}, f32[128,512]{1,0:T(8,128)}) custom-call(f32[64,256]{1,0:T(8,128)} %reshape.17.replica_ref, s32[2,8,128]{2,1,0:T(8,128)} %bitcast.8, f32[2,8,128]{2,1,0:T(8,128)} %bitcast.9, s32[512,1]{1,0:T(8,128)} %copy.11.sources_ref, ...), custom_call_target="tpu_custom_call" | custom-call | flops 500000000 | bytes 16000000 | tf_op jit(solution)/shard_map/prepare_tables/pallas_call | solution.py:130
  14.2 5.1 %all-to-all-done = bf16[16,64,128]{2,1,0:T(8,128)(2,1)S(1)} async-done(((bf16[16,64,128]{2,1,0:T(8,128)(2,1)}), bf16[16,64,128]{2,1,0:T(8,128)(2,1)S(1)}, u32[]{:S(2)}, u32[]{:S(2)}) %all-to-all-start) | async-done | bytes 262176 | tf_op jit(solution)/shard_map/all_to_all | solution.py:464
  19.3 0.0 copy-start.1
  19.3 0.7 %copy-done.1 = bf16[16,64,128]{2,1,0:T(8,128)(2,1)} copy-done((bf16[16,64,128]{2,1,0:T(8,128)(2,1)}, bf16[16,64,128]{2,1,0:T(8,128)(2,1)S(1)}, u32[]{:S(2)}) %copy-start.1) | copy-done | bytes 262168
  20.0 5.8 %warp_correlate.1 = (bf16[1040,128]{1,0:T(8,128)(2,1)}, bf16[1040,128]{1,0:T(8,128)(2,1)}) custom-call(s32[1]{0:T(128)} %bitcast.place_ref, bf16[1024,128]{1,0:T(8,128)(2,1)} %bitcast.7, bf16[256,256]{1,0:T(8,128)(2,1)} %get-tuple-element.18.interp_hbm, bf16[512,256]{1,0:T(8,128)(2,1)} %get-tuple-element.19.chosen_hbm, ...), custom_call_target="tpu_custom_call" | custom-call | flops 4000000000 | bytes 6000000 | tf_op jit(solution)/shard_map/warp_correlate/pallas_call | solution.py:332
  25.8 0.1 collective-permute-start
  25.9 1.7 %collective-permute-done.got_ref = bf16[1040,128]{1,0:T(8,128)(2,1)S(1)} collective-permute-done((bf16[1040,128]{1,0:T(8,128)(2,1)}, bf16[1040,128]{1,0:T(8,128)(2,1)S(1)}, u32[]{:S(2)}, u32[]{:S(2)}) %collective-permute-start) | collective-permute-done | bytes 266272 | tf_op jit(solution)/shard_map/ppermute | solution.py:454
  27.6 0.0 copy-start
  27.6 0.9 %copy-done = bf16[1040,128]{1,0:T(8,128)(2,1)S(1)} copy-done((bf16[1040,128]{1,0:T(8,128)(2,1)S(1)}, bf16[1040,128]{1,0:T(8,128)(2,1)}, u32[]{:S(2)}) %copy-start) | copy-done | bytes 266264
  28.6 0.1 arrange_chips.1
  28.7 0.2 collective-permute-start.1
  28.9 1.0 %collective-permute-start.2 = (bf16[272,128]{1,0:T(8,128)(2,1)S(1)}, bf16[272,128]{1,0:T(8,128)(2,1)S(1)}, u32[]{:S(2)}, u32[]{:S(2)}) collective-permute-start(bf16[272,128]{1,0:T(8,128)(2,1)S(1)} %get-tuple-element.25), channel_id=1, source_target_pairs={{0,4},{1,5},{2,6},{3,7},{4,0},{5,1},{6,2},{7,3},{8,12},{9,13},{10,... | collective-permute-start | bytes 208904 | tf_op jit(solution)/shard_map/ppermute | solution.py:454
  29.9 2.3 %collective-permute-start.3 = (bf16[272,128]{1,0:T(8,128)(2,1)S(1)}, bf16[272,128]{1,0:T(8,128)(2,1)S(1)}, u32[]{:S(2)}, u32[]{:S(2)}) collective-permute-start(bf16[272,128]{1,0:T(8,128)(2,1)S(1)} %get-tuple-element.26), channel_id=1, source_target_pairs={{0,6},{1,7},{2,4},{3,5},{4,2},{5,3},{6,0},{7,1},{8,14},{9,15},{10,... | collective-permute-start | bytes 208904 | tf_op jit(solution)/shard_map/ppermute | solution.py:454
  32.2 1.1 %collective-permute-start.4 = (bf16[272,128]{1,0:T(8,128)(2,1)S(1)}, bf16[272,128]{1,0:T(8,128)(2,1)S(1)}, u32[]{:S(2)}, u32[]{:S(2)}) collective-permute-start(bf16[272,128]{1,0:T(8,128)(2,1)S(1)} %get-tuple-element.27), channel_id=1, source_target_pairs={{0,8},{1,9},{2,10},{3,11},{4,12},{5,13},{6,14},{7,15},{8,0},{9,1},... | collective-permute-start | bytes 208904 | tf_op jit(solution)/shard_map/ppermute | solution.py:454
  33.3 1.5 %collective-permute-start.5 = (bf16[272,128]{1,0:T(8,128)(2,1)S(1)}, bf16[272,128]{1,0:T(8,128)(2,1)S(1)}, u32[]{:S(2)}, u32[]{:S(2)}) collective-permute-start(bf16[272,128]{1,0:T(8,128)(2,1)S(1)} %get-tuple-element.28), channel_id=1, source_target_pairs={{0,10},{1,11},{2,8},{3,9},{4,14},{5,15},{6,12},{7,13},{8,2},{9,3},... | collective-permute-start | bytes 208904 | tf_op jit(solution)/shard_map/ppermute | solution.py:454
  34.8 0.0 collective-permute-done.1.refs_1_
  34.8 2.0 %collective-permute-start.6 = (bf16[272,128]{1,0:T(8,128)(2,1)S(1)}, bf16[272,128]{1,0:T(8,128)(2,1)S(1)}, u32[]{:S(2)}, u32[]{:S(2)}) collective-permute-start(bf16[272,128]{1,0:T(8,128)(2,1)S(1)} %get-tuple-element.29), channel_id=1, source_target_pairs={{0,12},{1,13},{2,14},{3,15},{4,8},{5,9},{6,10},{7,11},{8,4},{9,5},... | collective-permute-start | bytes 208904 | tf_op jit(solution)/shard_map/ppermute | solution.py:454
  36.8 0.0 collective-permute-done.2.refs_2_
  36.8 3.1 %collective-permute-start.7 = (bf16[272,128]{1,0:T(8,128)(2,1)S(1)}, bf16[272,128]{1,0:T(8,128)(2,1)S(1)}, u32[]{:S(2)}, u32[]{:S(2)}) collective-permute-start(bf16[272,128]{1,0:T(8,128)(2,1)S(1)} %get-tuple-element.30), channel_id=1, source_target_pairs={{0,14},{1,15},{2,12},{3,13},{4,10},{5,11},{6,8},{7,9},{8,6},{9,7},... | collective-permute-start | bytes 208904 | tf_op jit(solution)/shard_map/ppermute | solution.py:454
  39.9 0.0 collective-permute-done.3.refs_3_
  39.9 2.5 %collective-permute-done.4.refs_4_ = bf16[272,128]{1,0:T(8,128)(2,1)S(1)} collective-permute-done((bf16[272,128]{1,0:T(8,128)(2,1)S(1)}, bf16[272,128]{1,0:T(8,128)(2,1)S(1)}, u32[]{:S(2)}, u32[]{:S(2)}) %collective-permute-start.4) | collective-permute-done | bytes 69664 | tf_op jit(solution)/shard_map/ppermute | solution.py:454
  42.4 2.1 %collective-permute-done.5.refs_5_ = bf16[272,128]{1,0:T(8,128)(2,1)S(1)} collective-permute-done((bf16[272,128]{1,0:T(8,128)(2,1)S(1)}, bf16[272,128]{1,0:T(8,128)(2,1)S(1)}, u32[]{:S(2)}, u32[]{:S(2)}) %collective-permute-start.5) | collective-permute-done | bytes 69664 | tf_op jit(solution)/shard_map/ppermute | solution.py:454
  44.5 0.0 collective-permute-done.6.refs_6_
  44.5 0.0 collective-permute-done.7.refs_7_
  44.5 1.2 %scale_power.1 = bf16[2,64,2048]{2,1,0:T(8,128)(2,1)} custom-call(s32[1]{0:T(128)} %bitcast.place_ref, bf16[272,128]{1,0:T(8,128)(2,1)S(1)} %get-tuple-element.23.refs_0_, bf16[272,128]{1,0:T(8,128)(2,1)S(1)} %collective-permute-done.1.refs_1_, bf16[272,128]{1,0:T(8,128)(2,1)S(1)} %collective-permute-done.2.refs_2_, ...), custom_call_target="tpu_custom_call" | custom-call | flops 1000000 | bytes 1200000 | tf_op jit(solution)/shard_map/scale_power/pallas_call | solution.py:441
Async XLA Ops:
  1.7 7.5 %copy-start.2 = (f32[16384]{0:T(1024)S(1)}, f32[16384]{0:T(1024)}, u32[]{:S(2)}) copy-start(f32[16384]{0:T(1024)} %param.12) | copy-start | bytes 196612
  1.7 17.6 %all-to-all-start = ((bf16[16,64,128]{2,1,0:T(8,128)(2,1)}), bf16[16,64,128]{2,1,0:T(8,128)(2,1)S(1)}, u32[]{:S(2)}, u32[]{:S(2)}) async-start(bf16[16,64,128]{2,1,0:T(8,128)(2,1)} %spread_beams.1), calls=%async_computation | async-start | bytes 524288 | tf_op jit(solution)/shard_map/all_to_all | solution.py:464
  9.3 0.7 %copy-start.3 = (s32[2,256]{1,0:T(2,128)S(1)}, s32[2,256]{1,0:T(2,128)}, u32[]{:S(2)}) copy-start(s32[2,256]{1,0:T(2,128)} %param.9) | copy-start | bytes 6148
  19.3 0.7 %copy-start.1 = (bf16[16,64,128]{2,1,0:T(8,128)(2,1)}, bf16[16,64,128]{2,1,0:T(8,128)(2,1)S(1)}, u32[]{:S(2)}) copy-start(bf16[16,64,128]{2,1,0:T(8,128)(2,1)S(1)} %all-to-all-done) | copy-start | bytes 786436
  25.8 1.8 %collective-permute-start = (bf16[1040,128]{1,0:T(8,128)(2,1)}, bf16[1040,128]{1,0:T(8,128)(2,1)S(1)}, u32[]{:S(2)}, u32[]{:S(2)}) collective-permute-start(bf16[1040,128]{1,0:T(8,128)(2,1)} %get-tuple-element.22), channel_id=1, source_target_pairs={{0,1},{1,0},{2,3},{3,2},{4,5},{5,4},{6,7},{7,6},{8,9},{9,8},{10,11... | collective-permute-start | bytes 798728 | tf_op jit(solution)/shard_map/ppermute | solution.py:454
  27.6 1.0 %copy-start = (bf16[1040,128]{1,0:T(8,128)(2,1)S(1)}, bf16[1040,128]{1,0:T(8,128)(2,1)}, u32[]{:S(2)}) copy-start(bf16[1040,128]{1,0:T(8,128)(2,1)} %get-tuple-element.21.mine_ref) | copy-start | bytes 798724
  28.7 6.1 %collective-permute-start.1 = (bf16[272,128]{1,0:T(8,128)(2,1)S(1)}, bf16[272,128]{1,0:T(8,128)(2,1)S(1)}, u32[]{:S(2)}, u32[]{:S(2)}) collective-permute-start(bf16[272,128]{1,0:T(8,128)(2,1)S(1)} %get-tuple-element.24), channel_id=1, source_target_pairs={{0,2},{1,3},{2,0},{3,1},{4,6},{5,7},{6,4},{7,5},{8,10},{9,11},{10,... | collective-permute-start | bytes 208904 | tf_op jit(solution)/shard_map/ppermute | solution.py:454
  28.9 7.8 %collective-permute-start.2 = (bf16[272,128]{1,0:T(8,128)(2,1)S(1)}, bf16[272,128]{1,0:T(8,128)(2,1)S(1)}, u32[]{:S(2)}, u32[]{:S(2)}) collective-permute-start(bf16[272,128]{1,0:T(8,128)(2,1)S(1)} %get-tuple-element.25), channel_id=1, source_target_pairs={{0,4},{1,5},{2,6},{3,7},{4,0},{5,1},{6,2},{7,3},{8,12},{9,13},{10,... | collective-permute-start | bytes 208904 | tf_op jit(solution)/shard_map/ppermute | solution.py:454
  29.9 10.0 %collective-permute-start.3 = (bf16[272,128]{1,0:T(8,128)(2,1)S(1)}, bf16[272,128]{1,0:T(8,128)(2,1)S(1)}, u32[]{:S(2)}, u32[]{:S(2)}) collective-permute-start(bf16[272,128]{1,0:T(8,128)(2,1)S(1)} %get-tuple-element.26), channel_id=1, source_target_pairs={{0,6},{1,7},{2,4},{3,5},{4,2},{5,3},{6,0},{7,1},{8,14},{9,15},{10,... | collective-permute-start | bytes 208904 | tf_op jit(solution)/shard_map/ppermute | solution.py:454
  32.2 10.2 %collective-permute-start.4 = (bf16[272,128]{1,0:T(8,128)(2,1)S(1)}, bf16[272,128]{1,0:T(8,128)(2,1)S(1)}, u32[]{:S(2)}, u32[]{:S(2)}) collective-permute-start(bf16[272,128]{1,0:T(8,128)(2,1)S(1)} %get-tuple-element.27), channel_id=1, source_target_pairs={{0,8},{1,9},{2,10},{3,11},{4,12},{5,13},{6,14},{7,15},{8,0},{9,1},... | collective-permute-start | bytes 208904 | tf_op jit(solution)/shard_map/ppermute | solution.py:454
  33.3 11.2 %collective-permute-start.5 = (bf16[272,128]{1,0:T(8,128)(2,1)S(1)}, bf16[272,128]{1,0:T(8,128)(2,1)S(1)}, u32[]{:S(2)}, u32[]{:S(2)}) collective-permute-start(bf16[272,128]{1,0:T(8,128)(2,1)S(1)} %get-tuple-element.28), channel_id=1, source_target_pairs={{0,10},{1,11},{2,8},{3,9},{4,14},{5,15},{6,12},{7,13},{8,2},{9,3},... | collective-permute-start | bytes 208904 | tf_op jit(solution)/shard_map/ppermute | solution.py:454
  34.8 9.8 %collective-permute-start.6 = (bf16[272,128]{1,0:T(8,128)(2,1)S(1)}, bf16[272,128]{1,0:T(8,128)(2,1)S(1)}, u32[]{:S(2)}, u32[]{:S(2)}) collective-permute-start(bf16[272,128]{1,0:T(8,128)(2,1)S(1)} %get-tuple-element.29), channel_id=1, source_target_pairs={{0,12},{1,13},{2,14},{3,15},{4,8},{5,9},{6,10},{7,11},{8,4},{9,5},... | collective-permute-start | bytes 208904 | tf_op jit(solution)/shard_map/ppermute | solution.py:454
  36.8 7.8 %collective-permute-start.7 = (bf16[272,128]{1,0:T(8,128)(2,1)S(1)}, bf16[272,128]{1,0:T(8,128)(2,1)S(1)}, u32[]{:S(2)}, u32[]{:S(2)}) collective-permute-start(bf16[272,128]{1,0:T(8,128)(2,1)S(1)} %get-tuple-element.30), channel_id=1, source_target_pairs={{0,14},{1,15},{2,12},{3,13},{4,10},{5,11},{6,8},{7,9},{8,6},{9,7},... | collective-permute-start | bytes 208904 | tf_op jit(solution)/shard_map/ppermute | solution.py:454

commit v2 on v1

--- a/solution.py
+++ b/solution.py
@@ -132,8 +132,8 @@
         grid=(1,),
         out_shape=[jax.ShapeDtypeStruct(*shape) for shape in shapes],
         in_specs=[whole(operand.shape) for operand in operands],
-        out_specs=[whole(shape[0]) for shape in shapes],
-        compiler_params=pltpu.CompilerParams(vmem_limit_bytes=56 * 1024 * 1024),
+        out_specs=[VMEM] * len(shapes),
+        compiler_params=pltpu.CompilerParams(vmem_limit_bytes=24 * 1024 * 1024),
         cost_estimate=pl.CostEstimate(flops=500_000_000, bytes_accessed=16_000_000, transcendentals=0),
         name="prepare_tables",
     )(*operands)
@@ -343,7 +343,7 @@
             pltpu.VMEM((count * points, 2 * PAIR), BF16),
             pltpu.VMEM((count * points, 2 * PAIR), F32),
         ],
-        compiler_params=pltpu.CompilerParams(vmem_limit_bytes=56 * 1024 * 1024),
+        compiler_params=pltpu.CompilerParams(vmem_limit_bytes=24 * 1024 * 1024),
         cost_estimate=pl.CostEstimate(flops=4_000_000_000, bytes_accessed=6_000_000, transcendentals=0),
         name="warp_correlate",
     )(place, source, *fetched)
@@ -386,13 +386,18 @@
     )(received, received)
 
 
+def chip_order(chips):
+    far, near = range(chips // 2, chips), [*range(1, chips // 2), 0]
+    return [offset for pair in zip(far, near) for offset in pair][:-1] + [0]
+
+
 def arrange_kernel(place_ref, mine_ref, got_ref, *out_refs):
     chip = place_ref[0] // 2
     count = len(out_refs)
     lines = (mine_ref.shape[0] - 16) // count
     tails = [ref[count * lines :, :] for ref in (mine_ref, got_ref)]
     tail = tail_of([total[:, :1] for total in totals_of(tails)])
-    for offset, out_ref in enumerate(out_refs):
+    for offset, out_ref in zip(chip_order(count), out_refs):
         rows = pl.ds(pl.multiple_of((chip ^ offset) * lines, lines), lines)
         out_ref[:lines, :] = mine_ref[rows, :]
         out_ref[lines : 2 * lines, :] = got_ref[rows, :]
@@ -420,7 +425,7 @@
     totals = totals_of([ref[lines:, :] for ref in chunk_refs])
     inverse = [1.0 / (total / count + 1e-06) for total in totals]
     run = lines // 2 // HYPS
-    for offset, ref in enumerate(chunk_refs):
+    for offset, ref in zip(chip_order(len(chunk_refs)), chunk_refs):
         for part in range(2):
             start = pl.multiple_of(((chip ^ offset) * 2 + (core ^ part)) * run, run)
             for hyp in range(HYPS):
@@ -473,10 +478,10 @@
     mine, theirs = sent
     chips = segments // 2
     chunks = arrange(place, mine, exchange(theirs, 1, segments), chips)
-    order = [offset for offset in (5, 4, 7, 6, 3, 2, 1) if offset < chips]
-    arrived = {offset: exchange(chunks[offset], 2 * offset, segments) for offset in order}
-    arrived[0] = chunks[0]
-    return join(place, [arrived[offset] for offset in range(chips)], count, signal.shape[0])
+    arrived = [
+        exchange(chunk, 2 * offset, segments) if offset else chunk for offset, chunk in zip(chip_order(chips), chunks)
+    ]
+    return join(place, arrived, count, signal.shape[0])
 
 
 def solution(mesh):

time: 46.2 us -> 41 us (0.89)
  Pallas kernels: 12 us -> 7.58 us
  waiting for transfers between devices: 11.5 us -> 14.5 us
  starting transfers between devices: 18.8 us -> 16.7 us
  local copies, waits for them, and re-layouts: 3.43 us -> 1.87 us
    pallas_call x1, Pallas kernels: 5.79 us -> 3.43 us  [correlate(): pl.pallas_call(functools.partial(correlate_kernel, beams, segments, paire...]
    pallas_call x1, Pallas kernels: 3.21 us -> 1.01 us  [prepare(): pl.pallas_call(prepare_kernel, grid=(1,), out_shape=[jax.ShapeDtypeStruct...]
    all_to_all x1, waiting for transfers between devices: 5.05 us -> 7.08 us  [body(): lax.all_to_all(spread(signal, segments), 'tm', split_axis=0, concat_axis=...]
    ppermute x8, starting transfers between devices: 11.3 us -> 9.28 us  [exchange(): lax.ppermute(value, 'tm', [(index, index ^ offset) for index in range(seg...]
    unnamed x8 -> x12, local copies, waits for them, and re-layouts: 1.7 us -> 0.63 us
    ppermute x8, waiting for transfers between devices: 6.4 us -> 7.39 us  [exchange(): lax.ppermute(value, 'tm', [(index, index ^ offset) for index in range(seg...]
    reshape x2, local copies, waits for them, and re-layouts: 1 us -> 0.3 us  [prepare(): warp_blocks.reshape(HYPS, points, 2).transpose(0, 2, 1)]
  transfers between devices with their start and end apart: 9 -> 9, of which waited for: 4 -> 7; matrix products, arithmetic and copies ran while one was open for 4% -> 3% of each run, Pallas kernels for 7% -> 2%
where the time goes in v2:
time: 41 us; the launch traced here: 40.7 us
  starting transfers between devices  16.7 us (41%)
  waiting for transfers between devices  14.5 us (35%)
  Pallas kernels  7.58 us (18%)
  local copies, waits for them, and re-layouts  1.87 us (5%)
    ppermute x8, starting transfers between devices, exchange(): lax.ppermute(value, 'tm', [(index, index ^ offset) for index in range(seg...  9.28 us
    ppermute x8, waiting for transfers between devices, exchange(): lax.ppermute(value, 'tm', [(index, index ^ offset) for index in range(seg...  7.39 us
    all_to_all x1, starting transfers between devices, body(): lax.all_to_all(spread(signal, segments), 'tm', split_axis=0, concat_axis=...  7.39 us
    all_to_all x1, waiting for transfers between devices, body(): lax.all_to_all(spread(signal, segments), 'tm', split_axis=0, concat_axis=...  7.08 us
    pallas_call x1, Pallas kernels, correlate(): pl.pallas_call(functools.partial(correlate_kernel, beams, segments, paire...  3.43 us
    pallas_call x1, Pallas kernels, spread(): pl.pallas_call(spread_kernel, out_shape=jax.ShapeDtypeStruct((segments, b...  1.8 us
    pallas_call x1, Pallas kernels, join(): pl.pallas_call(functools.partial(join_kernel, count), out_shape=jax.Shape...  1.23 us
    pallas_call x1, Pallas kernels, prepare(): pl.pallas_call(prepare_kernel, grid=(1,), out_shape=[jax.ShapeDtypeStruct...  1.01 us
  transfers between devices with their start and end apart: 9, of which 7 were waited for; matrix products, arithmetic and copies ran while one was open for 3% of the time, Pallas kernels for 2%

profile of v2, /device:TPU:0, one launch (start us, length us, event | category | flops | bytes accessed | tf_op | source)
XLA Modules:
  0.0 40.7 jit_solution(17551974464305031847)
XLA Ops:
  0.0 0.0 copy-start
  0.0 1.8 %spread_beams.1 = bf16[16,64,128]{2,1,0:T(8,128)(2,1)} custom-call(bf16[64,2048]{1,0:T(8,128)(2,1)} %signal_ref.1), custom_call_target="tpu_custom_call" | custom-call | tf_op jit(solution)/shard_map/spread_beams/pallas_call | solution.py:79
  1.8 7.4 %all-to-all-start = ((bf16[16,64,128]{2,1,0:T(8,128)(2,1)}), bf16[16,64,128]{2,1,0:T(8,128)(2,1)S(1)}, u32[]{:S(2)}, u32[]{:S(2)}) async-start(bf16[16,64,128]{2,1,0:T(8,128)(2,1)} %spread_beams.1), calls=%async_computation | async-start | bytes 524288 | tf_op jit(solution)/shard_map/all_to_all | solution.py:469
  9.2 0.0 copy-start.5
  9.2 0.0 copy-start.4
  9.2 0.9 %reshape.17.replica_ref = f32[64,256]{1,0:T(8,128)S(1)} reshape(f32[16384]{0:T(1024)} %param.12) | data formatting | bytes 131072 | tf_op jit(solution)/shard_map/reshape | solution.py:124
  10.1 0.0 copy-done.5
  10.1 0.0 copy-start.1
  10.1 0.0 copy-start.2
  10.1 0.1 reshape.18
  10.3 0.1 copy.10
  10.4 0.0 copy-start.3
  10.4 0.2 copy.11.sources_ref
  10.5 0.0 copy-done
  10.5 0.0 copy-done.4
  10.5 0.5 %copy-done.1 = f32[128,512]{1,0:T(8,128)S(1)} copy-done((f32[128,512]{1,0:T(8,128)S(1)}, f32[128,512]{1,0:T(8,128)}, u32[]{:S(2)}) %copy-start.1) | copy-done | bytes 262168
  11.1 0.1 copy-done.2
  11.1 0.0 copy-done.3
  11.1 1.0 %prepare_tables.1 = (bf16[256,256]{1,0:T(8,128)(2,1)S(1)}, bf16[512,256]{1,0:T(8,128)(2,1)S(1)}, f32[128,512]{1,0:T(8,128)S(1)}) custom-call(f32[64,256]{1,0:T(8,128)S(1)} %reshape.17.replica_ref, s32[2,8,128]{2,1,0:T(8,128)S(1)} %bitcast.7, f32[2,8,128]{2,1,0:T(8,128)S(1)} %bitcast.8, s32[512,1]{1,0:T(8,128)S(1)} %copy.11.sources_ref, ...), custom_call_target="tpu_custom_call" | custom-call | flops 500000000 | bytes 16000000 | tf_op jit(solution)/shard_map/prepare_tables/pallas_call | solution.py:130
  12.2 7.1 %all-to-all-done = bf16[16,64,128]{2,1,0:T(8,128)(2,1)S(1)} async-done(((bf16[16,64,128]{2,1,0:T(8,128)(2,1)}), bf16[16,64,128]{2,1,0:T(8,128)(2,1)S(1)}, u32[]{:S(2)}, u32[]{:S(2)}) %all-to-all-start) | async-done | bytes 262176 | tf_op jit(solution)/shard_map/all_to_all | solution.py:469
  19.2 3.4 %warp_correlate.1 = (bf16[1040,128]{1,0:T(8,128)(2,1)S(1)}, bf16[1040,128]{1,0:T(8,128)(2,1)S(1)}) custom-call(s32[1]{0:T(128)} %bitcast.place_ref, bf16[1024,128]{1,0:T(8,128)(2,1)S(1)} %bitcast.6, bf16[256,256]{1,0:T(8,128)(2,1)S(1)} %get-tuple-element.18.interp_hbm, bf16[512,256]{1,0:T(8,128)(2,1)S(1)} %get-tuple-element.19.chosen_hbm, ...), custom_call_target="tpu_custom_call" | custom-call | flops 4000000000 | bytes 6000000 | tf_op jit(solution)/shard_map/warp_correlate/pallas_call | solution.py:332
  22.7 0.1 collective-permute-start
  22.8 1.5 %collective-permute-done.got_ref = bf16[1040,128]{1,0:T(8,128)(2,1)S(1)} collective-permute-done((bf16[1040,128]{1,0:T(8,128)(2,1)S(1)}, bf16[1040,128]{1,0:T(8,128)(2,1)S(1)}, u32[]{:S(2)}, u32[]{:S(2)}) %collective-permute-start) | collective-permute-done | bytes 266272 | tf_op jit(solution)/shard_map/ppermute | solution.py:459
  24.3 0.1 arrange_chips.1
  24.4 1.1 %collective-permute-start.1 = (bf16[272,128]{1,0:T(8,128)(2,1)S(1)}, bf16[272,128]{1,0:T(8,128)(2,1)S(1)}, u32[]{:S(2)}, u32[]{:S(2)}) collective-permute-start(bf16[272,128]{1,0:T(8,128)(2,1)S(1)} %get-tuple-element.23), channel_id=1, source_target_pairs={{0,8},{1,9},{2,10},{3,11},{4,12},{5,13},{6,14},{7,15},{8,0},{9,1},... | collective-permute-start | bytes 208904 | tf_op jit(solution)/shard_map/ppermute | solution.py:459
  25.5 0.0 collective-permute-start.2
  25.5 3.3 %collective-permute-start.3 = (bf16[272,128]{1,0:T(8,128)(2,1)S(1)}, bf16[272,128]{1,0:T(8,128)(2,1)S(1)}, u32[]{:S(2)}, u32[]{:S(2)}) collective-permute-start(bf16[272,128]{1,0:T(8,128)(2,1)S(1)} %get-tuple-element.25), channel_id=1, source_target_pairs={{0,10},{1,11},{2,8},{3,9},{4,14},{5,15},{6,12},{7,13},{8,2},{9,3},... | collective-permute-start | bytes 208904 | tf_op jit(solution)/shard_map/ppermute | solution.py:459
  28.8 0.3 collective-permute-start.4
  29.2 2.2 %collective-permute-start.5 = (bf16[272,128]{1,0:T(8,128)(2,1)S(1)}, bf16[272,128]{1,0:T(8,128)(2,1)S(1)}, u32[]{:S(2)}, u32[]{:S(2)}) collective-permute-start(bf16[272,128]{1,0:T(8,128)(2,1)S(1)} %get-tuple-element.27), channel_id=1, source_target_pairs={{0,12},{1,13},{2,14},{3,15},{4,8},{5,9},{6,10},{7,11},{8,4},{9,5},... | collective-permute-start | bytes 208904 | tf_op jit(solution)/shard_map/ppermute | solution.py:459
  31.4 1.1 %collective-permute-done.1.refs_0_ = bf16[272,128]{1,0:T(8,128)(2,1)S(1)} collective-permute-done((bf16[272,128]{1,0:T(8,128)(2,1)S(1)}, bf16[272,128]{1,0:T(8,128)(2,1)S(1)}, u32[]{:S(2)}, u32[]{:S(2)}) %collective-permute-start.1) | collective-permute-done | bytes 69664 | tf_op jit(solution)/shard_map/ppermute | solution.py:459
  32.5 0.0 collective-permute-start.6
  32.5 0.0 collective-permute-done.2.refs_1_
  32.5 2.2 %collective-permute-start.7 = (bf16[272,128]{1,0:T(8,128)(2,1)S(1)}, bf16[272,128]{1,0:T(8,128)(2,1)S(1)}, u32[]{:S(2)}, u32[]{:S(2)}) collective-permute-start(bf16[272,128]{1,0:T(8,128)(2,1)S(1)} %get-tuple-element.29), channel_id=1, source_target_pairs={{0,14},{1,15},{2,12},{3,13},{4,10},{5,11},{6,8},{7,9},{8,6},{9,7},... | collective-permute-start | bytes 208904 | tf_op jit(solution)/shard_map/ppermute | solution.py:459
  34.7 0.5 %collective-permute-done.3.refs_2_ = bf16[272,128]{1,0:T(8,128)(2,1)S(1)} collective-permute-done((bf16[272,128]{1,0:T(8,128)(2,1)S(1)}, bf16[272,128]{1,0:T(8,128)(2,1)S(1)}, u32[]{:S(2)}, u32[]{:S(2)}) %collective-permute-start.3) | collective-permute-done | bytes 69664 | tf_op jit(solution)/shard_map/ppermute | solution.py:459
  35.2 2.1 %collective-permute-done.4.refs_3_ = bf16[272,128]{1,0:T(8,128)(2,1)S(1)} collective-permute-done((bf16[272,128]{1,0:T(8,128)(2,1)S(1)}, bf16[272,128]{1,0:T(8,128)(2,1)S(1)}, u32[]{:S(2)}, u32[]{:S(2)}) %collective-permute-start.4) | collective-permute-done | bytes 69664 | tf_op jit(solution)/shard_map/ppermute | solution.py:459
  37.3 0.0 collective-permute-done.5.refs_4_
  37.3 1.1 %collective-permute-done.6.refs_5_ = bf16[272,128]{1,0:T(8,128)(2,1)S(1)} collective-permute-done((bf16[272,128]{1,0:T(8,128)(2,1)S(1)}, bf16[272,128]{1,0:T(8,128)(2,1)S(1)}, u32[]{:S(2)}, u32[]{:S(2)}) %collective-permute-start.6) | collective-permute-done | bytes 69664 | tf_op jit(solution)/shard_map/ppermute | solution.py:459
  38.4 1.1 %collective-permute-done.7.refs_6_ = bf16[272,128]{1,0:T(8,128)(2,1)S(1)} collective-permute-done((bf16[272,128]{1,0:T(8,128)(2,1)S(1)}, bf16[272,128]{1,0:T(8,128)(2,1)S(1)}, u32[]{:S(2)}, u32[]{:S(2)}) %collective-permute-start.7) | collective-permute-done | bytes 69664 | tf_op jit(solution)/shard_map/ppermute | solution.py:459
  39.5 1.2 %scale_power.1 = bf16[2,64,2048]{2,1,0:T(8,128)(2,1)} custom-call(s32[1]{0:T(128)} %bitcast.place_ref, bf16[272,128]{1,0:T(8,128)(2,1)S(1)} %collective-permute-done.1.refs_0_, bf16[272,128]{1,0:T(8,128)(2,1)S(1)} %collective-permute-done.2.refs_1_, bf16[272,128]{1,0:T(8,128)(2,1)S(1)} %collective-permute-done.3.refs_2_, ...), custom_call_target="tpu_custom_call" | custom-call | flops 1000000 | bytes 1200000 | tf_op jit(solution)/shard_map/scale_power/pallas_call | solution.py:446
Async XLA Ops:
  0.0 10.5 %copy-start = (bf16[1024,512]{1,0:T(8,128)(2,1)S(1)}, bf16[1024,512]{1,0:T(8,128)(2,1)}, u32[]{:S(2)}) copy-start(bf16[1024,512]{1,0:T(8,128)(2,1)} %constant.11.clone.right_ref.right_hbm) | copy-start | bytes 3145732
  1.8 17.4 %all-to-all-start = ((bf16[16,64,128]{2,1,0:T(8,128)(2,1)}), bf16[16,64,128]{2,1,0:T(8,128)(2,1)S(1)}, u32[]{:S(2)}, u32[]{:S(2)}) async-start(bf16[16,64,128]{2,1,0:T(8,128)(2,1)} %spread_beams.1), calls=%async_computation | async-start | bytes 524288 | tf_op jit(solution)/shard_map/all_to_all | solution.py:469
  9.2 0.9 %copy-start.5 = (s32[2,256]{1,0:T(2,128)S(1)}, s32[2,256]{1,0:T(2,128)}, u32[]{:S(2)}) copy-start(s32[2,256]{1,0:T(2,128)} %param.9) | copy-start | bytes 6148
  9.2 1.3 %copy-start.4 = (f32[2,128,8]{1,2,0:T(8,128)S(1)}, f32[2,128,8]{1,2,0:T(8,128)}, u32[]{:S(2)}) copy-start(f32[2,128,8]{1,2,0:T(8,128)} %param.11) | copy-start | bytes 24580
  10.1 1.0 %copy-start.1 = (f32[128,512]{1,0:T(8,128)S(1)}, f32[128,512]{1,0:T(8,128)}, u32[]{:S(2)}) copy-start(f32[128,512]{1,0:T(8,128)} %constant.12.clone.turn_ref.turn_hbm) | copy-start | bytes 786436
  10.1 1.0 %copy-start.2 = (bf16[512,256]{1,0:T(8,128)(2,1)S(1)}, bf16[512,256]{1,0:T(8,128)(2,1)}, u32[]{:S(2)}) copy-start(bf16[512,256]{1,0:T(8,128)(2,1)} %constant.10.clone.left_ref.left_hbm) | copy-start | bytes 786436
  10.4 0.8 %copy-start.3 = (s32[2,128,8]{1,2,0:T(8,128)S(1)}, s32[2,128,8]{1,2,0:T(8,128)}, u32[]{:S(2)}) copy-start(s32[2,128,8]{1,2,0:T(8,128)} %param.10) | copy-start | bytes 24580
  22.7 1.6 %collective-permute-start = (bf16[1040,128]{1,0:T(8,128)(2,1)S(1)}, bf16[1040,128]{1,0:T(8,128)(2,1)S(1)}, u32[]{:S(2)}, u32[]{:S(2)}) collective-permute-start(bf16[1040,128]{1,0:T(8,128)(2,1)S(1)} %get-tuple-element.22), channel_id=1, source_target_pairs={{0,1},{1,0},{2,3},{3,2},{4,5},{5,4},{6,7},{7,6},{8,9},{9,8},{10,11... | collective-permute-start | bytes 798728 | tf_op jit(solution)/shard_map/ppermute | solution.py:459
  24.4 8.1 %collective-permute-start.1 = (bf16[272,128]{1,0:T(8,128)(2,1)S(1)}, bf16[272,128]{1,0:T(8,128)(2,1)S(1)}, u32[]{:S(2)}, u32[]{:S(2)}) collective-permute-start(bf16[272,128]{1,0:T(8,128)(2,1)S(1)} %get-tuple-element.23), channel_id=1, source_target_pairs={{0,8},{1,9},{2,10},{3,11},{4,12},{5,13},{6,14},{7,15},{8,0},{9,1},... | collective-permute-start | bytes 208904 | tf_op jit(solution)/shard_map/ppermute | solution.py:459
  25.5 6.9 %collective-permute-start.2 = (bf16[272,128]{1,0:T(8,128)(2,1)S(1)}, bf16[272,128]{1,0:T(8,128)(2,1)S(1)}, u32[]{:S(2)}, u32[]{:S(2)}) collective-permute-start(bf16[272,128]{1,0:T(8,128)(2,1)S(1)} %get-tuple-element.24), channel_id=1, source_target_pairs={{0,2},{1,3},{2,0},{3,1},{4,6},{5,7},{6,4},{7,5},{8,10},{9,11},{10,... | collective-permute-start | bytes 208904 | tf_op jit(solution)/shard_map/ppermute | solution.py:459
  25.5 9.7 %collective-permute-start.3 = (bf16[272,128]{1,0:T(8,128)(2,1)S(1)}, bf16[272,128]{1,0:T(8,128)(2,1)S(1)}, u32[]{:S(2)}, u32[]{:S(2)}) collective-permute-start(bf16[272,128]{1,0:T(8,128)(2,1)S(1)} %get-tuple-element.25), channel_id=1, source_target_pairs={{0,10},{1,11},{2,8},{3,9},{4,14},{5,15},{6,12},{7,13},{8,2},{9,3},... | collective-permute-start | bytes 208904 | tf_op jit(solution)/shard_map/ppermute | solution.py:459
  28.8 8.4 %collective-permute-start.4 = (bf16[272,128]{1,0:T(8,128)(2,1)S(1)}, bf16[272,128]{1,0:T(8,128)(2,1)S(1)}, u32[]{:S(2)}, u32[]{:S(2)}) collective-permute-start(bf16[272,128]{1,0:T(8,128)(2,1)S(1)} %get-tuple-element.26), channel_id=1, source_target_pairs={{0,4},{1,5},{2,6},{3,7},{4,0},{5,1},{6,2},{7,3},{8,12},{9,13},{10,... | collective-permute-start | bytes 208904 | tf_op jit(solution)/shard_map/ppermute | solution.py:459
  29.2 8.1 %collective-permute-start.5 = (bf16[272,128]{1,0:T(8,128)(2,1)S(1)}, bf16[272,128]{1,0:T(8,128)(2,1)S(1)}, u32[]{:S(2)}, u32[]{:S(2)}) collective-permute-start(bf16[272,128]{1,0:T(8,128)(2,1)S(1)} %get-tuple-element.27), channel_id=1, source_target_pairs={{0,12},{1,13},{2,14},{3,15},{4,8},{5,9},{6,10},{7,11},{8,4},{9,5},... | collective-permute-start | bytes 208904 | tf_op jit(solution)/shard_map/ppermute | solution.py:459
  32.5 6.0 %collective-permute-start.6 = (bf16[272,128]{1,0:T(8,128)(2,1)S(1)}, bf16[272,128]{1,0:T(8,128)(2,1)S(1)}, u32[]{:S(2)}, u32[]{:S(2)}) collective-permute-start(bf16[272,128]{1,0:T(8,128)(2,1)S(1)} %get-tuple-element.28), channel_id=1, source_target_pairs={{0,6},{1,7},{2,4},{3,5},{4,2},{5,3},{6,0},{7,1},{8,14},{9,15},{10,... | collective-permute-start | bytes 208904 | tf_op jit(solution)/shard_map/ppermute | solution.py:459
  32.5 7.0 %collective-permute-start.7 = (bf16[272,128]{1,0:T(8,128)(2,1)S(1)}, bf16[272,128]{1,0:T(8,128)(2,1)S(1)}, u32[]{:S(2)}, u32[]{:S(2)}) collective-permute-start(bf16[272,128]{1,0:T(8,128)(2,1)S(1)} %get-tuple-element.29), channel_id=1, source_target_pairs={{0,14},{1,15},{2,12},{3,13},{4,10},{5,11},{6,8},{7,9},{8,6},{9,7},... | collective-permute-start | bytes 208904 | tf_op jit(solution)/shard_map/ppermute | solution.py:459

commit v3 on v2

--- a/solution.py
+++ b/solution.py
@@ -22,7 +22,7 @@
 ANY = pl.BlockSpec(memory_space=pl.ANY)
 
 
-def transform_tables(points):
+def transform_tables(points, segments):
     k, p = np.arange(points)[:, None], np.arange(points)[None, :]
     angle = 2.0 * math.pi * (k * p % points) / points
     cos, sin = np.cos(angle), np.sin(angle)
@@ -39,7 +39,9 @@
         high = table.astype(jnp.bfloat16)
         low = (table - high.astype(np.float32)).astype(jnp.bfloat16)
         parts.append(np.concatenate([high, low], axis=0))
-    return jnp.asarray(parts[0]), jnp.asarray(parts[1]), jnp.asarray(turn)
+    halves = parts[0].reshape(4, segments // 2, 2, points // segments, 2 * points).transpose(2, 0, 1, 3, 4)
+    halves = halves.reshape(2, 2 * points, 2 * points)
+    return jnp.asarray(parts[0]), jnp.asarray(parts[1]), jnp.asarray(turn), jnp.asarray(halves)
 
 
 def split(value):
@@ -121,7 +123,7 @@
     blocks = warp_blocks.shape[1]
     points = blocks // 2
     ordered = warp_blocks.reshape(HYPS, points, 2).transpose(0, 2, 1).reshape(HYPS * blocks, 1)
-    operands = (replica.reshape(-1, PAIR), taps.transpose(0, 2, 1), tap_weights.transpose(0, 2, 1), ordered, *tables)
+    operands = (replica.reshape(-1, PAIR), taps.transpose(0, 2, 1), tap_weights.transpose(0, 2, 1), ordered, *tables[:3])
     shapes = ((PAIR, HYPS * BLOCK), BF16), ((HYPS * blocks, blocks), BF16), ((points, 2 * PAIR), F32)
 
     def whole(shape):
@@ -169,58 +171,15 @@
     return [(hyp, beam, beam + 1) for hyp in range(HYPS) for beam in range(0, beams, 2)]
 
 
-def correlate_kernel(
-    beams,
-    segments,
-    paired,
-    place_ref,
-    source_ref,
-    interp_hbm,
-    chosen_hbm,
-    left_hbm,
-    turn_hbm,
-    right_hbm,
-    spectrum_hbm,
-    *refs,
+def transform(
+    beams, source_ref, interp_ref, chosen_ref, left_ref, turn_ref, right_ref, spectrum_ref, column_ref, next_ref, block_ref, row_ref, wide_ref
 ):
-    out_refs, refs = refs[: 1 + paired], refs[1 + paired :]
-    (
-    interp_ref,
-    chosen_ref,
-    left_ref,
-    turn_ref,
-    right_ref,
-    spectrum_ref,
-    sems,
-    next_ref,
-    block_ref,
-    column_ref,
-    row_ref,
-    wide_ref,
-    ) = refs
-    fetches = [
-        pltpu.make_async_copy(source, target, sems.at[index])
-        for index, (source, target) in enumerate(
-            (
-                (interp_hbm, interp_ref),
-                (chosen_hbm, chosen_ref),
-                (left_hbm, left_ref),
-                (turn_hbm, turn_ref),
-                (right_hbm, right_ref),
-                (spectrum_hbm, spectrum_ref),
-            )
-        )
-    ]
-    for fetch in fetches:
-        fetch.start()
-    get_interp, get_chosen, get_left, get_turn, get_right, get_spectrum = fetches
     points = turn_ref.shape[0]
     blocks = 2 * points
     lines = source_ref.shape[0]
     rows = complex_rows(beams)
     chunk = min(512, lines)
 
-    get_interp.wait()
     for start in range(0, lines, chunk):
         next_ref[start : start + chunk, :] = dot(source_ref[start : start + chunk, :], interp_ref[BLOCK:, :])
     next_ref[lines : lines + 8, :] = next_ref[0:8, :]
@@ -232,7 +191,6 @@
         for hyp in range(HYPS):
             block_ref[hyp, start : start + chunk, :] = value[:, hyp * BLOCK : (hyp + 1) * BLOCK]
 
-    get_chosen.wait()
     for hyp in range(HYPS):
         warped = jnp.concatenate(
             [block_ref[hyp, pl.ds(beam, blocks, stride=beams), :].astype(BF16) for beam in range(beams)], axis=1
@@ -252,32 +210,28 @@
                             half * points : (half + 1) * points, beam * BLOCK : (beam + 1) * BLOCK
                         ]
 
-    def left_product(index):
-        both = dot(left_ref[...], column_ref[:, index * PAIR : (index + 1) * PAIR])
-        value = both[: 2 * points] + both[2 * points :]
-        return value[:points], value[points:]
-
     def right_product():
         value = row_ref[...]
         wide_ref[...] = dot(value, right_ref[: 2 * PAIR, :]) + dot(value, right_ref[2 * PAIR :, :])
 
-    get_left.wait()
-    get_turn.wait()
     turn_re, turn_im = turn_ref[:, :PAIR], turn_ref[:, PAIR:]
     for index in range(len(rows)):
-        real, imag = left_product(index)
+        real, imag = left_product(left_ref[...], column_ref, index)
         place = slice(index * points, (index + 1) * points)
         row_ref[place, :PAIR] = (real * turn_re - imag * turn_im).astype(BF16)
         row_ref[place, PAIR:] = (real * turn_im + imag * turn_re).astype(BF16)
-    get_right.wait()
     right_product()
-    get_spectrum.wait()
     spectrum_re, spectrum_im = spectrum_ref[:, :PAIR], spectrum_ref[:, PAIR:]
-    for index in range(len(rows)):
+    sums = [jnp.zeros((8, PAIR), F32) for _ in range(HYPS)]
+    for index, (hyp, _, _) in enumerate(rows):
         place = slice(index * points, (index + 1) * points)
         real, imag = wide_ref[place, :PAIR], wide_ref[place, PAIR:]
-        row_ref[place, PAIR:] = (real * spectrum_re - imag * spectrum_im).astype(BF16)
-        row_ref[place, :PAIR] = (real * spectrum_im + imag * spectrum_re).astype(BF16)
+        new_re = real * spectrum_re - imag * spectrum_im
+        new_im = real * spectrum_im + imag * spectrum_re
+        square = new_re * new_re + new_im * new_im
+        sums[hyp] = sums[hyp] + jnp.sum(square.reshape(points // 8, 8, PAIR), axis=0)
+        row_ref[place, PAIR:] = new_re.astype(BF16)
+        row_ref[place, :PAIR] = new_im.astype(BF16)
     right_product()
     for index in range(len(rows)):
         place = slice(index * points, (index + 1) * points)
@@ -285,68 +239,117 @@
         imag, real = wide_ref[place, :PAIR], wide_ref[place, PAIR:]
         column_ref[points:, lanes] = (real * turn_re + imag * turn_im).astype(BF16)
         column_ref[:points, lanes] = (imag * turn_re - real * turn_im).astype(BF16)
-
-    share = points // segments
-    sums = [jnp.zeros((8, PAIR), F32) for _ in range(HYPS)]
-    for index, (hyp, real_beam, imag_beam) in enumerate(rows):
-        imag, real = left_product(index)
+    return [
+        jnp.sum(jnp.sum(value, axis=1, keepdims=True), axis=0, keepdims=True) * (points * PAIR) for value in sums
+    ]
+
+
+def left_product(matrix, column_ref, index):
+    both = dot(matrix, column_ref[:, index * PAIR : (index + 1) * PAIR])
+    value = both[: both.shape[0] // 2] + both[both.shape[0] // 2 :]
+    return value[: value.shape[0] // 2], value[value.shape[0] // 2 :]
+
+
+def powers(matrix, column_ref, beams):
+    for index, (hyp, real_beam, imag_beam) in enumerate(complex_rows(beams)):
+        imag, real = left_product(matrix, column_ref, index)
         for beam, value in ((real_beam, real), (imag_beam, imag)):
-            if beam is None:
-                continue
-            power = value * value
-            sums[hyp] = sums[hyp] + jnp.sum(power.reshape(points // 8, 8, PAIR), axis=0)
-            first = (hyp * beams + beam) * 2 * share
-            pieces = [power[segment * share : (segment + 1) * share, :] for segment in range(segments)]
-            pieces = [jnp.concatenate([piece[:, :BLOCK], piece[:, BLOCK:]], axis=0) for piece in pieces]
-            if paired:
-                is_even = place_ref[0] % 2 == 0
-                for chip in range(segments // 2):
-                    start = chip * HYPS * beams * 2 * share + first
-                    even, odd = pieces[2 * chip], pieces[2 * chip + 1]
-                    out_refs[0][start : start + 2 * share, :] = jnp.where(is_even, even, odd).astype(BF16)
-                    out_refs[1][start : start + 2 * share, :] = jnp.where(is_even, odd, even).astype(BF16)
-            else:
-                for segment, piece in enumerate(pieces):
-                    out_refs[0][segment, first : first + 2 * share, :] = piece.astype(BF16)
-    tail = tail_of([jnp.sum(jnp.sum(value, axis=1, keepdims=True), axis=0, keepdims=True) for value in sums])
-    if paired:
-        for out_ref in out_refs:
-            out_ref[out_ref.shape[0] - 16 :, :] = tail
-    else:
+            if beam is not None:
+                yield hyp * beams + beam, value * value
+
+
+def store_powers(matrix, column_ref, beams, segments, target):
+    for number, power in powers(matrix, column_ref, beams):
+        share = power.shape[0] // segments
         for segment in range(segments):
-            out_refs[0][segment, HYPS * beams * 2 * share :, :] = tail
-
-
-def correlate(place, source, interp, chosen, spectrum, tables, beams, segments, paired):
-    left, right, turn = tables
+            piece = power[segment * share : (segment + 1) * share, :]
+            piece = jnp.concatenate([piece[:, :BLOCK], piece[:, BLOCK:]], axis=0)
+            target(segment)[number * 2 * share : (number + 1) * 2 * share, :] = piece.astype(BF16)
+
+
+def correlate_kernel(beams, segments, source_ref, *refs):
+    tables, out_ref, scratch = refs[:6], refs[6], refs[7:]
+    totals = transform(beams, source_ref, *tables, *scratch)
+    store_powers(tables[2][...], scratch[0], beams, segments, lambda segment: out_ref.at[segment])
+    tail = tail_of(totals)
+    for segment in range(segments):
+        out_ref[segment, out_ref.shape[1] - 16 :, :] = tail
+
+
+def first_half_kernel(beams, segments, place_ref, source_ref, *refs):
+    tables, halves_ref, column_ref, theirs_ref, scratch = refs[:6], refs[6], refs[7], refs[8], refs[9:]
+    totals = transform(beams, source_ref, *tables, column_ref, *scratch)
+    chips = segments // 2
+    lines = (theirs_ref.shape[0] - 16) // chips
+    parity = (place_ref[0] + 1) % 2
+    store_powers(
+        halves_ref[parity], column_ref, beams, chips, lambda chip: theirs_ref.at[chip * lines : (chip + 1) * lines]
+    )
+    theirs_ref[chips * lines :, :] = tail_of(totals)
+
+
+def second_half_kernel(beams, segments, place_ref, column_ref, halves_ref, mine_ref):
+    chips = segments // 2
+    lines = mine_ref.shape[0] // chips
+    parity = place_ref[0] % 2
+    store_powers(
+        halves_ref[parity], column_ref, beams, chips, lambda chip: mine_ref.at[chip * lines : (chip + 1) * lines]
+    )
+
+
+def correlate_shapes(lines, points, beams):
+    count = len(complex_rows(beams))
+    column = ((2 * points, count * PAIR), BF16)
+    scratch = [
+        ((lines + 8, PAIR), F32),
+        ((HYPS, lines, BLOCK), F32),
+        ((count * points, 2 * PAIR), BF16),
+        ((count * points, 2 * PAIR), F32),
+    ]
+    return column, scratch
+
+
+def correlate(source, interp, chosen, spectrum, tables, beams, segments):
+    left, right, turn, _ = tables
     points = turn.shape[0]
-    lines = source.shape[0]
-    count = len(complex_rows(beams))
-    fetched = (interp, chosen, left, turn, right, spectrum)
-    out_rows = HYPS * beams * 2 * (points // segments) + 16
-    if paired:
-        shape = jax.ShapeDtypeStruct((segments // 2 * (out_rows - 16) + 16, BLOCK), BF16)
-        out_shape, out_specs = (shape, shape), (VMEM, VMEM)
-    else:
-        out_shape, out_specs = jax.ShapeDtypeStruct((segments, out_rows, BLOCK), BF16), VMEM
-    return pl.pallas_call(
-        functools.partial(correlate_kernel, beams, segments, paired),
-        out_shape=out_shape,
-        in_specs=[SMEM, VMEM] + [ANY] * len(fetched),
-        out_specs=out_specs,
-        scratch_shapes=[pltpu.VMEM(array.shape, array.dtype) for array in fetched]
-        + [
-            pltpu.SemaphoreType.DMA((len(fetched),)),
-            pltpu.VMEM((lines + 8, PAIR), F32),
-            pltpu.VMEM((HYPS, lines, BLOCK), F32),
-            pltpu.VMEM((2 * points, count * PAIR), BF16),
-            pltpu.VMEM((count * points, 2 * PAIR), BF16),
-            pltpu.VMEM((count * points, 2 * PAIR), F32),
-        ],
+    column, scratch = correlate_shapes(source.shape[0], points, beams)
+    return pl.pallas_call(
+        functools.partial(correlate_kernel, beams, segments),
+        out_shape=jax.ShapeDtypeStruct((segments, HYPS * beams * 2 * (points // segments) + 16, BLOCK), BF16),
+        in_specs=[VMEM] * 7,
+        out_specs=VMEM,
+        scratch_shapes=[pltpu.VMEM(*shape) for shape in (column, *scratch)],
+        compiler_params=pltpu.CompilerParams(vmem_limit_bytes=48 * 1024 * 1024),
+        cost_estimate=pl.CostEstimate(flops=4_000_000_000, bytes_accessed=6_000_000, transcendentals=0),
+        name="warp_correlate",
+    )(source, interp, chosen, left, turn, right, spectrum)
+
+
+def correlate_in_halves(place, source, interp, chosen, spectrum, tables, beams, segments):
+    left, right, turn, halves = tables
+    points = turn.shape[0]
+    column, scratch = correlate_shapes(source.shape[0], points, beams)
+    rows = segments // 2 * HYPS * beams * 2 * (points // segments)
+    columns, theirs = pl.pallas_call(
+        functools.partial(first_half_kernel, beams, segments),
+        out_shape=(jax.ShapeDtypeStruct(*column), jax.ShapeDtypeStruct((rows + 16, BLOCK), BF16)),
+        in_specs=[SMEM] + [VMEM] * 8,
+        out_specs=(VMEM, VMEM),
+        scratch_shapes=[pltpu.VMEM(*shape) for shape in scratch],
         compiler_params=pltpu.CompilerParams(vmem_limit_bytes=24 * 1024 * 1024),
         cost_estimate=pl.CostEstimate(flops=4_000_000_000, bytes_accessed=6_000_000, transcendentals=0),
         name="warp_correlate",
-    )(place, source, *fetched)
+    )(place, source, interp, chosen, left, turn, right, spectrum, halves)
+    mine = pl.pallas_call(
+        functools.partial(second_half_kernel, beams, segments),
+        out_shape=jax.ShapeDtypeStruct((rows, BLOCK), BF16),
+        in_specs=[SMEM, VMEM, VMEM],
+        out_specs=VMEM,
+        compiler_params=pltpu.CompilerParams(vmem_limit_bytes=16 * 1024 * 1024),
+        cost_estimate=pl.CostEstimate(flops=1_000_000_000, bytes_accessed=2_000_000, transcendentals=0),
+        name="second_half",
+    )(place, columns, halves)
+    return theirs, mine
 
 
 def finish_kernel(count, power_ref, sums_ref, out_ref, scratch_ref):
@@ -391,11 +394,11 @@
     return [offset for pair in zip(far, near) for offset in pair][:-1] + [0]
 
 
-def arrange_kernel(place_ref, mine_ref, got_ref, *out_refs):
+def arrange_kernel(place_ref, mine_ref, sums_ref, got_ref, *out_refs):
     chip = place_ref[0] // 2
     count = len(out_refs)
-    lines = (mine_ref.shape[0] - 16) // count
-    tails = [ref[count * lines :, :] for ref in (mine_ref, got_ref)]
+    lines = mine_ref.shape[0] // count
+    tails = [ref[count * lines :, :] for ref in (sums_ref, got_ref)]
     tail = tail_of([total[:, :1] for total in totals_of(tails)])
     for offset, out_ref in zip(chip_order(count), out_refs):
         rows = pl.ds(pl.multiple_of((chip ^ offset) * lines, lines), lines)
@@ -404,18 +407,18 @@
         out_ref[2 * lines :, :] = tail
 
 
-def arrange(place, mine, got, chips):
-    lines = (mine.shape[0] - 16) // chips
+def arrange(place, mine, theirs, got, chips):
+    lines = mine.shape[0] // chips
     shape = jax.ShapeDtypeStruct((2 * lines + 16, BLOCK), BF16)
     return pl.pallas_call(
         arrange_kernel,
         out_shape=[shape] * chips,
-        in_specs=[SMEM, VMEM, VMEM],
+        in_specs=[SMEM] + [VMEM] * 3,
         out_specs=[VMEM] * chips,
         compiler_params=pltpu.CompilerParams(vmem_limit_bytes=16 * 1024 * 1024),
         cost_estimate=pl.CostEstimate(flops=1_000_000, bytes_accessed=1_200_000, transcendentals=0),
         name="arrange_chips",
-    )(place, mine, got)
+    )(place, mine, theirs, got)
 
 
 def join_kernel(count, place_ref, *refs):
@@ -464,20 +467,18 @@
     beams = signal.shape[0] // segments
     samples = signal.shape[1] * segments
     count = float(BEAMS * samples)
-    paired = segments == 16
-    place = lax.axis_index("tm").astype(jnp.int32).reshape(1)
     received = lax.all_to_all(spread(signal, segments), "tm", split_axis=0, concat_axis=0, tiled=True)
-    tables = transform_tables(samples // PAIR)
+    source = received.reshape(-1, BLOCK)
+    tables = transform_tables(samples // PAIR, segments)
     interp, chosen, spectrum = prepare(replica, taps, tap_weights, warp_blocks, tables)
-    sent = correlate(
-        place, received.reshape(-1, BLOCK), interp, chosen, spectrum, tables, beams, segments, paired
-    )
-    if not paired:
+    if segments != 16:
+        sent = correlate(source, interp, chosen, spectrum, tables, beams, segments)
         back = lax.all_to_all(sent, "tm", split_axis=0, concat_axis=0, tiled=True)
         return finish(back, count, beams)
-    mine, theirs = sent
+    place = lax.axis_index("tm").astype(jnp.int32).reshape(1)
+    theirs, mine = correlate_in_halves(place, source, interp, chosen, spectrum, tables, beams, segments)
     chips = segments // 2
-    chunks = arrange(place, mine, exchange(theirs, 1, segments), chips)
+    chunks = arrange(place, mine, theirs, exchange(theirs, 1, segments), chips)
     arrived = [
         exchange(chunk, 2 * offset, segments) if offset else chunk for offset, chunk in zip(chip_order(chips), chunks)
     ]

time: 41 us -> 40.1 us (0.978)
  Pallas kernels: 7.58 us -> 7.01 us
    pallas_call x2 -> x3, Pallas kernels: 3.53 us -> 2.96 us  [the longest x1 2.56 us: correlate_in_halves(): pl.pallas_call(functools.partial(first_half_kernel, beams, segments), out...]
  transfers between devices with their start and end apart: 9 -> 9, of which waited for: 7 -> 7; matrix products, arithmetic and copies ran while one was open for 3% -> 3% of each run, Pallas kernels for 2% -> 3%
where the time goes in v3:
time: 40.1 us; the launch traced here: 39.8 us
  starting transfers between devices  16.7 us (42%)
  waiting for transfers between devices  14.1 us (35%)
  Pallas kernels  7.01 us (17%)
  local copies, waits for them, and re-layouts  1.87 us (5%)
    ppermute x8, starting transfers between devices, exchange(): lax.ppermute(value, 'tm', [(index, index ^ offset) for index in range(seg...  9.29 us
    all_to_all x1, starting transfers between devices, body(): lax.all_to_all(spread(signal, segments), 'tm', split_axis=0, concat_axis=...  7.39 us
    all_to_all x1, waiting for transfers between devices, body(): lax.all_to_all(spread(signal, segments), 'tm', split_axis=0, concat_axis=...  7.08 us
    ppermute x8, waiting for transfers between devices, exchange(): lax.ppermute(value, 'tm', [(index, index ^ offset) for index in range(seg...  7.07 us
    pallas_call x1, Pallas kernels, correlate_in_halves(): pl.pallas_call(functools.partial(first_half_kernel, beams, segments), out...  2.56 us
    pallas_call x1, Pallas kernels, spread(): pl.pallas_call(spread_kernel, out_shape=jax.ShapeDtypeStruct((segments, b...  1.8 us
    pallas_call x1, Pallas kernels, join(): pl.pallas_call(functools.partial(join_kernel, count), out_shape=jax.Shape...  1.23 us
    pallas_call x1, Pallas kernels, prepare(): pl.pallas_call(prepare_kernel, grid=(1,), out_shape=[jax.ShapeDtypeStruct...  1.01 us
  transfers between devices with their start and end apart: 9, of which 7 were waited for; matrix products, arithmetic and copies ran while one was open for 3% of the time, Pallas kernels for 3%

profile of v3, /device:TPU:0, one launch (start us, length us, event | category | flops | bytes accessed | tf_op | source)
XLA Modules:
  0.0 39.8 jit_solution(9095523920556514733)
XLA Ops:
  0.0 0.0 copy-start
  0.0 1.8 %spread_beams.1 = bf16[16,64,128]{2,1,0:T(8,128)(2,1)} custom-call(bf16[64,2048]{1,0:T(8,128)(2,1)} %signal_ref.1), custom_call_target="tpu_custom_call" | custom-call | tf_op jit(solution)/shard_map/spread_beams/pallas_call | solution.py:81
  1.8 7.4 %all-to-all-start = ((bf16[16,64,128]{2,1,0:T(8,128)(2,1)}), bf16[16,64,128]{2,1,0:T(8,128)(2,1)S(1)}, u32[]{:S(2)}, u32[]{:S(2)}) async-start(bf16[16,64,128]{2,1,0:T(8,128)(2,1)} %spread_beams.1), calls=%async_computation | async-start | bytes 524288 | tf_op jit(solution)/shard_map/all_to_all | solution.py:470
  9.2 0.0 copy-start.6
  9.2 0.0 copy-start.4
  9.2 0.9 %reshape.17.replica_ref = f32[64,256]{1,0:T(8,128)S(1)} reshape(f32[16384]{0:T(1024)} %param.13) | data formatting | bytes 131072 | tf_op jit(solution)/shard_map/reshape | solution.py:126
  10.1 0.0 copy-done.6
  10.1 0.0 copy-start.1
  10.1 0.0 copy-start.2
  10.1 0.1 reshape.18
  10.3 0.1 copy.11
  10.4 0.0 copy-start.3
  10.4 0.2 copy.12.sources_ref
  10.5 0.0 copy-done
  10.5 0.0 copy-done.4
  10.5 0.5 %copy-done.1 = f32[128,512]{1,0:T(8,128)S(1)} copy-done((f32[128,512]{1,0:T(8,128)S(1)}, f32[128,512]{1,0:T(8,128)}, u32[]{:S(2)}) %copy-start.1) | copy-done | bytes 262168
  11.1 0.1 copy-done.2
  11.1 0.0 copy-done.3
  11.1 0.0 copy-start.5
  11.1 1.0 %prepare_tables.1 = (bf16[256,256]{1,0:T(8,128)(2,1)S(1)}, bf16[512,256]{1,0:T(8,128)(2,1)S(1)}, f32[128,512]{1,0:T(8,128)S(1)}) custom-call(f32[64,256]{1,0:T(8,128)S(1)} %reshape.17.replica_ref, s32[2,8,128]{2,1,0:T(8,128)S(1)} %bitcast.7, f32[2,8,128]{2,1,0:T(8,128)S(1)} %bitcast.8, s32[512,1]{1,0:T(8,128)S(1)} %copy.12.sources_ref, ...), custom_call_target="tpu_custom_call" | custom-call | flops 500000000 | bytes 16000000 | tf_op jit(solution)/shard_map/prepare_tables/pallas_call | solution.py:132
  12.2 7.1 %all-to-all-done = bf16[16,64,128]{2,1,0:T(8,128)(2,1)S(1)} async-done(((bf16[16,64,128]{2,1,0:T(8,128)(2,1)}), bf16[16,64,128]{2,1,0:T(8,128)(2,1)S(1)}, u32[]{:S(2)}, u32[]{:S(2)}) %all-to-all-start) | async-done | bytes 262176 | tf_op jit(solution)/shard_map/all_to_all | solution.py:470
  19.2 0.0 copy-done.5
  19.2 2.6 %warp_correlate.1 = (bf16[256,1024]{1,0:T(8,128)(2,1)S(1)}, bf16[1040,128]{1,0:T(8,128)(2,1)S(1)}) custom-call(s32[1]{0:T(128)} %bitcast.place_ref, bf16[1024,128]{1,0:T(8,128)(2,1)S(1)} %bitcast.6, bf16[256,256]{1,0:T(8,128)(2,1)S(1)} %get-tuple-element.18.refs_0_, bf16[512,256]{1,0:T(8,128)(2,1)S(1)} %get-tuple-element.19.refs_1_, ...), custom_call_target="tpu_custom_call" | custom-call | flops 4000000000 | bytes 6000000 | tf_op jit(solution)/shard_map/warp_correlate/pallas_call | solution.py:333
  21.8 0.1 collective-permute-start
  21.9 0.3 second_half.1.mine_ref
  22.2 1.2 %collective-permute-done.got_ref = bf16[1040,128]{1,0:T(8,128)(2,1)S(1)} collective-permute-done((bf16[1040,128]{1,0:T(8,128)(2,1)S(1)}, bf16[1040,128]{1,0:T(8,128)(2,1)S(1)}, u32[]{:S(2)}, u32[]{:S(2)}) %collective-permute-start) | collective-permute-done | bytes 266272 | tf_op jit(solution)/shard_map/ppermute | solution.py:462
  23.4 0.1 arrange_chips.1
  23.5 1.1 %collective-permute-start.1 = (bf16[272,128]{1,0:T(8,128)(2,1)S(1)}, bf16[272,128]{1,0:T(8,128)(2,1)S(1)}, u32[]{:S(2)}, u32[]{:S(2)}) collective-permute-start(bf16[272,128]{1,0:T(8,128)(2,1)S(1)} %get-tuple-element.23), channel_id=1, source_target_pairs={{0,8},{1,9},{2,10},{3,11},{4,12},{5,13},{6,14},{7,15},{8,0},{9,1},... | collective-permute-start | bytes 208904 | tf_op jit(solution)/shard_map/ppermute | solution.py:462
  24.6 0.0 collective-permute-start.2
  24.7 3.3 %collective-permute-start.3 = (bf16[272,128]{1,0:T(8,128)(2,1)S(1)}, bf16[272,128]{1,0:T(8,128)(2,1)S(1)}, u32[]{:S(2)}, u32[]{:S(2)}) collective-permute-start(bf16[272,128]{1,0:T(8,128)(2,1)S(1)} %get-tuple-element.25), channel_id=1, source_target_pairs={{0,10},{1,11},{2,8},{3,9},{4,14},{5,15},{6,12},{7,13},{8,2},{9,3},... | collective-permute-start | bytes 208904 | tf_op jit(solution)/shard_map/ppermute | solution.py:462
  28.0 0.3 collective-permute-start.4
  28.3 2.2 %collective-permute-start.5 = (bf16[272,128]{1,0:T(8,128)(2,1)S(1)}, bf16[272,128]{1,0:T(8,128)(2,1)S(1)}, u32[]{:S(2)}, u32[]{:S(2)}) collective-permute-start(bf16[272,128]{1,0:T(8,128)(2,1)S(1)} %get-tuple-element.27), channel_id=1, source_target_pairs={{0,12},{1,13},{2,14},{3,15},{4,8},{5,9},{6,10},{7,11},{8,4},{9,5},... | collective-permute-start | bytes 208904 | tf_op jit(solution)/shard_map/ppermute | solution.py:462
  30.5 1.1 %collective-permute-done.1.refs_0_ = bf16[272,128]{1,0:T(8,128)(2,1)S(1)} collective-permute-done((bf16[272,128]{1,0:T(8,128)(2,1)S(1)}, bf16[272,128]{1,0:T(8,128)(2,1)S(1)}, u32[]{:S(2)}, u32[]{:S(2)}) %collective-permute-start.1) | collective-permute-done | bytes 69664 | tf_op jit(solution)/shard_map/ppermute | solution.py:462
  31.6 0.0 collective-permute-start.6
  31.6 0.0 collective-permute-done.2.refs_1_
  31.6 2.2 %collective-permute-start.7 = (bf16[272,128]{1,0:T(8,128)(2,1)S(1)}, bf16[272,128]{1,0:T(8,128)(2,1)S(1)}, u32[]{:S(2)}, u32[]{:S(2)}) collective-permute-start(bf16[272,128]{1,0:T(8,128)(2,1)S(1)} %get-tuple-element.29), channel_id=1, source_target_pairs={{0,14},{1,15},{2,12},{3,13},{4,10},{5,11},{6,8},{7,9},{8,6},{9,7},... | collective-permute-start | bytes 208904 | tf_op jit(solution)/shard_map/ppermute | solution.py:462
  33.8 0.5 %collective-permute-done.3.refs_2_ = bf16[272,128]{1,0:T(8,128)(2,1)S(1)} collective-permute-done((bf16[272,128]{1,0:T(8,128)(2,1)S(1)}, bf16[272,128]{1,0:T(8,128)(2,1)S(1)}, u32[]{:S(2)}, u32[]{:S(2)}) %collective-permute-start.3) | collective-permute-done | bytes 69664 | tf_op jit(solution)/shard_map/ppermute | solution.py:462
  34.3 2.1 %collective-permute-done.4.refs_3_ = bf16[272,128]{1,0:T(8,128)(2,1)S(1)} collective-permute-done((bf16[272,128]{1,0:T(8,128)(2,1)S(1)}, bf16[272,128]{1,0:T(8,128)(2,1)S(1)}, u32[]{:S(2)}, u32[]{:S(2)}) %collective-permute-start.4) | collective-permute-done | bytes 69664 | tf_op jit(solution)/shard_map/ppermute | solution.py:462
  36.4 0.0 collective-permute-done.5.refs_4_
  36.4 1.1 %collective-permute-done.6.refs_5_ = bf16[272,128]{1,0:T(8,128)(2,1)S(1)} collective-permute-done((bf16[272,128]{1,0:T(8,128)(2,1)S(1)}, bf16[272,128]{1,0:T(8,128)(2,1)S(1)}, u32[]{:S(2)}, u32[]{:S(2)}) %collective-permute-start.6) | collective-permute-done | bytes 69664 | tf_op jit(solution)/shard_map/ppermute | solution.py:462
  37.5 1.1 %collective-permute-done.7.refs_6_ = bf16[272,128]{1,0:T(8,128)(2,1)S(1)} collective-permute-done((bf16[272,128]{1,0:T(8,128)(2,1)S(1)}, bf16[272,128]{1,0:T(8,128)(2,1)S(1)}, u32[]{:S(2)}, u32[]{:S(2)}) %collective-permute-start.7) | collective-permute-done | bytes 69664 | tf_op jit(solution)/shard_map/ppermute | solution.py:462
  38.6 1.2 %scale_power.1 = bf16[2,64,2048]{2,1,0:T(8,128)(2,1)} custom-call(s32[1]{0:T(128)} %bitcast.place_ref, bf16[272,128]{1,0:T(8,128)(2,1)S(1)} %collective-permute-done.1.refs_0_, bf16[272,128]{1,0:T(8,128)(2,1)S(1)} %collective-permute-done.2.refs_1_, bf16[272,128]{1,0:T(8,128)(2,1)S(1)} %collective-permute-done.3.refs_2_, ...), custom_call_target="tpu_custom_call" | custom-call | flops 1000000 | bytes 1200000 | tf_op jit(solution)/shard_map/scale_power/pallas_call | solution.py:449
Async XLA Ops:
  0.0 10.5 %copy-start = (bf16[1024,512]{1,0:T(8,128)(2,1)S(1)}, bf16[1024,512]{1,0:T(8,128)(2,1)}, u32[]{:S(2)}) copy-start(bf16[1024,512]{1,0:T(8,128)(2,1)} %constant.13.clone.right_ref.refs_4_) | copy-start | bytes 3145732
  1.8 17.4 %all-to-all-start = ((bf16[16,64,128]{2,1,0:T(8,128)(2,1)}), bf16[16,64,128]{2,1,0:T(8,128)(2,1)S(1)}, u32[]{:S(2)}, u32[]{:S(2)}) async-start(bf16[16,64,128]{2,1,0:T(8,128)(2,1)} %spread_beams.1), calls=%async_computation | async-start | bytes 524288 | tf_op jit(solution)/shard_map/all_to_all | solution.py:470
  9.2 0.9 %copy-start.6 = (s32[2,256]{1,0:T(2,128)S(1)}, s32[2,256]{1,0:T(2,128)}, u32[]{:S(2)}) copy-start(s32[2,256]{1,0:T(2,128)} %param.10) | copy-start | bytes 6148
  9.2 1.3 %copy-start.4 = (f32[2,128,8]{1,2,0:T(8,128)S(1)}, f32[2,128,8]{1,2,0:T(8,128)}, u32[]{:S(2)}) copy-start(f32[2,128,8]{1,2,0:T(8,128)} %param.12) | copy-start | bytes 24580
  10.1 1.0 %copy-start.1 = (f32[128,512]{1,0:T(8,128)S(1)}, f32[128,512]{1,0:T(8,128)}, u32[]{:S(2)}) copy-start(f32[128,512]{1,0:T(8,128)} %constant.14.clone.turn_ref.refs_3_) | copy-start | bytes 786436
  10.1 1.0 %copy-start.2 = (bf16[512,256]{1,0:T(8,128)(2,1)S(1)}, bf16[512,256]{1,0:T(8,128)(2,1)}, u32[]{:S(2)}) copy-start(bf16[512,256]{1,0:T(8,128)(2,1)} %constant.12.clone.left_ref.refs_2_) | copy-start | bytes 786436
  10.4 0.8 %copy-start.3 = (s32[2,128,8]{1,2,0:T(8,128)S(1)}, s32[2,128,8]{1,2,0:T(8,128)}, u32[]{:S(2)}) copy-start(s32[2,128,8]{1,2,0:T(8,128)} %param.11) | copy-start | bytes 24580
  11.1 8.1 %copy-start.5 = (bf16[2,256,256]{2,1,0:T(8,128)(2,1)S(1)}, bf16[2,256,256]{2,1,0:T(8,128)(2,1)}, u32[]{:S(2)}) copy-start(bf16[2,256,256]{2,1,0:T(8,128)(2,1)} %constant.15.clone.refs_6_.halves_ref) | copy-start | bytes 786436
  21.8 1.6 %collective-permute-start = (bf16[1040,128]{1,0:T(8,128)(2,1)S(1)}, bf16[1040,128]{1,0:T(8,128)(2,1)S(1)}, u32[]{:S(2)}, u32[]{:S(2)}) collective-permute-start(bf16[1040,128]{1,0:T(8,128)(2,1)S(1)} %get-tuple-element.22.sums_ref), channel_id=1, source_target_pairs={{0,1},{1,0},{2,3},{3,2},{4,5},{5,4},{6,7},{7,6},{8,9},{9,8},{10,11... | collective-permute-start | bytes 798728 | tf_op jit(solution)/shard_map/ppermute | solution.py:462
  23.5 8.1 %collective-permute-start.1 = (bf16[272,128]{1,0:T(8,128)(2,1)S(1)}, bf16[272,128]{1,0:T(8,128)(2,1)S(1)}, u32[]{:S(2)}, u32[]{:S(2)}) collective-permute-start(bf16[272,128]{1,0:T(8,128)(2,1)S(1)} %get-tuple-element.23), channel_id=1, source_target_pairs={{0,8},{1,9},{2,10},{3,11},{4,12},{5,13},{6,14},{7,15},{8,0},{9,1},... | collective-permute-start | bytes 208904 | tf_op jit(solution)/shard_map/ppermute | solution.py:462
  24.6 6.9 %collective-permute-start.2 = (bf16[272,128]{1,0:T(8,128)(2,1)S(1)}, bf16[272,128]{1,0:T(8,128)(2,1)S(1)}, u32[]{:S(2)}, u32[]{:S(2)}) collective-permute-start(bf16[272,128]{1,0:T(8,128)(2,1)S(1)} %get-tuple-element.24), channel_id=1, source_target_pairs={{0,2},{1,3},{2,0},{3,1},{4,6},{5,7},{6,4},{7,5},{8,10},{9,11},{10,... | collective-permute-start | bytes 208904 | tf_op jit(solution)/shard_map/ppermute | solution.py:462
  24.7 9.7 %collective-permute-start.3 = (bf16[272,128]{1,0:T(8,128)(2,1)S(1)}, bf16[272,128]{1,0:T(8,128)(2,1)S(1)}, u32[]{:S(2)}, u32[]{:S(2)}) collective-permute-start(bf16[272,128]{1,0:T(8,128)(2,1)S(1)} %get-tuple-element.25), channel_id=1, source_target_pairs={{0,10},{1,11},{2,8},{3,9},{4,14},{5,15},{6,12},{7,13},{8,2},{9,3},... | collective-permute-start | bytes 208904 | tf_op jit(solution)/shard_map/ppermute | solution.py:462
  28.0 8.4 %collective-permute-start.4 = (bf16[272,128]{1,0:T(8,128)(2,1)S(1)}, bf16[272,128]{1,0:T(8,128)(2,1)S(1)}, u32[]{:S(2)}, u32[]{:S(2)}) collective-permute-start(bf16[272,128]{1,0:T(8,128)(2,1)S(1)} %get-tuple-element.26), channel_id=1, source_target_pairs={{0,4},{1,5},{2,6},{3,7},{4,0},{5,1},{6,2},{7,3},{8,12},{9,13},{10,... | collective-permute-start | bytes 208904 | tf_op jit(solution)/shard_map/ppermute | solution.py:462
  28.3 8.1 %collective-permute-start.5 = (bf16[272,128]{1,0:T(8,128)(2,1)S(1)}, bf16[272,128]{1,0:T(8,128)(2,1)S(1)}, u32[]{:S(2)}, u32[]{:S(2)}) collective-permute-start(bf16[272,128]{1,0:T(8,128)(2,1)S(1)} %get-tuple-element.27), channel_id=1, source_target_pairs={{0,12},{1,13},{2,14},{3,15},{4,8},{5,9},{6,10},{7,11},{8,4},{9,5},... | collective-permute-start | bytes 208904 | tf_op jit(solution)/shard_map/ppermute | solution.py:462
  31.6 6.0 %collective-permute-start.6 = (bf16[272,128]{1,0:T(8,128)(2,1)S(1)}, bf16[272,128]{1,0:T(8,128)(2,1)S(1)}, u32[]{:S(2)}, u32[]{:S(2)}) collective-permute-start(bf16[272,128]{1,0:T(8,128)(2,1)S(1)} %get-tuple-element.28), channel_id=1, source_target_pairs={{0,6},{1,7},{2,4},{3,5},{4,2},{5,3},{6,0},{7,1},{8,14},{9,15},{10,... | collective-permute-start | bytes 208904 | tf_op jit(solution)/shard_map/ppermute | solution.py:462
  31.6 7.0 %collective-permute-start.7 = (bf16[272,128]{1,0:T(8,128)(2,1)S(1)}, bf16[272,128]{1,0:T(8,128)(2,1)S(1)}, u32[]{:S(2)}, u32[]{:S(2)}) collective-permute-start(bf16[272,128]{1,0:T(8,128)(2,1)S(1)} %get-tuple-element.29), channel_id=1, source_target_pairs={{0,14},{1,15},{2,12},{3,13},{4,10},{5,11},{6,8},{7,9},{8,6},{9,7},... | collective-permute-start | bytes 208904 | tf_op jit(solution)/shard_map/ppermute | solution.py:462

commit v4 on v3

--- a/solution.py
+++ b/solution.py
@@ -53,58 +53,41 @@
     return jnp.dot(left, right, preferred_element_type=F32)
 
 
-def spread_kernel(signal_ref, out_ref):
-    upper = lax.broadcasted_iota(jnp.int32, (8, BLOCK), 0) < 4
-    groups, blocks = signal_ref.shape[0] // 16, signal_ref.shape[1] // BLOCK
-    for group in range(groups):
-        for quad in range(0, blocks, 4):
-            tiles = []
-            for block in range(quad, quad + 4):
-                value = signal_ref[group * 16 : group * 16 + 16, block * BLOCK : (block + 1) * BLOCK].astype(F32)
-                tiles.append((value[:8], value[8:]))
-            for half in range(2):
-                parts = [tile[half] for tile in tiles]
-                turned = [pltpu.roll(part, 4, 0) for part in parts]
-                first = [jnp.where(upper, parts[d], turned[d + 1]) for d in (0, 2)]
-                second = [jnp.where(upper, turned[d], parts[d + 1]) for d in (0, 2)]
-                device = group * 4 + half * 2
-                rows = slice(quad * 4, quad * 4 + 16)
-                out_ref[device, rows, :] = jnp.concatenate(first, axis=0).astype(BF16)
-                out_ref[device + 1, rows, :] = jnp.concatenate(second, axis=0).astype(BF16)
-
-
 def spread(signal, segments):
     beams, blocks = signal.shape[0] // segments, signal.shape[1] // BLOCK
-    if beams != 4 or signal.shape[0] % 16 or blocks % 4:
-        send = signal.reshape(segments, beams, blocks, BLOCK).transpose(0, 2, 1, 3)
-        return send.reshape(segments, blocks * beams, BLOCK)
-    return pl.pallas_call(
-        spread_kernel,
-        out_shape=jax.ShapeDtypeStruct((segments, blocks * beams, BLOCK), BF16),
-        in_specs=[VMEM],
-        out_specs=VMEM,
-        name="spread_beams",
-    )(signal)
-
-
-def prepare_kernel(replica_ref, taps_ref, weights_ref, sources_ref, left_ref, right_ref, turn_ref, interp_ref, chosen_ref, spectrum_ref):
+    send = signal.reshape(segments, beams, blocks, BLOCK).transpose(0, 2, 1, 3)
+    return send.reshape(segments, blocks * beams, BLOCK)
+
+
+def prepare_kernel(
+    segments, paired, place_ref, replica_ref, taps_ref, weights_ref, sources_ref, left_ref, right_ref, turn_ref, interp_ref, chosen_ref, spectrum_ref
+):
+    core = place_ref[0] % 2
+    blocks = chosen_ref.shape[1]
+    points = blocks // 2
     window = lax.broadcasted_iota(jnp.int32, (PAIR, BLOCK), 0)
-    for hyp in range(HYPS):
+    row = lax.broadcasted_iota(jnp.int32, (blocks, blocks), 0)
+    column = lax.broadcasted_iota(jnp.int32, (blocks, blocks), 1)
+    order = (column == row % points * 2 + row // points).astype(F32).astype(BF16)
+    held = row
+    if paired:
+        chips, local = segments // 2, blocks // segments
+        held = row % chips * 2 * local + (row // points + core) % 2 * local + row // chips % local
+    for index, hyp in enumerate([core] if paired else range(HYPS)):
+        taps, weights = taps_ref[hyp], weights_ref[hyp]
         total = jnp.zeros((PAIR, BLOCK), F32)
         for tap in range(TAPS):
-            hit = taps_ref[hyp, tap : tap + 1, :] == window
-            total = total + jnp.where(hit, weights_ref[hyp, tap : tap + 1, :], 0.0)
-        interp_ref[:, hyp * BLOCK : (hyp + 1) * BLOCK] = total.astype(BF16)
-
-    blocks = chosen_ref.shape[1]
-    column = lax.broadcasted_iota(jnp.int32, (blocks, blocks), 1)
-    for hyp in range(HYPS):
-        rows = slice(hyp * blocks, (hyp + 1) * blocks)
-        chosen_ref[rows, :] = (sources_ref[rows, :] == column).astype(F32).astype(BF16)
-
-    points = turn_ref.shape[0]
-    lines = replica_ref.shape[0]
-    high, low = split(replica_ref[...])
+            total = total + jnp.where(taps[tap : tap + 1, :] == window, weights[tap : tap + 1, :], 0.0)
+        if paired:
+            interp_ref[...] = jnp.concatenate([total[:BLOCK], total[BLOCK:]], axis=1).astype(BF16)
+        else:
+            interp_ref[:, hyp * BLOCK : (hyp + 1) * BLOCK] = total.astype(BF16)
+        hits = (held == sources_ref[pl.ds(hyp, 1), :]).astype(F32).astype(BF16)
+        picked = lax.dot_general(order, hits, (((1,), (1,)), ((), ())), preferred_element_type=F32)
+        chosen_ref[index * blocks : (index + 1) * blocks, :] = picked.astype(BF16)
+
+    lines = replica_ref.shape[0] // 2
+    high, low = split(jnp.concatenate([replica_ref[pl.ds(half, lines, stride=2), :] for half in range(2)], axis=1))
     both = dot(left_ref[:, :lines], high)
     value = both[: 2 * points] + both[2 * points :] + dot(left_ref[: 2 * points, :lines], low)
     value_re, value_im = value[:points], value[points:]
@@ -119,26 +102,27 @@
     spectrum_ref[:, PAIR:] = -value[:, PAIR:]
 
 
-def prepare(replica, taps, tap_weights, warp_blocks, tables):
+def prepare(place, replica, taps, tap_weights, warp_blocks, tables, segments, paired):
     blocks = warp_blocks.shape[1]
     points = blocks // 2
-    ordered = warp_blocks.reshape(HYPS, points, 2).transpose(0, 2, 1).reshape(HYPS * blocks, 1)
-    operands = (replica.reshape(-1, PAIR), taps.transpose(0, 2, 1), tap_weights.transpose(0, 2, 1), ordered, *tables[:3])
-    shapes = ((PAIR, HYPS * BLOCK), BF16), ((HYPS * blocks, blocks), BF16), ((points, 2 * PAIR), F32)
+    taps, tap_weights = taps.transpose(0, 2, 1), tap_weights.transpose(0, 2, 1)
+    operands = (replica.reshape(-1, BLOCK), taps, tap_weights, warp_blocks, *tables[:3])
+    interp, count = ((BLOCK, PAIR), 1) if paired else ((PAIR, HYPS * BLOCK), HYPS)
+    shapes = (interp, BF16), ((count * blocks, blocks), BF16), ((points, 2 * PAIR), F32)
 
     def whole(shape):
         return pl.BlockSpec(shape, lambda g: (0,) * len(shape))
 
     return pl.pallas_call(
-        prepare_kernel,
+        functools.partial(prepare_kernel, segments, paired),
         grid=(1,),
         out_shape=[jax.ShapeDtypeStruct(*shape) for shape in shapes],
-        in_specs=[whole(operand.shape) for operand in operands],
+        in_specs=[SMEM] + [whole(operand.shape) for operand in operands],
         out_specs=[VMEM] * len(shapes),
         compiler_params=pltpu.CompilerParams(vmem_limit_bytes=24 * 1024 * 1024),
         cost_estimate=pl.CostEstimate(flops=500_000_000, bytes_accessed=16_000_000, transcendentals=0),
         name="prepare_tables",
-    )(*operands)
+    )(place, *operands)
 
 
 def split_sum(total):
@@ -165,19 +149,15 @@
     ]
 
 
-def complex_rows(beams):
+def complex_rows(hyps, beams):
     if beams % 2:
-        return [(hyp, beam, None) for hyp in range(HYPS) for beam in range(beams)]
-    return [(hyp, beam, beam + 1) for hyp in range(HYPS) for beam in range(0, beams, 2)]
-
-
-def transform(
-    beams, source_ref, interp_ref, chosen_ref, left_ref, turn_ref, right_ref, spectrum_ref, column_ref, next_ref, block_ref, row_ref, wide_ref
-):
-    points = turn_ref.shape[0]
-    blocks = 2 * points
+        return [(hyp, beam, None) for hyp in range(hyps) for beam in range(beams)]
+    return [(hyp, beam, beam + 1) for hyp in range(hyps) for beam in range(0, beams, 2)]
+
+
+def warp(beams, source_ref, interp_ref, chosen_ref, column_ref, next_ref, block_ref):
     lines = source_ref.shape[0]
-    rows = complex_rows(beams)
+    blocks = lines // beams
     chunk = min(512, lines)
 
     for start in range(0, lines, chunk):
@@ -190,25 +170,60 @@
         )
         for hyp in range(HYPS):
             block_ref[hyp, start : start + chunk, :] = value[:, hyp * BLOCK : (hyp + 1) * BLOCK]
-
     for hyp in range(HYPS):
         warped = jnp.concatenate(
             [block_ref[hyp, pl.ds(beam, blocks, stride=beams), :].astype(BF16) for beam in range(beams)], axis=1
         )
-        gathered = dot(chosen_ref[hyp * blocks : (hyp + 1) * blocks, :], warped).astype(BF16)
-        for index, (row_hyp, *pair) in enumerate(rows):
-            if row_hyp != hyp:
-                continue
-            for part, beam in enumerate(pair):
-                for half in range(2):
-                    lane = index * PAIR + half * BLOCK
-                    target = (slice(part * points, (part + 1) * points), slice(lane, lane + BLOCK))
-                    if beam is None:
-                        column_ref[target] = jnp.zeros((points, BLOCK), BF16)
-                    else:
-                        column_ref[target] = gathered[
-                            half * points : (half + 1) * points, beam * BLOCK : (beam + 1) * BLOCK
-                        ]
+        choose(hyp, HYPS, beams, chosen_ref[hyp * blocks : (hyp + 1) * blocks, :], warped, column_ref)
+
+
+def choose(hyp, hyps, beams, chosen, warped, column_ref):
+    gathered = dot(chosen, warped).astype(BF16)
+    points = gathered.shape[0] // 2
+    for index, (row_hyp, *pair) in enumerate(complex_rows(hyps, beams)):
+        if row_hyp != hyp:
+            continue
+        for part, beam in enumerate(pair):
+            for half in range(2):
+                lane = index * PAIR + half * BLOCK
+                target = (slice(part * points, (part + 1) * points), slice(lane, lane + BLOCK))
+                if beam is None:
+                    column_ref[target] = jnp.zeros((points, BLOCK), BF16)
+                else:
+                    column_ref[target] = gathered[
+                        half * points : (half + 1) * points, beam * BLOCK : (beam + 1) * BLOCK
+                    ]
+
+
+def warp_paired(beams, core, own_ref, other_ref, interp_ref, chosen_ref, column_ref, next_ref, block_ref):
+    lines, samples = own_ref.shape
+    local = samples // BLOCK
+    for part, source_ref in enumerate((own_ref, other_ref)):
+        stacked = jnp.concatenate(
+            [source_ref[:, block * BLOCK : (block + 1) * BLOCK] for block in range(local)], axis=0
+        )
+        value = dot(stacked, interp_ref[...])
+        block_ref[part] = value[:, :BLOCK]
+        next_ref[part] = value[:, BLOCK:]
+    last = (local - 1) * lines
+    for part in range(2):
+        block_ref[part, :last, :] = block_ref[part, :last, :] + next_ref[part, lines:, :]
+        after = next_ref[1 - part, :lines, :]
+        turned = jnp.concatenate([after[beams:], after[:beams]], axis=0)
+        block_ref[part, last:, :] = block_ref[part, last:, :] + jnp.where((core + part) % 2 == 0, after, turned)
+    count = local * lines // beams
+    warped = [
+        jnp.concatenate(
+            [block_ref[part, pl.ds(beam, count, stride=beams), :].astype(BF16) for beam in range(beams)], axis=1
+        )
+        for part in range(2)
+    ]
+    choose(0, 1, beams, chosen_ref[...], jnp.concatenate(warped, axis=0), column_ref)
+
+
+def transform(hyps, beams, left_ref, turn_ref, right_ref, spectrum_ref, column_ref, row_ref, wide_ref):
+    points = turn_ref.shape[0]
+    rows = complex_rows(hyps, beams)
 
     def right_product():
         value = row_ref[...]
@@ -222,7 +237,7 @@
         row_ref[place, PAIR:] = (real * turn_im + imag * turn_re).astype(BF16)
     right_product()
     spectrum_re, spectrum_im = spectrum_ref[:, :PAIR], spectrum_ref[:, PAIR:]
-    sums = [jnp.zeros((8, PAIR), F32) for _ in range(HYPS)]
+    sums = [jnp.zeros((8, PAIR), F32) for _ in range(hyps)]
     for index, (hyp, _, _) in enumerate(rows):
         place = slice(index * points, (index + 1) * points)
         real, imag = wide_ref[place, :PAIR], wide_ref[place, PAIR:]
@@ -250,96 +265,100 @@
     return value[: value.shape[0] // 2], value[value.shape[0] // 2 :]
 
 
-def powers(matrix, column_ref, beams):
-    for index, (hyp, real_beam, imag_beam) in enumerate(complex_rows(beams)):
+def store_powers(matrix, column_ref, hyps, beams, segments, target):
+    for index, (hyp, real_beam, imag_beam) in enumerate(complex_rows(hyps, beams)):
         imag, real = left_product(matrix, column_ref, index)
         for beam, value in ((real_beam, real), (imag_beam, imag)):
-            if beam is not None:
-                yield hyp * beams + beam, value * value
-
-
-def store_powers(matrix, column_ref, beams, segments, target):
-    for number, power in powers(matrix, column_ref, beams):
-        share = power.shape[0] // segments
-        for segment in range(segments):
-            piece = power[segment * share : (segment + 1) * share, :]
-            piece = jnp.concatenate([piece[:, :BLOCK], piece[:, BLOCK:]], axis=0)
-            target(segment)[number * 2 * share : (number + 1) * 2 * share, :] = piece.astype(BF16)
-
-
-def correlate_kernel(beams, segments, source_ref, *refs):
-    tables, out_ref, scratch = refs[:6], refs[6], refs[7:]
-    totals = transform(beams, source_ref, *tables, *scratch)
-    store_powers(tables[2][...], scratch[0], beams, segments, lambda segment: out_ref.at[segment])
+            if beam is None:
+                continue
+            number = hyp * beams + beam
+            power = value * value
+            share = power.shape[0] // segments
+            for segment in range(segments):
+                piece = power[segment * share : (segment + 1) * share, :]
+                piece = jnp.concatenate([piece[:, :BLOCK], piece[:, BLOCK:]], axis=0)
+                target(segment)[number * 2 * share : (number + 1) * 2 * share, :] = piece.astype(BF16)
+
+
+def correlate_kernel(beams, segments, source_ref, interp_ref, chosen_ref, left_ref, turn_ref, right_ref, spectrum_ref, *refs):
+    out_ref, column_ref, row_ref, wide_ref, next_ref, block_ref = refs
+    warp(beams, source_ref, interp_ref, chosen_ref, column_ref, next_ref, block_ref)
+    totals = transform(HYPS, beams, left_ref, turn_ref, right_ref, spectrum_ref, column_ref, row_ref, wide_ref)
+    store_powers(left_ref[...], column_ref, HYPS, beams, segments, lambda segment: out_ref.at[segment])
     tail = tail_of(totals)
     for segment in range(segments):
         out_ref[segment, out_ref.shape[1] - 16 :, :] = tail
 
 
-def first_half_kernel(beams, segments, place_ref, source_ref, *refs):
-    tables, halves_ref, column_ref, theirs_ref, scratch = refs[:6], refs[6], refs[7], refs[8], refs[9:]
-    totals = transform(beams, source_ref, *tables, column_ref, *scratch)
+def first_half_kernel(
+    beams, segments, place_ref, own_ref, other_ref, interp_ref, chosen_ref, left_ref, turn_ref, right_ref, spectrum_ref, halves_ref, *refs
+):
+    column_ref, theirs_ref, row_ref, wide_ref, next_ref, block_ref = refs
+    core = place_ref[0] % 2
+    warp_paired(beams, core, own_ref, other_ref, interp_ref, chosen_ref, column_ref, next_ref, block_ref)
+    (total,) = transform(1, beams, left_ref, turn_ref, right_ref, spectrum_ref, column_ref, row_ref, wide_ref)
     chips = segments // 2
     lines = (theirs_ref.shape[0] - 16) // chips
-    parity = (place_ref[0] + 1) % 2
     store_powers(
-        halves_ref[parity], column_ref, beams, chips, lambda chip: theirs_ref.at[chip * lines : (chip + 1) * lines]
+        halves_ref[1 - core], column_ref, 1, beams, chips, lambda chip: theirs_ref.at[chip * lines : (chip + 1) * lines]
     )
-    theirs_ref[chips * lines :, :] = tail_of(totals)
+    theirs_ref[chips * lines :, :] = tail_of([jnp.where(core == hyp, total, 0.0) for hyp in range(HYPS)])
 
 
 def second_half_kernel(beams, segments, place_ref, column_ref, halves_ref, mine_ref):
     chips = segments // 2
     lines = mine_ref.shape[0] // chips
-    parity = place_ref[0] % 2
     store_powers(
-        halves_ref[parity], column_ref, beams, chips, lambda chip: mine_ref.at[chip * lines : (chip + 1) * lines]
+        halves_ref[place_ref[0] % 2],
+        column_ref,
+        1,
+        beams,
+        chips,
+        lambda chip: mine_ref.at[chip * lines : (chip + 1) * lines],
     )
 
 
-def correlate_shapes(lines, points, beams):
-    count = len(complex_rows(beams))
-    column = ((2 * points, count * PAIR), BF16)
-    scratch = [
-        ((lines + 8, PAIR), F32),
-        ((HYPS, lines, BLOCK), F32),
+def correlate_shapes(points, count):
+    return (
+        ((2 * points, count * PAIR), BF16),
         ((count * points, 2 * PAIR), BF16),
         ((count * points, 2 * PAIR), F32),
-    ]
-    return column, scratch
+    )
 
 
 def correlate(source, interp, chosen, spectrum, tables, beams, segments):
     left, right, turn, _ = tables
-    points = turn.shape[0]
-    column, scratch = correlate_shapes(source.shape[0], points, beams)
+    points, lines = turn.shape[0], source.shape[0]
+    scratch = correlate_shapes(points, len(complex_rows(HYPS, beams)))
+    scratch += (((lines + 8, PAIR), F32), ((HYPS, lines, BLOCK), F32))
     return pl.pallas_call(
         functools.partial(correlate_kernel, beams, segments),
         out_shape=jax.ShapeDtypeStruct((segments, HYPS * beams * 2 * (points // segments) + 16, BLOCK), BF16),
         in_specs=[VMEM] * 7,
         out_specs=VMEM,
-        scratch_shapes=[pltpu.VMEM(*shape) for shape in (column, *scratch)],
+        scratch_shapes=[pltpu.VMEM(*shape) for shape in scratch],
         compiler_params=pltpu.CompilerParams(vmem_limit_bytes=48 * 1024 * 1024),
         cost_estimate=pl.CostEstimate(flops=4_000_000_000, bytes_accessed=6_000_000, transcendentals=0),
         name="warp_correlate",
     )(source, interp, chosen, left, turn, right, spectrum)
 
 
-def correlate_in_halves(place, source, interp, chosen, spectrum, tables, beams, segments):
+def correlate_in_halves(place, own, other, interp, chosen, spectrum, tables, beams, segments):
     left, right, turn, halves = tables
-    points = turn.shape[0]
-    column, scratch = correlate_shapes(source.shape[0], points, beams)
-    rows = segments // 2 * HYPS * beams * 2 * (points // segments)
+    points, lines = turn.shape[0], own.shape[0] * own.shape[1] // BLOCK
+    column, *scratch = correlate_shapes(points, len(complex_rows(1, beams)))
+    scratch += [((2, lines, BLOCK), F32), ((2, lines, BLOCK), F32)]
+    rows = segments // 2 * beams * 2 * (points // segments)
     columns, theirs = pl.pallas_call(
         functools.partial(first_half_kernel, beams, segments),
         out_shape=(jax.ShapeDtypeStruct(*column), jax.ShapeDtypeStruct((rows + 16, BLOCK), BF16)),
-        in_specs=[SMEM] + [VMEM] * 8,
+        in_specs=[SMEM] + [VMEM] * 9,
         out_specs=(VMEM, VMEM),
         scratch_shapes=[pltpu.VMEM(*shape) for shape in scratch],
         compiler_params=pltpu.CompilerParams(vmem_limit_bytes=24 * 1024 * 1024),
         cost_estimate=pl.CostEstimate(flops=4_000_000_000, bytes_accessed=6_000_000, transcendentals=0),
         name="warp_correlate",
-    )(place, source, interp, chosen, left, turn, right, spectrum, halves)
+    )(place, own, other, interp, chosen, left, turn, right, spectrum, halves)
     mine = pl.pallas_call(
         functools.partial(second_half_kernel, beams, segments),
         out_shape=jax.ShapeDtypeStruct((rows, BLOCK), BF16),
@@ -427,13 +446,13 @@
     lines = chunk_refs[0].shape[0] - 16
     totals = totals_of([ref[lines:, :] for ref in chunk_refs])
     inverse = [1.0 / (total / count + 1e-06) for total in totals]
-    run = lines // 2 // HYPS
-    for offset, ref in zip(chip_order(len(chunk_refs)), chunk_refs):
-        for part in range(2):
-            start = pl.multiple_of(((chip ^ offset) * 2 + (core ^ part)) * run, run)
-            for hyp in range(HYPS):
-                first = (part * HYPS + hyp) * run
-                scratch_ref[hyp, pl.ds(start, run), :] = ref[first : first + run, :].astype(F32) * inverse[hyp]
+    run = lines // 2
+    for part in range(2):
+        hyp = core ^ part
+        scale = jnp.where(hyp == 0, inverse[0], inverse[1])
+        for offset, ref in zip(chip_order(len(chunk_refs)), chunk_refs):
+            rows = pl.ds(pl.multiple_of((chip ^ offset) * run, run), run)
+            scratch_ref[hyp, rows, :] = ref[part * run : (part + 1) * run, :].astype(F32) * scale
     beams = out_ref.shape[1]
     step = scratch_ref.shape[1] // beams
     for hyp in range(HYPS):
@@ -467,16 +486,22 @@
     beams = signal.shape[0] // segments
     samples = signal.shape[1] * segments
     count = float(BEAMS * samples)
-    received = lax.all_to_all(spread(signal, segments), "tm", split_axis=0, concat_axis=0, tiled=True)
-    source = received.reshape(-1, BLOCK)
+    paired = segments == 16
+    place = lax.axis_index("tm").astype(jnp.int32).reshape(1)
     tables = transform_tables(samples // PAIR, segments)
-    interp, chosen, spectrum = prepare(replica, taps, tap_weights, warp_blocks, tables)
-    if segments != 16:
-        sent = correlate(source, interp, chosen, spectrum, tables, beams, segments)
+    prepared = prepare(place, replica, taps, tap_weights, warp_blocks, tables, segments, paired)
+    if not paired:
+        received = lax.all_to_all(spread(signal, segments), "tm", split_axis=0, concat_axis=0, tiled=True)
+        sent = correlate(received.reshape(-1, BLOCK), *prepared, tables, beams, segments)
         back = lax.all_to_all(sent, "tm", split_axis=0, concat_axis=0, tiled=True)
         return finish(back, count, beams)
-    place = lax.axis_index("tm").astype(jnp.int32).reshape(1)
-    theirs, mine = correlate_in_halves(place, source, interp, chosen, spectrum, tables, beams, segments)
+    groups = [list(range(core, segments, 2)) for core in range(2)]
+    own = lax.all_to_all(
+        signal.reshape(segments // 2, 2 * beams, -1), "tm", 0, 0, axis_index_groups=groups, tiled=True
+    ).reshape(signal.shape)
+    own, *prepared = lax.optimization_barrier((own, *prepared))
+    other = exchange(own, 1, segments)
+    theirs, mine = correlate_in_halves(place, own, other, *prepared, tables, 2 * beams, segments)
     chips = segments // 2
     chunks = arrange(place, mine, theirs, exchange(theirs, 1, segments), chips)
     arrived = [

time: 40.1 us -> 39.7 us (0.990)
  Pallas kernels: 7.01 us -> 5.33 us
  local copies, waits for them, and re-layouts: 1.87 us -> 2.85 us
  waiting for transfers between devices: 14.1 us -> 15 us
  starting transfers between devices: 16.7 us -> 16.1 us
    ppermute x8 -> x9, waiting for transfers between devices: 7.07 us -> 10 us  [exchange(): lax.ppermute(value, 'tm', [(index, index ^ offset) for index in range(seg...]
    unnamed x14 -> x20, local copies, waits for them, and re-layouts: 0.63 us -> 2.85 us
    all_to_all x1, waiting for transfers between devices: 7.08 us -> 4.95 us  [body(): lax.all_to_all(signal.reshape(segments // 2, 2 * beams, -1), 'tm', 0, 0,...]
    pallas_call x2 -> x1, Pallas kernels: 2.81 us -> 1.08 us  [prepare(): pl.pallas_call(functools.partial(prepare_kernel, segments, paired), grid=...]
    reshape x3 -> x0, local copies, waits for them, and re-layouts: 1.17 us -> none  [the longest x1 0.87 us: prepare(): replica.reshape(-1, PAIR)]
    ppermute x8 -> x9, starting transfers between devices: 9.29 us -> 8.69 us  [exchange(): lax.ppermute(value, 'tm', [(index, index ^ offset) for index in range(seg...]
  transfers between devices with their start and end apart: 9 -> 10, of which waited for: 7 -> 8; matrix products, arithmetic and copies ran while one was open for 3% -> 0% of each run, Pallas kernels for 3% -> 3%
where the time goes in v4:
time: 39.7 us; the launch traced here: 39.4 us
  starting transfers between devices  16.1 us (41%)
  waiting for transfers between devices  15 us (38%)
  Pallas kernels  5.33 us (13%)
  local copies, waits for them, and re-layouts  2.85 us (7%)
    ppermute x9, waiting for transfers between devices, exchange(): lax.ppermute(value, 'tm', [(index, index ^ offset) for index in range(seg...  10 us
    ppermute x9, starting transfers between devices, exchange(): lax.ppermute(value, 'tm', [(index, index ^ offset) for index in range(seg...  8.69 us
    all_to_all x1, starting transfers between devices, body(): lax.all_to_all(signal.reshape(segments // 2, 2 * beams, -1), 'tm', 0, 0,...  7.43 us
    all_to_all x1, waiting for transfers between devices, body(): lax.all_to_all(signal.reshape(segments // 2, 2 * beams, -1), 'tm', 0, 0,...  4.95 us
    unnamed x20, local copies, waits for them, and re-layouts  2.85 us
    pallas_call x1, Pallas kernels, correlate_in_halves(): pl.pallas_call(functools.partial(first_half_kernel, beams, segments), out...  2.62 us
    pallas_call x1, Pallas kernels, join(): pl.pallas_call(functools.partial(join_kernel, count), out_shape=jax.Shape...  1.24 us
    pallas_call x1, Pallas kernels, prepare(): pl.pallas_call(functools.partial(prepare_kernel, segments, paired), grid=...  1.08 us
  transfers between devices with their start and end apart: 10, of which 8 were waited for; matrix products, arithmetic and copies ran while one was open for 0% of the time, Pallas kernels for 3%

profile of v4, /device:TPU:0, one launch (start us, length us, event | category | flops | bytes accessed | tf_op | source)
XLA Modules:
  0.0 39.4 jit_solution(5222421363518704220)
XLA Ops:
  0.0 0.0 copy-start
  0.0 0.0 copy-start.2
  0.0 0.0 copy-start.7
  0.0 7.4 %all-to-all-start = ((bf16[8,8,2048]{2,1,0:T(8,128)(2,1)}), bf16[8,8,2048]{2,1,0:T(8,128)(2,1)S(1)}, u32[]{:S(2)}, u32[]{:S(2)}) async-start(bf16[8,8,2048]{2,1,0:T(8,128)(2,1)} %bitcast.11), calls=%async_computation | async-start | bytes 524288 | tf_op jit(solution)/shard_map/all_to_all | solution.py:499
  7.4 0.0 copy-start.1
  7.4 0.0 copy-start.3
  7.5 0.0 copy-done
  7.5 0.0 copy-done.2
  7.5 0.0 copy-done.7
  7.5 0.6 %copy-done.1 = s32[2,128,8]{1,2,0:T(8,128)S(1)} copy-done((s32[2,128,8]{1,2,0:T(8,128)S(1)}, s32[2,128,8]{1,2,0:T(8,128)}, u32[]{:S(2)}) %copy-start.1) | copy-done | bytes 8216
  8.1 0.0 copy-done.3
  8.1 0.0 copy-start.4
  8.1 1.2 %copy-done.4 = bf16[1024,512]{1,0:T(8,128)(2,1)S(1)} copy-done((bf16[1024,512]{1,0:T(8,128)(2,1)S(1)}, bf16[1024,512]{1,0:T(8,128)(2,1)}, u32[]{:S(2)}) %copy-start.4) | copy-done | bytes 1048600
  9.4 0.0 copy-start.8
  9.4 0.9 %copy-done.8 = bf16[512,256]{1,0:T(8,128)(2,1)S(1)} copy-done((bf16[512,256]{1,0:T(8,128)(2,1)S(1)}, bf16[512,256]{1,0:T(8,128)(2,1)}, u32[]{:S(2)}) %copy-start.8) | copy-done | bytes 262168
  10.3 0.0 copy-start.5
  10.3 0.0 copy-start.6
  10.3 0.0 copy-start.9
  10.3 1.1 %prepare_tables.1 = (bf16[128,256]{1,0:T(8,128)(2,1)S(1)}, bf16[256,256]{1,0:T(8,128)(2,1)S(1)}, f32[128,512]{1,0:T(8,128)S(1)}) custom-call(s32[1]{0:T(128)} %bitcast.place_ref, f32[128,128]{1,0:T(8,128)S(1)} %bitcast.8, s32[2,8,128]{2,1,0:T(8,128)S(1)} %bitcast.9, f32[2,8,128]{2,1,0:T(8,128)S(1)} %bitcast.10, s32[2,256]{1,0:T(2,128)S(1)} %copy-done.3, ...), custom_call_target="tpu_custom_call" | custom-call | flops 500000000 | bytes 16000000 | tf_op jit(solution)/shard_map/prepare_tables/pallas_call | solution.py:116
  11.4 4.9 %all-to-all-done = bf16[8,8,2048]{2,1,0:T(8,128)(2,1)S(1)} async-done(((bf16[8,8,2048]{2,1,0:T(8,128)(2,1)}), bf16[8,8,2048]{2,1,0:T(8,128)(2,1)S(1)}, u32[]{:S(2)}, u32[]{:S(2)}) %all-to-all-start) | async-done | bytes 262176 | tf_op jit(solution)/shard_map/all_to_all | solution.py:499
  16.4 0.0 collective-permute-start
  16.4 1.5 %collective-permute-done.other_ref = bf16[64,2048]{1,0:T(8,128)(2,1)S(1)} collective-permute-done((bf16[64,2048]{1,0:T(8,128)(2,1)S(1)}, bf16[64,2048]{1,0:T(8,128)(2,1)S(1)}, u32[]{:S(2)}, u32[]{:S(2)}) %collective-permute-start) | collective-permute-done | bytes 262176 | tf_op jit(solution)/shard_map/ppermute | solution.py:481
  17.9 0.0 copy-done.5
  17.9 0.0 copy-done.6
  17.9 0.0 copy-done.9
  17.9 2.6 %warp_correlate.1 = (bf16[256,1024]{1,0:T(8,128)(2,1)S(1)}, bf16[1040,128]{1,0:T(8,128)(2,1)S(1)}) custom-call(s32[1]{0:T(128)} %bitcast.place_ref, bf16[64,2048]{1,0:T(8,128)(2,1)S(1)} %bitcast.7, bf16[64,2048]{1,0:T(8,128)(2,1)S(1)} %collective-permute-done.other_ref, bf16[128,256]{1,0:T(8,128)(2,1)S(1)} %get-tuple-element.26.interp_ref, ...), custom_call_target="tpu_custom_call" | custom-call | flops 4000000000 | bytes 6000000 | tf_op jit(solution)/shard_map/warp_correlate/pallas_call | solution.py:352
  20.5 0.2 collective-permute-start.1
  20.7 0.3 second_half.1.mine_ref
  21.0 1.1 %collective-permute-done.1.got_ref = bf16[1040,128]{1,0:T(8,128)(2,1)S(1)} collective-permute-done((bf16[1040,128]{1,0:T(8,128)(2,1)S(1)}, bf16[1040,128]{1,0:T(8,128)(2,1)S(1)}, u32[]{:S(2)}, u32[]{:S(2)}) %collective-permute-start.1) | collective-permute-done | bytes 266272 | tf_op jit(solution)/shard_map/ppermute | solution.py:481
  22.1 0.1 arrange_chips.1
  22.2 1.1 %collective-permute-start.2 = (bf16[272,128]{1,0:T(8,128)(2,1)S(1)}, bf16[272,128]{1,0:T(8,128)(2,1)S(1)}, u32[]{:S(2)}, u32[]{:S(2)}) collective-permute-start(bf16[272,128]{1,0:T(8,128)(2,1)S(1)} %get-tuple-element.31), channel_id=1, source_target_pairs={{0,8},{1,9},{2,10},{3,11},{4,12},{5,13},{6,14},{7,15},{8,0},{9,1},... | collective-permute-start | bytes 208904 | tf_op jit(solution)/shard_map/ppermute | solution.py:481
  23.3 0.4 %collective-permute-start.3 = (bf16[272,128]{1,0:T(8,128)(2,1)S(1)}, bf16[272,128]{1,0:T(8,128)(2,1)S(1)}, u32[]{:S(2)}, u32[]{:S(2)}) collective-permute-start(bf16[272,128]{1,0:T(8,128)(2,1)S(1)} %get-tuple-element.32), channel_id=1, source_target_pairs={{0,2},{1,3},{2,0},{3,1},{4,6},{5,7},{6,4},{7,5},{8,10},{9,11},{10,... | collective-permute-start | bytes 208904 | tf_op jit(solution)/shard_map/ppermute | solution.py:481
  23.8 2.9 %collective-permute-start.4 = (bf16[272,128]{1,0:T(8,128)(2,1)S(1)}, bf16[272,128]{1,0:T(8,128)(2,1)S(1)}, u32[]{:S(2)}, u32[]{:S(2)}) collective-permute-start(bf16[272,128]{1,0:T(8,128)(2,1)S(1)} %get-tuple-element.33), channel_id=1, source_target_pairs={{0,10},{1,11},{2,8},{3,9},{4,14},{5,15},{6,12},{7,13},{8,2},{9,3},... | collective-permute-start | bytes 208904 | tf_op jit(solution)/shard_map/ppermute | solution.py:481
  26.7 1.1 %collective-permute-start.5 = (bf16[272,128]{1,0:T(8,128)(2,1)S(1)}, bf16[272,128]{1,0:T(8,128)(2,1)S(1)}, u32[]{:S(2)}, u32[]{:S(2)}) collective-permute-start(bf16[272,128]{1,0:T(8,128)(2,1)S(1)} %get-tuple-element.34), channel_id=1, source_target_pairs={{0,4},{1,5},{2,6},{3,7},{4,0},{5,1},{6,2},{7,3},{8,12},{9,13},{10,... | collective-permute-start | bytes 208904 | tf_op jit(solution)/shard_map/ppermute | solution.py:481
  27.8 1.4 %collective-permute-start.6 = (bf16[272,128]{1,0:T(8,128)(2,1)S(1)}, bf16[272,128]{1,0:T(8,128)(2,1)S(1)}, u32[]{:S(2)}, u32[]{:S(2)}) collective-permute-start(bf16[272,128]{1,0:T(8,128)(2,1)S(1)} %get-tuple-element.35), channel_id=1, source_target_pairs={{0,12},{1,13},{2,14},{3,15},{4,8},{5,9},{6,10},{7,11},{8,4},{9,5},... | collective-permute-start | bytes 208904 | tf_op jit(solution)/shard_map/ppermute | solution.py:481
  29.2 1.8 %collective-permute-done.2.refs_0_ = bf16[272,128]{1,0:T(8,128)(2,1)S(1)} collective-permute-done((bf16[272,128]{1,0:T(8,128)(2,1)S(1)}, bf16[272,128]{1,0:T(8,128)(2,1)S(1)}, u32[]{:S(2)}, u32[]{:S(2)}) %collective-permute-start.2) | collective-permute-done | bytes 69664 | tf_op jit(solution)/shard_map/ppermute | solution.py:481
  31.0 0.0 collective-permute-start.7
  31.0 0.0 collective-permute-done.3.refs_1_
  31.0 1.5 %collective-permute-start.8 = (bf16[272,128]{1,0:T(8,128)(2,1)S(1)}, bf16[272,128]{1,0:T(8,128)(2,1)S(1)}, u32[]{:S(2)}, u32[]{:S(2)}) collective-permute-start(bf16[272,128]{1,0:T(8,128)(2,1)S(1)} %get-tuple-element.37), channel_id=1, source_target_pairs={{0,14},{1,15},{2,12},{3,13},{4,10},{5,11},{6,8},{7,9},{8,6},{9,7},... | collective-permute-start | bytes 208904 | tf_op jit(solution)/shard_map/ppermute | solution.py:481
  32.5 0.5 %collective-permute-done.4.refs_2_ = bf16[272,128]{1,0:T(8,128)(2,1)S(1)} collective-permute-done((bf16[272,128]{1,0:T(8,128)(2,1)S(1)}, bf16[272,128]{1,0:T(8,128)(2,1)S(1)}, u32[]{:S(2)}, u32[]{:S(2)}) %collective-permute-start.4) | collective-permute-done | bytes 69664 | tf_op jit(solution)/shard_map/ppermute | solution.py:481
  33.1 2.0 %collective-permute-done.5.refs_3_ = bf16[272,128]{1,0:T(8,128)(2,1)S(1)} collective-permute-done((bf16[272,128]{1,0:T(8,128)(2,1)S(1)}, bf16[272,128]{1,0:T(8,128)(2,1)S(1)}, u32[]{:S(2)}, u32[]{:S(2)}) %collective-permute-start.5) | collective-permute-done | bytes 69664 | tf_op jit(solution)/shard_map/ppermute | solution.py:481
  35.1 0.0 collective-permute-done.6.refs_4_
  35.1 1.4 %collective-permute-done.7.refs_5_ = bf16[272,128]{1,0:T(8,128)(2,1)S(1)} collective-permute-done((bf16[272,128]{1,0:T(8,128)(2,1)S(1)}, bf16[272,128]{1,0:T(8,128)(2,1)S(1)}, u32[]{:S(2)}, u32[]{:S(2)}) %collective-permute-start.7) | collective-permute-done | bytes 69664 | tf_op jit(solution)/shard_map/ppermute | solution.py:481
  36.5 1.6 %collective-permute-done.8.refs_6_ = bf16[272,128]{1,0:T(8,128)(2,1)S(1)} collective-permute-done((bf16[272,128]{1,0:T(8,128)(2,1)S(1)}, bf16[272,128]{1,0:T(8,128)(2,1)S(1)}, u32[]{:S(2)}, u32[]{:S(2)}) %collective-permute-start.8) | collective-permute-done | bytes 69664 | tf_op jit(solution)/shard_map/ppermute | solution.py:481
  38.1 1.2 %scale_power.1 = bf16[2,64,2048]{2,1,0:T(8,128)(2,1)} custom-call(s32[1]{0:T(128)} %bitcast.place_ref, bf16[272,128]{1,0:T(8,128)(2,1)S(1)} %collective-permute-done.2.refs_0_, bf16[272,128]{1,0:T(8,128)(2,1)S(1)} %collective-permute-done.3.refs_1_, bf16[272,128]{1,0:T(8,128)(2,1)S(1)} %collective-permute-done.4.refs_2_, ...), custom_call_target="tpu_custom_call" | custom-call | flops 1000000 | bytes 1200000 | tf_op jit(solution)/shard_map/scale_power/pallas_call | solution.py:468
Async XLA Ops:
  0.0 7.5 %copy-start = (f32[16384]{0:T(1024)S(1)}, f32[16384]{0:T(1024)}, u32[]{:S(2)}) copy-start(f32[16384]{0:T(1024)} %param.13) | copy-start | bytes 196612
  0.0 7.5 %copy-start.2 = (f32[2,128,8]{1,2,0:T(8,128)S(1)}, f32[2,128,8]{1,2,0:T(8,128)}, u32[]{:S(2)}) copy-start(f32[2,128,8]{1,2,0:T(8,128)} %param.12) | copy-start | bytes 24580
  0.0 7.5 %copy-start.7 = (f32[128,512]{1,0:T(8,128)S(1)}, f32[128,512]{1,0:T(8,128)}, u32[]{:S(2)}) copy-start(f32[128,512]{1,0:T(8,128)} %constant.14.clone.turn_ref) | copy-start | bytes 786436
  0.0 16.3 %all-to-all-start = ((bf16[8,8,2048]{2,1,0:T(8,128)(2,1)}), bf16[8,8,2048]{2,1,0:T(8,128)(2,1)S(1)}, u32[]{:S(2)}, u32[]{:S(2)}) async-start(bf16[8,8,2048]{2,1,0:T(8,128)(2,1)} %bitcast.11), calls=%async_computation | async-start | bytes 524288 | tf_op jit(solution)/shard_map/all_to_all | solution.py:499
  7.4 0.7 %copy-start.1 = (s32[2,128,8]{1,2,0:T(8,128)S(1)}, s32[2,128,8]{1,2,0:T(8,128)}, u32[]{:S(2)}) copy-start(s32[2,128,8]{1,2,0:T(8,128)} %param.11) | copy-start | bytes 24580
  7.4 0.7 %copy-start.3 = (s32[2,256]{1,0:T(2,128)S(1)}, s32[2,256]{1,0:T(2,128)}, u32[]{:S(2)}) copy-start(s32[2,256]{1,0:T(2,128)} %sources_ref.1) | copy-start | bytes 6148
  8.1 1.2 %copy-start.4 = (bf16[1024,512]{1,0:T(8,128)(2,1)S(1)}, bf16[1024,512]{1,0:T(8,128)(2,1)}, u32[]{:S(2)}) copy-start(bf16[1024,512]{1,0:T(8,128)(2,1)} %constant.13.clone.right_ref) | copy-start | bytes 3145732
  9.4 0.9 %copy-start.8 = (bf16[512,256]{1,0:T(8,128)(2,1)S(1)}, bf16[512,256]{1,0:T(8,128)(2,1)}, u32[]{:S(2)}) copy-start(bf16[512,256]{1,0:T(8,128)(2,1)} %constant.12.clone.left_ref) | copy-start | bytes 786436
  10.3 7.6 %copy-start.5 = (bf16[1024,512]{1,0:T(8,128)(2,1)S(1)}, bf16[1024,512]{1,0:T(8,128)(2,1)}, u32[]{:S(2)}) copy-start(bf16[1024,512]{1,0:T(8,128)(2,1)} %constant.13.clone.right_ref) | copy-start | bytes 3145732
  10.3 7.6 %copy-start.6 = (bf16[2,256,256]{2,1,0:T(8,128)(2,1)S(1)}, bf16[2,256,256]{2,1,0:T(8,128)(2,1)}, u32[]{:S(2)}) copy-start(bf16[2,256,256]{2,1,0:T(8,128)(2,1)} %constant.15.clone.halves_ref) | copy-start | bytes 786436
  10.3 7.6 %copy-start.9 = (bf16[512,256]{1,0:T(8,128)(2,1)S(1)}, bf16[512,256]{1,0:T(8,128)(2,1)}, u32[]{:S(2)}) copy-start(bf16[512,256]{1,0:T(8,128)(2,1)} %constant.12.clone.left_ref) | copy-start | bytes 786436
  16.4 1.5 %collective-permute-start = (bf16[64,2048]{1,0:T(8,128)(2,1)S(1)}, bf16[64,2048]{1,0:T(8,128)(2,1)S(1)}, u32[]{:S(2)}, u32[]{:S(2)}) collective-permute-start(bf16[64,2048]{1,0:T(8,128)(2,1)S(1)} %bitcast.6), channel_id=1, source_target_pairs={{0,1},{1,0},{2,3},{3,2},{4,5},{5,4},{6,7},{7,6},{8,9},{9,8},{10,11... | collective-permute-start | bytes 786440 | tf_op jit(solution)/shard_map/ppermute | solution.py:481
  20.5 1.6 %collective-permute-start.1 = (bf16[1040,128]{1,0:T(8,128)(2,1)S(1)}, bf16[1040,128]{1,0:T(8,128)(2,1)S(1)}, u32[]{:S(2)}, u32[]{:S(2)}) collective-permute-start(bf16[1040,128]{1,0:T(8,128)(2,1)S(1)} %get-tuple-element.30.sums_ref), channel_id=1, source_target_pairs={{0,1},{1,0},{2,3},{3,2},{4,5},{5,4},{6,7},{7,6},{8,9},{9,8},{10,11... | collective-permute-start | bytes 798728 | tf_op jit(solution)/shard_map/ppermute | solution.py:481
  22.2 8.8 %collective-permute-start.2 = (bf16[272,128]{1,0:T(8,128)(2,1)S(1)}, bf16[272,128]{1,0:T(8,128)(2,1)S(1)}, u32[]{:S(2)}, u32[]{:S(2)}) collective-permute-start(bf16[272,128]{1,0:T(8,128)(2,1)S(1)} %get-tuple-element.31), channel_id=1, source_target_pairs={{0,8},{1,9},{2,10},{3,11},{4,12},{5,13},{6,14},{7,15},{8,0},{9,1},... | collective-permute-start | bytes 208904 | tf_op jit(solution)/shard_map/ppermute | solution.py:481
  23.3 7.7 %collective-permute-start.3 = (bf16[272,128]{1,0:T(8,128)(2,1)S(1)}, bf16[272,128]{1,0:T(8,128)(2,1)S(1)}, u32[]{:S(2)}, u32[]{:S(2)}) collective-permute-start(bf16[272,128]{1,0:T(8,128)(2,1)S(1)} %get-tuple-element.32), channel_id=1, source_target_pairs={{0,2},{1,3},{2,0},{3,1},{4,6},{5,7},{6,4},{7,5},{8,10},{9,11},{10,... | collective-permute-start | bytes 208904 | tf_op jit(solution)/shard_map/ppermute | solution.py:481
  23.8 9.3 %collective-permute-start.4 = (bf16[272,128]{1,0:T(8,128)(2,1)S(1)}, bf16[272,128]{1,0:T(8,128)(2,1)S(1)}, u32[]{:S(2)}, u32[]{:S(2)}) collective-permute-start(bf16[272,128]{1,0:T(8,128)(2,1)S(1)} %get-tuple-element.33), channel_id=1, source_target_pairs={{0,10},{1,11},{2,8},{3,9},{4,14},{5,15},{6,12},{7,13},{8,2},{9,3},... | collective-permute-start | bytes 208904 | tf_op jit(solution)/shard_map/ppermute | solution.py:481
  26.7 8.4 %collective-permute-start.5 = (bf16[272,128]{1,0:T(8,128)(2,1)S(1)}, bf16[272,128]{1,0:T(8,128)(2,1)S(1)}, u32[]{:S(2)}, u32[]{:S(2)}) collective-permute-start(bf16[272,128]{1,0:T(8,128)(2,1)S(1)} %get-tuple-element.34), channel_id=1, source_target_pairs={{0,4},{1,5},{2,6},{3,7},{4,0},{5,1},{6,2},{7,3},{8,12},{9,13},{10,... | collective-permute-start | bytes 208904 | tf_op jit(solution)/shard_map/ppermute | solution.py:481
  27.8 7.4 %collective-permute-start.6 = (bf16[272,128]{1,0:T(8,128)(2,1)S(1)}, bf16[272,128]{1,0:T(8,128)(2,1)S(1)}, u32[]{:S(2)}, u32[]{:S(2)}) collective-permute-start(bf16[272,128]{1,0:T(8,128)(2,1)S(1)} %get-tuple-element.35), channel_id=1, source_target_pairs={{0,12},{1,13},{2,14},{3,15},{4,8},{5,9},{6,10},{7,11},{8,4},{9,5},... | collective-permute-start | bytes 208904 | tf_op jit(solution)/shard_map/ppermute | solution.py:481
  31.0 5.5 %collective-permute-start.7 = (bf16[272,128]{1,0:T(8,128)(2,1)S(1)}, bf16[272,128]{1,0:T(8,128)(2,1)S(1)}, u32[]{:S(2)}, u32[]{:S(2)}) collective-permute-start(bf16[272,128]{1,0:T(8,128)(2,1)S(1)} %get-tuple-element.36), channel_id=1, source_target_pairs={{0,6},{1,7},{2,4},{3,5},{4,2},{5,3},{6,0},{7,1},{8,14},{9,15},{10,... | collective-permute-start | bytes 208904 | tf_op jit(solution)/shard_map/ppermute | solution.py:481
  31.0 7.1 %collective-permute-start.8 = (bf16[272,128]{1,0:T(8,128)(2,1)S(1)}, bf16[272,128]{1,0:T(8,128)(2,1)S(1)}, u32[]{:S(2)}, u32[]{:S(2)}) collective-permute-start(bf16[272,128]{1,0:T(8,128)(2,1)S(1)} %get-tuple-element.37), channel_id=1, source_target_pairs={{0,14},{1,15},{2,12},{3,13},{4,10},{5,11},{6,8},{7,9},{8,6},{9,7},... | collective-permute-start | bytes 208904 | tf_op jit(solution)/shard_map/ppermute | solution.py:481

commit v5 on v4

--- a/solution.py
+++ b/solution.py
@@ -15,6 +15,7 @@
 TAPS = 8
 REPLICA = 16384
 HYPS = 2
+TAIL = 8
 F32 = jnp.float32
 BF16 = jnp.bfloat16
 VMEM = pl.BlockSpec(memory_space=pltpu.VMEM)
@@ -132,8 +133,8 @@
 
 
 def tail_of(totals):
-    place = lax.broadcasted_iota(jnp.int32, (16, BLOCK), 0)
-    tail = jnp.zeros((16, BLOCK), F32)
+    place = lax.broadcasted_iota(jnp.int32, (TAIL, BLOCK), 0)
+    tail = jnp.zeros((TAIL, BLOCK), F32)
     for hyp, total in enumerate(totals):
         for index, piece in enumerate(split_sum(total)):
             tail = jnp.where(place == hyp * 3 + index, piece, tail)
@@ -141,7 +142,7 @@
 
 
 def totals_of(tails):
-    place = lax.broadcasted_iota(jnp.int32, (16, BLOCK), 0)
+    place = lax.broadcasted_iota(jnp.int32, (TAIL, BLOCK), 0)
     total = functools.reduce(jnp.add, [tail.astype(F32) for tail in tails])
     return [
         jnp.sum(jnp.where((place >= 3 * hyp) & (place < 3 * hyp + 3), total, 0.0), axis=0, keepdims=True)
@@ -287,7 +288,7 @@
     store_powers(left_ref[...], column_ref, HYPS, beams, segments, lambda segment: out_ref.at[segment])
     tail = tail_of(totals)
     for segment in range(segments):
-        out_ref[segment, out_ref.shape[1] - 16 :, :] = tail
+        out_ref[segment, out_ref.shape[1] - TAIL :, :] = tail
 
 
 def first_half_kernel(
@@ -298,7 +299,7 @@
     warp_paired(beams, core, own_ref, other_ref, interp_ref, chosen_ref, column_ref, next_ref, block_ref)
     (total,) = transform(1, beams, left_ref, turn_ref, right_ref, spectrum_ref, column_ref, row_ref, wide_ref)
     chips = segments // 2
-    lines = (theirs_ref.shape[0] - 16) // chips
+    lines = (theirs_ref.shape[0] - TAIL) // chips
     store_powers(
         halves_ref[1 - core], column_ref, 1, beams, chips, lambda chip: theirs_ref.at[chip * lines : (chip + 1) * lines]
     )
@@ -333,7 +334,7 @@
     scratch += (((lines + 8, PAIR), F32), ((HYPS, lines, BLOCK), F32))
     return pl.pallas_call(
         functools.partial(correlate_kernel, beams, segments),
-        out_shape=jax.ShapeDtypeStruct((segments, HYPS * beams * 2 * (points // segments) + 16, BLOCK), BF16),
+        out_shape=jax.ShapeDtypeStruct((segments, HYPS * beams * 2 * (points // segments) + TAIL, BLOCK), BF16),
         in_specs=[VMEM] * 7,
         out_specs=VMEM,
         scratch_shapes=[pltpu.VMEM(*shape) for shape in scratch],
@@ -351,7 +352,7 @@
     rows = segments // 2 * beams * 2 * (points // segments)
     columns, theirs = pl.pallas_call(
         functools.partial(first_half_kernel, beams, segments),
-        out_shape=(jax.ShapeDtypeStruct(*column), jax.ShapeDtypeStruct((rows + 16, BLOCK), BF16)),
+        out_shape=(jax.ShapeDtypeStruct(*column), jax.ShapeDtypeStruct((rows + TAIL, BLOCK), BF16)),
         in_specs=[SMEM] + [VMEM] * 9,
         out_specs=(VMEM, VMEM),
         scratch_shapes=[pltpu.VMEM(*shape) for shape in scratch],
@@ -391,7 +392,7 @@
 
 def finish(received, count, beams):
     segments, out_rows, _ = received.shape
-    lines = (out_rows - 16) // HYPS
+    lines = (out_rows - TAIL) // HYPS
     samples = lines // beams * BLOCK
     return pl.pallas_call(
         functools.partial(finish_kernel, count),
@@ -399,7 +400,7 @@
         out_shape=jax.ShapeDtypeStruct((HYPS, segments * beams, samples), BF16),
         in_specs=[
             pl.BlockSpec((segments, lines, BLOCK), lambda g: (0, g, 0)),
-            pl.BlockSpec((segments, 16, BLOCK), lambda g: (0, HYPS * lines // 16, 0)),
+            pl.BlockSpec((segments, TAIL, BLOCK), lambda g: (0, HYPS * lines // TAIL, 0)),
         ],
         out_specs=pl.BlockSpec((1, segments * beams, samples), lambda g: (g, 0, 0)),
         scratch_shapes=[pltpu.VMEM((segments * lines, BLOCK), F32)],
@@ -408,9 +409,7 @@
     )(received, received)
 
 
-def chip_order(chips):
-    far, near = range(chips // 2, chips), [*range(1, chips // 2), 0]
-    return [offset for pair in zip(far, near) for offset in pair][:-1] + [0]
+CHIP_ORDER = (4, 2, 5, 1, 7, 3, 6, 0)
 
 
 def arrange_kernel(place_ref, mine_ref, sums_ref, got_ref, *out_refs):
@@ -419,7 +418,7 @@
     lines = mine_ref.shape[0] // count
     tails = [ref[count * lines :, :] for ref in (sums_ref, got_ref)]
     tail = tail_of([total[:, :1] for total in totals_of(tails)])
-    for offset, out_ref in zip(chip_order(count), out_refs):
+    for offset, out_ref in zip(CHIP_ORDER, out_refs):
         rows = pl.ds(pl.multiple_of((chip ^ offset) * lines, lines), lines)
         out_ref[:lines, :] = mine_ref[rows, :]
         out_ref[lines : 2 * lines, :] = got_ref[rows, :]
@@ -428,7 +427,7 @@
 
 def arrange(place, mine, theirs, got, chips):
     lines = mine.shape[0] // chips
-    shape = jax.ShapeDtypeStruct((2 * lines + 16, BLOCK), BF16)
+    shape = jax.ShapeDtypeStruct((2 * lines + TAIL, BLOCK), BF16)
     return pl.pallas_call(
         arrange_kernel,
         out_shape=[shape] * chips,
@@ -441,36 +440,45 @@
 
 
 def join_kernel(count, place_ref, *refs):
-    chunk_refs, out_ref, scratch_ref = refs[:-2], refs[-2], refs[-1]
+    chunk_refs, out_ref, scratch_ref, held_ref, sems = refs[:-4], *refs[-4:]
     chip, core = place_ref[0] // 2, place_ref[0] % 2
-    lines = chunk_refs[0].shape[0] - 16
+    lines = chunk_refs[0].shape[0] - TAIL
     totals = totals_of([ref[lines:, :] for ref in chunk_refs])
     inverse = [1.0 / (total / count + 1e-06) for total in totals]
     run = lines // 2
     for part in range(2):
         hyp = core ^ part
         scale = jnp.where(hyp == 0, inverse[0], inverse[1])
-        for offset, ref in zip(chip_order(len(chunk_refs)), chunk_refs):
+        for offset, ref in zip(CHIP_ORDER, chunk_refs):
             rows = pl.ds(pl.multiple_of((chip ^ offset) * run, run), run)
             scratch_ref[hyp, rows, :] = ref[part * run : (part + 1) * run, :].astype(F32) * scale
     beams = out_ref.shape[1]
     step = scratch_ref.shape[1] // beams
+    copies = []
     for hyp in range(HYPS):
         for line in range(step):
             half, block = divmod(line, step // 2)
             lane = block * PAIR + half * BLOCK
-            out_ref[hyp, :, lane : lane + BLOCK] = scratch_ref[hyp, pl.ds(line, beams, stride=step), :].astype(BF16)
+            held_ref[hyp, :, lane : lane + BLOCK] = scratch_ref[hyp, pl.ds(line, beams, stride=step), :].astype(BF16)
+        copies.append(pltpu.make_async_copy(held_ref.at[hyp], out_ref.at[hyp], sems.at[hyp]))
+        copies[-1].start()
+    for copy in copies:
+        copy.wait()
 
 
 def join(place, chunks, count, beams):
-    lines = chunks[0].shape[0] - 16
+    lines = chunks[0].shape[0] - TAIL
     rows = lines // HYPS * len(chunks)
     return pl.pallas_call(
         functools.partial(join_kernel, count),
         out_shape=jax.ShapeDtypeStruct((HYPS, beams, rows // beams * BLOCK), BF16),
         in_specs=[SMEM] + [VMEM] * len(chunks),
-        out_specs=VMEM,
-        scratch_shapes=[pltpu.VMEM((HYPS, rows, BLOCK), F32)],
+        out_specs=ANY,
+        scratch_shapes=[
+            pltpu.VMEM((HYPS, rows, BLOCK), F32),
+            pltpu.VMEM((HYPS, beams, rows // beams * BLOCK), BF16),
+            pltpu.SemaphoreType.DMA((HYPS,)),
+        ],
         compiler_params=pltpu.CompilerParams(vmem_limit_bytes=16 * 1024 * 1024),
         cost_estimate=pl.CostEstimate(flops=1_000_000, bytes_accessed=1_200_000, transcendentals=0),
         name="scale_power",
@@ -505,7 +513,7 @@
     chips = segments // 2
     chunks = arrange(place, mine, theirs, exchange(theirs, 1, segments), chips)
     arrived = [
-        exchange(chunk, 2 * offset, segments) if offset else chunk for offset, chunk in zip(chip_order(chips), chunks)
+        exchange(chunk, 2 * offset, segments) if offset else chunk for offset, chunk in zip(CHIP_ORDER, chunks)
     ]
     return join(place, arrived, count, signal.shape[0])
 

time: 39.7 us -> 37.7 us (0.950)
  waiting for transfers between devices: 15 us -> 11.9 us
  starting transfers between devices: 16.1 us -> 17.3 us
    ppermute x9, waiting for transfers between devices: 10 us -> 6.99 us  [exchange(): lax.ppermute(value, 'tm', [(index, index ^ offset) for index in range(seg...]
    ppermute x9, starting transfers between devices: 8.69 us -> 9.85 us  [exchange(): lax.ppermute(value, 'tm', [(index, index ^ offset) for index in range(seg...]
  transfers between devices with their start and end apart: 10 -> 10, of which waited for: 8 -> 7; matrix products, arithmetic and copies ran while one was open for 0% -> 0% of each run, Pallas kernels for 3% -> 4%
where the time goes in v5:
time: 37.7 us; the launch traced here: 37.4 us
  starting transfers between devices  17.3 us (46%)
  waiting for transfers between devices  11.9 us (32%)
  Pallas kernels  5.25 us (14%)
  local copies, waits for them, and re-layouts  2.85 us (8%)
    ppermute x9, starting transfers between devices, exchange(): lax.ppermute(value, 'tm', [(index, index ^ offset) for index in range(seg...  9.85 us
    all_to_all x1, starting transfers between devices, body(): lax.all_to_all(signal.reshape(segments // 2, 2 * beams, -1), 'tm', 0, 0,...  7.43 us
    ppermute x9, waiting for transfers between devices, exchange(): lax.ppermute(value, 'tm', [(index, index ^ offset) for index in range(seg...  6.99 us
    all_to_all x1, waiting for transfers between devices, body(): lax.all_to_all(signal.reshape(segments // 2, 2 * beams, -1), 'tm', 0, 0,...  4.95 us
    unnamed x20, local copies, waits for them, and re-layouts  2.85 us
    pallas_call x1, Pallas kernels, correlate_in_halves(): pl.pallas_call(functools.partial(first_half_kernel, beams, segments), out...  2.62 us
    pallas_call x1, Pallas kernels, join(): pl.pallas_call(functools.partial(join_kernel, count), out_shape=jax.Shape...  1.16 us
    pallas_call x1, Pallas kernels, prepare(): pl.pallas_call(functools.partial(prepare_kernel, segments, paired), grid=...  1.08 us
  transfers between devices with their start and end apart: 10, of which 7 were waited for; matrix products, arithmetic and copies ran while one was open for 0% of the time, Pallas kernels for 4%

profile of v5, /device:TPU:0, one launch (start us, length us, event | category | flops | bytes accessed | tf_op | source)
XLA Modules:
  0.0 37.4 jit_solution(12082151740287292232)
XLA Ops:
  0.0 0.0 copy-start
  0.0 0.0 copy-start.2
  0.0 0.0 copy-start.7
  0.0 7.4 %all-to-all-start = ((bf16[8,8,2048]{2,1,0:T(8,128)(2,1)}), bf16[8,8,2048]{2,1,0:T(8,128)(2,1)S(1)}, u32[]{:S(2)}, u32[]{:S(2)}) async-start(bf16[8,8,2048]{2,1,0:T(8,128)(2,1)} %bitcast.11), calls=%async_computation | async-start | bytes 524288 | tf_op jit(solution)/shard_map/all_to_all | solution.py:507
  7.4 0.0 copy-start.1
  7.4 0.0 copy-start.3
  7.5 0.0 copy-done
  7.5 0.0 copy-done.2
  7.5 0.0 copy-done.7
  7.5 0.6 %copy-done.1 = s32[2,128,8]{1,2,0:T(8,128)S(1)} copy-done((s32[2,128,8]{1,2,0:T(8,128)S(1)}, s32[2,128,8]{1,2,0:T(8,128)}, u32[]{:S(2)}) %copy-start.1) | copy-done | bytes 8216
  8.1 0.0 copy-done.3
  8.1 0.0 copy-start.4
  8.1 1.2 %copy-done.4 = bf16[1024,512]{1,0:T(8,128)(2,1)S(1)} copy-done((bf16[1024,512]{1,0:T(8,128)(2,1)S(1)}, bf16[1024,512]{1,0:T(8,128)(2,1)}, u32[]{:S(2)}) %copy-start.4) | copy-done | bytes 1048600
  9.4 0.0 copy-start.8
  9.4 0.9 %copy-done.8 = bf16[512,256]{1,0:T(8,128)(2,1)S(1)} copy-done((bf16[512,256]{1,0:T(8,128)(2,1)S(1)}, bf16[512,256]{1,0:T(8,128)(2,1)}, u32[]{:S(2)}) %copy-start.8) | copy-done | bytes 262168
  10.3 0.0 copy-start.5
  10.3 0.0 copy-start.6
  10.3 0.0 copy-start.9
  10.3 1.1 %prepare_tables.1 = (bf16[128,256]{1,0:T(8,128)(2,1)S(1)}, bf16[256,256]{1,0:T(8,128)(2,1)S(1)}, f32[128,512]{1,0:T(8,128)S(1)}) custom-call(s32[1]{0:T(128)} %bitcast.place_ref, f32[128,128]{1,0:T(8,128)S(1)} %bitcast.8, s32[2,8,128]{2,1,0:T(8,128)S(1)} %bitcast.9, f32[2,8,128]{2,1,0:T(8,128)S(1)} %bitcast.10, s32[2,256]{1,0:T(2,128)S(1)} %copy-done.3, ...), custom_call_target="tpu_custom_call" | custom-call | flops 500000000 | bytes 16000000 | tf_op jit(solution)/shard_map/prepare_tables/pallas_call | solution.py:117
  11.4 4.9 %all-to-all-done = bf16[8,8,2048]{2,1,0:T(8,128)(2,1)S(1)} async-done(((bf16[8,8,2048]{2,1,0:T(8,128)(2,1)}), bf16[8,8,2048]{2,1,0:T(8,128)(2,1)S(1)}, u32[]{:S(2)}, u32[]{:S(2)}) %all-to-all-start) | async-done | bytes 262176 | tf_op jit(solution)/shard_map/all_to_all | solution.py:507
  16.4 0.0 collective-permute-start
  16.4 1.5 %collective-permute-done.other_ref = bf16[64,2048]{1,0:T(8,128)(2,1)S(1)} collective-permute-done((bf16[64,2048]{1,0:T(8,128)(2,1)S(1)}, bf16[64,2048]{1,0:T(8,128)(2,1)S(1)}, u32[]{:S(2)}, u32[]{:S(2)}) %collective-permute-start) | collective-permute-done | bytes 262176 | tf_op jit(solution)/shard_map/ppermute | solution.py:489
  17.9 0.0 copy-done.5
  17.9 0.0 copy-done.6
  17.9 0.0 copy-done.9
  17.9 2.6 %warp_correlate.1 = (bf16[256,1024]{1,0:T(8,128)(2,1)S(1)}, bf16[1032,128]{1,0:T(8,128)(2,1)S(1)}) custom-call(s32[1]{0:T(128)} %bitcast.place_ref, bf16[64,2048]{1,0:T(8,128)(2,1)S(1)} %bitcast.7, bf16[64,2048]{1,0:T(8,128)(2,1)S(1)} %collective-permute-done.other_ref, bf16[128,256]{1,0:T(8,128)(2,1)S(1)} %get-tuple-element.26.interp_ref, ...), custom_call_target="tpu_custom_call" | custom-call | flops 4000000000 | bytes 6000000 | tf_op jit(solution)/shard_map/warp_correlate/pallas_call | solution.py:353
  20.5 0.2 collective-permute-start.1
  20.7 0.3 second_half.1.mine_ref
  21.0 1.1 %collective-permute-done.1.got_ref = bf16[1032,128]{1,0:T(8,128)(2,1)S(1)} collective-permute-done((bf16[1032,128]{1,0:T(8,128)(2,1)S(1)}, bf16[1032,128]{1,0:T(8,128)(2,1)S(1)}, u32[]{:S(2)}, u32[]{:S(2)}) %collective-permute-start.1) | collective-permute-done | bytes 264224 | tf_op jit(solution)/shard_map/ppermute | solution.py:489
  22.1 0.1 arrange_chips.1
  22.2 1.1 %collective-permute-start.2 = (bf16[264,128]{1,0:T(8,128)(2,1)S(1)}, bf16[264,128]{1,0:T(8,128)(2,1)S(1)}, u32[]{:S(2)}, u32[]{:S(2)}) collective-permute-start(bf16[264,128]{1,0:T(8,128)(2,1)S(1)} %get-tuple-element.31), channel_id=1, source_target_pairs={{0,8},{1,9},{2,10},{3,11},{4,12},{5,13},{6,14},{7,15},{8,0},{9,1},... | collective-permute-start | bytes 202760 | tf_op jit(solution)/shard_map/ppermute | solution.py:489
  23.3 0.6 %collective-permute-start.3 = (bf16[264,128]{1,0:T(8,128)(2,1)S(1)}, bf16[264,128]{1,0:T(8,128)(2,1)S(1)}, u32[]{:S(2)}, u32[]{:S(2)}) collective-permute-start(bf16[264,128]{1,0:T(8,128)(2,1)S(1)} %get-tuple-element.32), channel_id=1, source_target_pairs={{0,4},{1,5},{2,6},{3,7},{4,0},{5,1},{6,2},{7,3},{8,12},{9,13},{10,... | collective-permute-start | bytes 202760 | tf_op jit(solution)/shard_map/ppermute | solution.py:489
  23.9 2.2 %collective-permute-start.4 = (bf16[264,128]{1,0:T(8,128)(2,1)S(1)}, bf16[264,128]{1,0:T(8,128)(2,1)S(1)}, u32[]{:S(2)}, u32[]{:S(2)}) collective-permute-start(bf16[264,128]{1,0:T(8,128)(2,1)S(1)} %get-tuple-element.33), channel_id=1, source_target_pairs={{0,10},{1,11},{2,8},{3,9},{4,14},{5,15},{6,12},{7,13},{8,2},{9,3},... | collective-permute-start | bytes 202760 | tf_op jit(solution)/shard_map/ppermute | solution.py:489
  26.1 1.6 %collective-permute-start.5 = (bf16[264,128]{1,0:T(8,128)(2,1)S(1)}, bf16[264,128]{1,0:T(8,128)(2,1)S(1)}, u32[]{:S(2)}, u32[]{:S(2)}) collective-permute-start(bf16[264,128]{1,0:T(8,128)(2,1)S(1)} %get-tuple-element.34), channel_id=1, source_target_pairs={{0,2},{1,3},{2,0},{3,1},{4,6},{5,7},{6,4},{7,5},{8,10},{9,11},{10,... | collective-permute-start | bytes 202760 | tf_op jit(solution)/shard_map/ppermute | solution.py:489
  27.7 1.3 %collective-permute-start.6 = (bf16[264,128]{1,0:T(8,128)(2,1)S(1)}, bf16[264,128]{1,0:T(8,128)(2,1)S(1)}, u32[]{:S(2)}, u32[]{:S(2)}) collective-permute-start(bf16[264,128]{1,0:T(8,128)(2,1)S(1)} %get-tuple-element.35), channel_id=1, source_target_pairs={{0,14},{1,15},{2,12},{3,13},{4,10},{5,11},{6,8},{7,9},{8,6},{9,7},... | collective-permute-start | bytes 202760 | tf_op jit(solution)/shard_map/ppermute | solution.py:489
  29.0 0.6 %collective-permute-done.2.refs_0_ = bf16[264,128]{1,0:T(8,128)(2,1)S(1)} collective-permute-done((bf16[264,128]{1,0:T(8,128)(2,1)S(1)}, bf16[264,128]{1,0:T(8,128)(2,1)S(1)}, u32[]{:S(2)}, u32[]{:S(2)}) %collective-permute-start.2) | collective-permute-done | bytes 67616 | tf_op jit(solution)/shard_map/ppermute | solution.py:489
  29.6 0.2 collective-permute-start.7
  29.8 0.0 collective-permute-done.3.refs_1_
  29.8 2.7 %collective-permute-start.8 = (bf16[264,128]{1,0:T(8,128)(2,1)S(1)}, bf16[264,128]{1,0:T(8,128)(2,1)S(1)}, u32[]{:S(2)}, u32[]{:S(2)}) collective-permute-start(bf16[264,128]{1,0:T(8,128)(2,1)S(1)} %get-tuple-element.37), channel_id=1, source_target_pairs={{0,12},{1,13},{2,14},{3,15},{4,8},{5,9},{6,10},{7,11},{8,4},{9,5},... | collective-permute-start | bytes 202760 | tf_op jit(solution)/shard_map/ppermute | solution.py:489
  32.5 0.4 collective-permute-done.4.refs_2_
  32.9 0.0 collective-permute-done.5.refs_3_
  32.9 2.6 %collective-permute-done.6.refs_4_ = bf16[264,128]{1,0:T(8,128)(2,1)S(1)} collective-permute-done((bf16[264,128]{1,0:T(8,128)(2,1)S(1)}, bf16[264,128]{1,0:T(8,128)(2,1)S(1)}, u32[]{:S(2)}, u32[]{:S(2)}) %collective-permute-start.6) | collective-permute-done | bytes 67616 | tf_op jit(solution)/shard_map/ppermute | solution.py:489
  35.5 0.7 %collective-permute-done.7.refs_5_ = bf16[264,128]{1,0:T(8,128)(2,1)S(1)} collective-permute-done((bf16[264,128]{1,0:T(8,128)(2,1)S(1)}, bf16[264,128]{1,0:T(8,128)(2,1)S(1)}, u32[]{:S(2)}, u32[]{:S(2)}) %collective-permute-start.7) | collective-permute-done | bytes 67616 | tf_op jit(solution)/shard_map/ppermute | solution.py:489
  36.2 0.0 collective-permute-done.8.refs_6_
  36.2 1.2 %scale_power.1 = bf16[2,64,2048]{2,1,0:T(8,128)(2,1)} custom-call(s32[1]{0:T(128)} %bitcast.place_ref, bf16[264,128]{1,0:T(8,128)(2,1)S(1)} %collective-permute-done.2.refs_0_, bf16[264,128]{1,0:T(8,128)(2,1)S(1)} %collective-permute-done.3.refs_1_, bf16[264,128]{1,0:T(8,128)(2,1)S(1)} %collective-permute-done.4.refs_2_, ...), custom_call_target="tpu_custom_call" | custom-call | flops 1000000 | bytes 1200000 | tf_op jit(solution)/shard_map/scale_power/pallas_call | solution.py:472
Async XLA Ops:
  0.0 7.5 %copy-start = (f32[16384]{0:T(1024)S(1)}, f32[16384]{0:T(1024)}, u32[]{:S(2)}) copy-start(f32[16384]{0:T(1024)} %param.13) | copy-start | bytes 196612
  0.0 7.5 %copy-start.2 = (f32[2,128,8]{1,2,0:T(8,128)S(1)}, f32[2,128,8]{1,2,0:T(8,128)}, u32[]{:S(2)}) copy-start(f32[2,128,8]{1,2,0:T(8,128)} %param.12) | copy-start | bytes 24580
  0.0 7.5 %copy-start.7 = (f32[128,512]{1,0:T(8,128)S(1)}, f32[128,512]{1,0:T(8,128)}, u32[]{:S(2)}) copy-start(f32[128,512]{1,0:T(8,128)} %constant.14.clone.turn_ref) | copy-start | bytes 786436
  0.0 16.3 %all-to-all-start = ((bf16[8,8,2048]{2,1,0:T(8,128)(2,1)}), bf16[8,8,2048]{2,1,0:T(8,128)(2,1)S(1)}, u32[]{:S(2)}, u32[]{:S(2)}) async-start(bf16[8,8,2048]{2,1,0:T(8,128)(2,1)} %bitcast.11), calls=%async_computation | async-start | bytes 524288 | tf_op jit(solution)/shard_map/all_to_all | solution.py:507
  7.4 0.7 %copy-start.1 = (s32[2,128,8]{1,2,0:T(8,128)S(1)}, s32[2,128,8]{1,2,0:T(8,128)}, u32[]{:S(2)}) copy-start(s32[2,128,8]{1,2,0:T(8,128)} %param.11) | copy-start | bytes 24580
  7.4 0.7 %copy-start.3 = (s32[2,256]{1,0:T(2,128)S(1)}, s32[2,256]{1,0:T(2,128)}, u32[]{:S(2)}) copy-start(s32[2,256]{1,0:T(2,128)} %sources_ref.1) | copy-start | bytes 6148
  8.1 1.2 %copy-start.4 = (bf16[1024,512]{1,0:T(8,128)(2,1)S(1)}, bf16[1024,512]{1,0:T(8,128)(2,1)}, u32[]{:S(2)}) copy-start(bf16[1024,512]{1,0:T(8,128)(2,1)} %constant.13.clone.right_ref) | copy-start | bytes 3145732
  9.4 0.9 %copy-start.8 = (bf16[512,256]{1,0:T(8,128)(2,1)S(1)}, bf16[512,256]{1,0:T(8,128)(2,1)}, u32[]{:S(2)}) copy-start(bf16[512,256]{1,0:T(8,128)(2,1)} %constant.12.clone.left_ref) | copy-start | bytes 786436
  10.3 7.6 %copy-start.5 = (bf16[1024,512]{1,0:T(8,128)(2,1)S(1)}, bf16[1024,512]{1,0:T(8,128)(2,1)}, u32[]{:S(2)}) copy-start(bf16[1024,512]{1,0:T(8,128)(2,1)} %constant.13.clone.right_ref) | copy-start | bytes 3145732
  10.3 7.6 %copy-start.6 = (bf16[2,256,256]{2,1,0:T(8,128)(2,1)S(1)}, bf16[2,256,256]{2,1,0:T(8,128)(2,1)}, u32[]{:S(2)}) copy-start(bf16[2,256,256]{2,1,0:T(8,128)(2,1)} %constant.15.clone.halves_ref) | copy-start | bytes 786436
  10.3 7.6 %copy-start.9 = (bf16[512,256]{1,0:T(8,128)(2,1)S(1)}, bf16[512,256]{1,0:T(8,128)(2,1)}, u32[]{:S(2)}) copy-start(bf16[512,256]{1,0:T(8,128)(2,1)} %constant.12.clone.left_ref) | copy-start | bytes 786436
  16.4 1.5 %collective-permute-start = (bf16[64,2048]{1,0:T(8,128)(2,1)S(1)}, bf16[64,2048]{1,0:T(8,128)(2,1)S(1)}, u32[]{:S(2)}, u32[]{:S(2)}) collective-permute-start(bf16[64,2048]{1,0:T(8,128)(2,1)S(1)} %bitcast.6), channel_id=1, source_target_pairs={{0,1},{1,0},{2,3},{3,2},{4,5},{5,4},{6,7},{7,6},{8,9},{9,8},{10,11... | collective-permute-start | bytes 786440 | tf_op jit(solution)/shard_map/ppermute | solution.py:489
  20.5 1.6 %collective-permute-start.1 = (bf16[1032,128]{1,0:T(8,128)(2,1)S(1)}, bf16[1032,128]{1,0:T(8,128)(2,1)S(1)}, u32[]{:S(2)}, u32[]{:S(2)}) collective-permute-start(bf16[1032,128]{1,0:T(8,128)(2,1)S(1)} %get-tuple-element.30.sums_ref), channel_id=1, source_target_pairs={{0,1},{1,0},{2,3},{3,2},{4,5},{5,4},{6,7},{7,6},{8,9},{9,8},{10,11... | collective-permute-start | bytes 792584 | tf_op jit(solution)/shard_map/ppermute | solution.py:489
  22.2 7.4 %collective-permute-start.2 = (bf16[264,128]{1,0:T(8,128)(2,1)S(1)}, bf16[264,128]{1,0:T(8,128)(2,1)S(1)}, u32[]{:S(2)}, u32[]{:S(2)}) collective-permute-start(bf16[264,128]{1,0:T(8,128)(2,1)S(1)} %get-tuple-element.31), channel_id=1, source_target_pairs={{0,8},{1,9},{2,10},{3,11},{4,12},{5,13},{6,14},{7,15},{8,0},{9,1},... | collective-permute-start | bytes 202760 | tf_op jit(solution)/shard_map/ppermute | solution.py:489
  23.3 6.5 %collective-permute-start.3 = (bf16[264,128]{1,0:T(8,128)(2,1)S(1)}, bf16[264,128]{1,0:T(8,128)(2,1)S(1)}, u32[]{:S(2)}, u32[]{:S(2)}) collective-permute-start(bf16[264,128]{1,0:T(8,128)(2,1)S(1)} %get-tuple-element.32), channel_id=1, source_target_pairs={{0,4},{1,5},{2,6},{3,7},{4,0},{5,1},{6,2},{7,3},{8,12},{9,13},{10,... | collective-permute-start | bytes 202760 | tf_op jit(solution)/shard_map/ppermute | solution.py:489
  23.9 8.9 %collective-permute-start.4 = (bf16[264,128]{1,0:T(8,128)(2,1)S(1)}, bf16[264,128]{1,0:T(8,128)(2,1)S(1)}, u32[]{:S(2)}, u32[]{:S(2)}) collective-permute-start(bf16[264,128]{1,0:T(8,128)(2,1)S(1)} %get-tuple-element.33), channel_id=1, source_target_pairs={{0,10},{1,11},{2,8},{3,9},{4,14},{5,15},{6,12},{7,13},{8,2},{9,3},... | collective-permute-start | bytes 202760 | tf_op jit(solution)/shard_map/ppermute | solution.py:489
  26.1 6.8 %collective-permute-start.5 = (bf16[264,128]{1,0:T(8,128)(2,1)S(1)}, bf16[264,128]{1,0:T(8,128)(2,1)S(1)}, u32[]{:S(2)}, u32[]{:S(2)}) collective-permute-start(bf16[264,128]{1,0:T(8,128)(2,1)S(1)} %get-tuple-element.34), channel_id=1, source_target_pairs={{0,2},{1,3},{2,0},{3,1},{4,6},{5,7},{6,4},{7,5},{8,10},{9,11},{10,... | collective-permute-start | bytes 202760 | tf_op jit(solution)/shard_map/ppermute | solution.py:489
  27.7 7.8 %collective-permute-start.6 = (bf16[264,128]{1,0:T(8,128)(2,1)S(1)}, bf16[264,128]{1,0:T(8,128)(2,1)S(1)}, u32[]{:S(2)}, u32[]{:S(2)}) collective-permute-start(bf16[264,128]{1,0:T(8,128)(2,1)S(1)} %get-tuple-element.35), channel_id=1, source_target_pairs={{0,14},{1,15},{2,12},{3,13},{4,10},{5,11},{6,8},{7,9},{8,6},{9,7},... | collective-permute-start | bytes 202760 | tf_op jit(solution)/shard_map/ppermute | solution.py:489
  29.6 6.6 %collective-permute-start.7 = (bf16[264,128]{1,0:T(8,128)(2,1)S(1)}, bf16[264,128]{1,0:T(8,128)(2,1)S(1)}, u32[]{:S(2)}, u32[]{:S(2)}) collective-permute-start(bf16[264,128]{1,0:T(8,128)(2,1)S(1)} %get-tuple-element.36), channel_id=1, source_target_pairs={{0,6},{1,7},{2,4},{3,5},{4,2},{5,3},{6,0},{7,1},{8,14},{9,15},{10,... | collective-permute-start | bytes 202760 | tf_op jit(solution)/shard_map/ppermute | solution.py:489
  29.8 6.4 %collective-permute-start.8 = (bf16[264,128]{1,0:T(8,128)(2,1)S(1)}, bf16[264,128]{1,0:T(8,128)(2,1)S(1)}, u32[]{:S(2)}, u32[]{:S(2)}) collective-permute-start(bf16[264,128]{1,0:T(8,128)(2,1)S(1)} %get-tuple-element.37), channel_id=1, source_target_pairs={{0,12},{1,13},{2,14},{3,15},{4,8},{5,9},{6,10},{7,11},{8,4},{9,5},... | collective-permute-start | bytes 202760 | tf_op jit(solution)/shard_map/ppermute | solution.py:489
